TPU v7x, 32 devices: a whole 2x2x4 slice. The times are simulated.
32 devices in a mesh: dp: 8 (over z, core), tensor: 4 (over y, x).
Axes of the slice: x: 2, y: 2, z: 4, core: 2. Of those that a mesh axis runs over, the one named last changes fastest.
Arguments:
- hidden_in: bfloat16 [8192, 2048], P(('dp', 'tensor')), may hold values from -6 to 6
- doc_lengths: int32 [8, 8], P('dp'), may hold values from 1 to 512, 1024 in all within a row
- gain_attn: bfloat16 [2048], P('dp'), may hold values from 0.099609375 to 1.8984375
- w_query: bfloat16 [2048, 2048], P('dp', 'tensor'), may hold values from -0.125 to 0.125
- w_key: bfloat16 [2048, 2048], P('dp', 'tensor'), may hold values from -0.125 to 0.125
- w_value: bfloat16 [2048, 2048], P('dp', 'tensor'), may hold values from -0.125 to 0.125
- w_out: bfloat16 [2048, 2048], P('tensor', 'dp'), may hold values from -1 to 1
- gain_mlp: bfloat16 [2048], P('dp'), may hold values from 0.099609375 to 1.8984375
- w_gate: bfloat16 [2048, 8192], P('dp', 'tensor'), may hold values from -0.125 to 0.125
- w_up: bfloat16 [2048, 8192], P('dp', 'tensor'), may hold values from -0.125 to 0.125
- w_down: bfloat16 [8192, 2048], P('tensor', 'dp'), may hold values from -0.125 to 0.125
- cotangent: bfloat16 [8192, 2048], P(('dp', 'tensor')), may hold values from -16 to 16
Outputs:
- output: bfloat16 [8192, 2048], P(('dp', 'tensor'))
- input_grad: float32 [8192, 2048], P(('dp', 'tensor'))
- grad_gain_attn: float32 [2048], P(('dp', 'tensor'))
- grad_query: float32 [2048, 2048], P('dp', 'tensor')
- grad_key: float32 [2048, 2048], P('dp', 'tensor')
- grad_value: float32 [2048, 2048], P('dp', 'tensor')
- grad_out: float32 [2048, 2048], P('tensor', 'dp')
- grad_gain_mlp: float32 [2048], P(('dp', 'tensor'))
- grad_gate: float32 [2048, 8192], P('dp', 'tensor')
- grad_up: float32 [2048, 8192], P('dp', 'tensor')
- grad_down: float32 [8192, 2048], P('tensor', 'dp')
Inputs may be any that keep to these rules, and one draw needn't show every extreme that they name: `doc_lengths`: each row holds the lengths of the 8 documents of one packed sequence in order; a row sums to 1024 and its largest length is exactly 512.
All inputs are finite; a program needn't handle non-finite values.
Results may differ from a plain program's by a relative error of at most 0.02.
Values may be sent and summed in bfloat16 or wider, within the bound.
A program may use at most 256 MiB of HBM per device.

v0:
```python
import jax
import jax.numpy as jnp
from jax import lax
from jax.sharding import PartitionSpec as P

HEAD_DIM = 64
LEN = 1024


EPSILON = 1e-05
ROPE_BASE = 130000.0


def doc_tables(doc_lengths):
    steps_axis = jnp.arange(LEN, dtype=jnp.int32)
    doc_ends = jnp.cumsum(doc_lengths, axis=1)
    passed_end = steps_axis[None, :, None] >= doc_ends[:, None, :]
    segment = jnp.sum(passed_end.astype(jnp.int32), axis=2)
    doc_start = jnp.sum(jnp.where(passed_end, doc_lengths[:, None, :], 0), axis=2)
    return (segment, steps_axis[None, :] - doc_start)


def rotary_tables(position):
    half_dim = HEAD_DIM // 2
    inverse = jnp.power(ROPE_BASE, -jnp.arange(half_dim, dtype=jnp.float32) * 2.0 / HEAD_DIM)
    angles = position.astype(jnp.float32)[..., None] * inverse
    return (jnp.cos(angles), jnp.sin(angles))


def rotate(values, cosine_table, sine_table):
    half_dim = values.shape[-1] // 2
    front_half = values[..., :half_dim]
    back_half = values[..., half_dim:]
    cosine_part = cosine_table[..., None, :]
    sine_part = sine_table[..., None, :]
    return jnp.concatenate(
        [
            front_half * cosine_part - back_half * sine_part,
            back_half * cosine_part + front_half * sine_part,
        ],
        axis=-1,
    )


def rotate_back(grads, cosine_table, sine_table):
    half_dim = grads.shape[-1] // 2
    front_half = grads[..., :half_dim]
    back_half = grads[..., half_dim:]
    cosine_part = cosine_table[..., None, :]
    sine_part = sine_table[..., None, :]
    return jnp.concatenate(
        [
            front_half * cosine_part + back_half * sine_part,
            back_half * cosine_part - front_half * sine_part,
        ],
        axis=-1,
    )


def contract_rows(left, right):
    return lax.dot_general(
        left, right, (((0,), (0,)), ((), ())), preferred_element_type=jnp.float32
    )


def contract_cols(left, right):
    return lax.dot_general(
        left, right, (((1,), (1,)), ((), ())), preferred_element_type=jnp.float32
    )


def norm_factor(values):
    return lax.rsqrt(jnp.mean(values * values, axis=-1, keepdims=True) + EPSILON)


def norm_back(values, factor, gain, grads):
    scaled = grads * gain
    grad_in = factor * scaled - values * factor * factor * factor * jnp.mean(
        scaled * values, axis=-1, keepdims=True
    )
    gain_part = jnp.sum(grads * values * factor, axis=0)
    return (grad_in, gain_part)


def on_device(
    hidden_in,
    doc_lengths,
    gain_attn,
    w_query,
    w_key,
    w_value,
    w_out,
    gain_mlp,
    w_gate,
    w_up,
    w_down,
    cotangent,
):
    seq_count = doc_lengths.shape[0]
    all_rows = seq_count * LEN
    head_count = w_query.shape[1] // HEAD_DIM
    block_rows = min(512, LEN)
    block_count = LEN // block_rows
    scale_factor = HEAD_DIM ** (-0.5)
    head_shape = (seq_count, LEN, head_count, HEAD_DIM)
    segment, position = doc_tables(doc_lengths)
    cosine_table, sine_table = rotary_tables(position)
    attn_set = (
        lax.all_gather(gain_attn, "dp", axis=0, tiled=True),
        lax.all_gather(w_query, "dp", axis=0, tiled=True),
        lax.all_gather(w_key, "dp", axis=0, tiled=True),
        lax.all_gather(w_value, "dp", axis=0, tiled=True),
        lax.all_gather(w_out, "dp", axis=1, tiled=True),
    )
    gain_one, query_w, key_w, value_w, out_w = attn_set
    inputs = hidden_in.astype(jnp.float32)
    factor_one = norm_factor(inputs)
    normed = (inputs * factor_one * gain_one.astype(jnp.float32)).astype(jnp.bfloat16)
    normed_all = lax.all_gather(normed, "tensor", axis=0, tiled=True)
    query = rotate(
        jnp.dot(normed_all, query_w, preferred_element_type=jnp.float32).reshape(head_shape),
        cosine_table,
        sine_table,
    ).astype(jnp.bfloat16)
    keys = rotate(
        jnp.dot(normed_all, key_w, preferred_element_type=jnp.float32).reshape(head_shape),
        cosine_table,
        sine_table,
    ).astype(jnp.bfloat16)
    values = (
        jnp.dot(normed_all, value_w, preferred_element_type=jnp.float32)
        .astype(jnp.bfloat16)
        .reshape(head_shape)
    )

    def block_scores(seq_index, first_row):
        query_rows = lax.dynamic_index_in_dim(query, seq_index, 0, keepdims=False)
        query_block = lax.dynamic_slice_in_dim(query_rows, first_row, block_rows, 0)
        key_rows = lax.dynamic_index_in_dim(keys, seq_index, 0, keepdims=False)
        scores = (
            jnp.einsum("qhc,khc->hqk", query_block, key_rows, preferred_element_type=jnp.float32)
            * scale_factor
        )
        seg_row = lax.dynamic_index_in_dim(segment, seq_index, 0, keepdims=False)
        seg_query = lax.dynamic_slice_in_dim(seg_row, first_row, block_rows, 0)
        query_pos = first_row + jnp.arange(block_rows, dtype=jnp.int32)
        key_pos = jnp.arange(LEN, dtype=jnp.int32)
        allowed = (seg_query[:, None] == seg_row[None, :]) & (
            key_pos[None, :] <= query_pos[:, None]
        )
        return (jnp.where(allowed[None], scores, -1e30), query_block, key_rows)

    def forward_block(block_index):
        seq_index = block_index // block_count
        first_row = block_index % block_count * block_rows
        masked, query_block, key_rows = block_scores(seq_index, first_row)
        value_rows = lax.dynamic_index_in_dim(values, seq_index, 0, keepdims=False)
        row_max = jnp.max(masked, axis=-1, keepdims=True)
        exponent = jnp.exp(masked - row_max)
        row_total = jnp.sum(exponent, axis=-1, keepdims=True)
        weights = (exponent / row_total).astype(jnp.bfloat16)
        mixed_block = jnp.einsum(
            "hqk,khc->qhc", weights, value_rows, preferred_element_type=jnp.float32
        )
        return (mixed_block.astype(jnp.bfloat16), (row_max + jnp.log(row_total))[..., 0])

    mixed_blocks, log_totals = lax.map(
        forward_block, jnp.arange(seq_count * block_count, dtype=jnp.int32)
    )
    mixed_all = mixed_blocks.reshape(all_rows, head_count * HEAD_DIM)
    piece = mixed_all
    attended = lax.psum_scatter(
        jnp.dot(piece, out_w, preferred_element_type=jnp.float32),
        "tensor",
        scatter_dimension=0,
        tiled=True,
    )
    middle = inputs + attended
    mlp_set = (
        lax.all_gather(gain_mlp, "dp", axis=0, tiled=True),
        lax.all_gather(w_gate, "dp", axis=0, tiled=True),
        lax.all_gather(w_up, "dp", axis=0, tiled=True),
        lax.all_gather(w_down, "dp", axis=1, tiled=True),
    )
    gain_two, gate_w, up_w, down_w = mlp_set
    factor_two = norm_factor(middle)
    normed_mlp = (middle * factor_two * gain_two.astype(jnp.float32)).astype(jnp.bfloat16)
    normed_mlp_all = lax.all_gather(normed_mlp, "tensor", axis=0, tiled=True)
    gate_pre = jnp.dot(normed_mlp_all, gate_w, preferred_element_type=jnp.float32)
    upward = jnp.dot(normed_mlp_all, up_w, preferred_element_type=jnp.float32)
    sigmoid_gate = jax.nn.sigmoid(gate_pre)
    activated = gate_pre * sigmoid_gate
    hidden = (activated * upward).astype(jnp.bfloat16)
    piece = hidden
    mlp_part = lax.psum_scatter(
        jnp.dot(piece, down_w, preferred_element_type=jnp.float32).astype(jnp.bfloat16),
        "tensor",
        scatter_dimension=0,
        tiled=True,
    ).astype(jnp.float32)
    output = (middle + mlp_part).astype(jnp.bfloat16)
    mlp_back = (
        lax.all_gather(gain_mlp, "dp", axis=0, tiled=True),
        lax.all_gather(w_gate, "dp", axis=0, tiled=True),
        lax.all_gather(w_up, "dp", axis=0, tiled=True),
        lax.all_gather(w_down, "dp", axis=1, tiled=True),
    )
    gain_two_back, gate_back, up_back, down_back = mlp_back
    grad_out_rows = lax.all_gather(cotangent, "tensor", axis=0, tiled=True)
    grad_down = contract_rows(hidden, grad_out_rows)
    grad_hidden = contract_cols(grad_out_rows, down_back)
    grad_gate_pre = (
        grad_hidden * upward * sigmoid_gate * (1.0 + gate_pre * (1.0 - sigmoid_gate))
    ).astype(jnp.bfloat16)
    grad_upward = (grad_hidden * activated).astype(jnp.bfloat16)
    grad_gate = contract_rows(normed_mlp_all, grad_gate_pre)
    grad_up = contract_rows(normed_mlp_all, grad_upward)
    grad_normed_mlp = lax.psum_scatter(
        (contract_cols(grad_gate_pre, gate_back) + contract_cols(grad_upward, up_back)).astype(
            jnp.bfloat16
        ),
        "tensor",
        scatter_dimension=0,
        tiled=True,
    ).astype(jnp.float32)
    grad_mid_norm, gain_two_part = norm_back(
        middle, factor_two, gain_two_back.astype(jnp.float32), grad_normed_mlp
    )
    grad_middle = cotangent.astype(jnp.float32) + grad_mid_norm
    attn_back = (
        lax.all_gather(gain_attn, "dp", axis=0, tiled=True),
        lax.all_gather(w_query, "dp", axis=0, tiled=True),
        lax.all_gather(w_key, "dp", axis=0, tiled=True),
        lax.all_gather(w_value, "dp", axis=0, tiled=True),
        lax.all_gather(w_out, "dp", axis=1, tiled=True),
    )
    gain_one_back, query_back, key_back, value_back, out_back = attn_back
    grad_mid_all = lax.all_gather(grad_middle.astype(jnp.bfloat16), "tensor", axis=0, tiled=True)
    grad_out_w = contract_rows(mixed_all, grad_mid_all)
    grad_mixed = contract_cols(grad_mid_all, out_back).astype(jnp.bfloat16).reshape(head_shape)

    def backward_seq(seq_index):
        value_rows = lax.dynamic_index_in_dim(values, seq_index, 0, keepdims=False)
        grad_mixed_rows = lax.dynamic_index_in_dim(grad_mixed, seq_index, 0, keepdims=False)

        def backward_step(running, block_index):
            grad_keys, grad_values = running
            first_row = block_index * block_rows
            masked, query_block, key_rows = block_scores(seq_index, first_row)
            log_block = lax.dynamic_index_in_dim(
                log_totals, seq_index * block_count + block_index, 0, keepdims=False
            )
            weights = jnp.exp(masked - log_block[..., None])
            grad_block = lax.dynamic_slice_in_dim(grad_mixed_rows, first_row, block_rows, 0)
            grad_weights = jnp.einsum(
                "qhc,khc->hqk", grad_block, value_rows, preferred_element_type=jnp.float32
            )
            inner_sum = jnp.sum(weights * grad_weights, axis=-1, keepdims=True)
            grad_scores = (weights * (grad_weights - inner_sum) * scale_factor).astype(jnp.bfloat16)
            grad_values = grad_values + jnp.einsum(
                "hqk,qhc->khc",
                weights.astype(jnp.bfloat16),
                grad_block,
                preferred_element_type=jnp.float32,
            )
            grad_query_block = jnp.einsum(
                "hqk,khc->qhc", grad_scores, key_rows, preferred_element_type=jnp.float32
            )
            grad_keys = grad_keys + jnp.einsum(
                "hqk,qhc->khc", grad_scores, query_block, preferred_element_type=jnp.float32
            )
            return ((grad_keys, grad_values), grad_query_block)

        zero_block = jnp.zeros((LEN, head_count, HEAD_DIM), jnp.float32)
        finals, grad_queries = lax.scan(
            backward_step, (zero_block, zero_block), jnp.arange(block_count, dtype=jnp.int32)
        )
        return (grad_queries.reshape(LEN, head_count, HEAD_DIM), finals[0], finals[1])

    grad_q_heads, grad_k_heads, grad_v_heads = lax.map(
        backward_seq, jnp.arange(seq_count, dtype=jnp.int32)
    )
    grad_query_rows = (
        rotate_back(grad_q_heads, cosine_table, sine_table)
        .reshape(all_rows, -1)
        .astype(jnp.bfloat16)
    )
    grad_key_rows = (
        rotate_back(grad_k_heads, cosine_table, sine_table)
        .reshape(all_rows, -1)
        .astype(jnp.bfloat16)
    )
    grad_value_rows = grad_v_heads.reshape(all_rows, -1).astype(jnp.bfloat16)
    grad_query = contract_rows(normed_all, grad_query_rows)
    grad_key = contract_rows(normed_all, grad_key_rows)
    grad_value = contract_rows(normed_all, grad_value_rows)
    grad_normed = lax.psum_scatter(
        (
            contract_cols(grad_query_rows, query_back)
            + contract_cols(grad_key_rows, key_back)
            + contract_cols(grad_value_rows, value_back)
        ).astype(jnp.bfloat16),
        "tensor",
        scatter_dimension=0,
        tiled=True,
    ).astype(jnp.float32)
    grad_in_norm, gain_one_part = norm_back(
        inputs, factor_one, gain_one_back.astype(jnp.float32), grad_normed
    )
    input_grad = grad_middle + grad_in_norm
    gain_sums = lax.psum_scatter(
        jnp.stack([gain_one_part, gain_two_part]), ("dp", "tensor"), scatter_dimension=1, tiled=True
    )
    weight_sums = (
        lax.psum_scatter(
            grad_query.astype(jnp.bfloat16), "dp", scatter_dimension=0, tiled=True
        ).astype(jnp.float32),
        lax.psum_scatter(
            grad_key.astype(jnp.bfloat16), "dp", scatter_dimension=0, tiled=True
        ).astype(jnp.float32),
        lax.psum_scatter(
            grad_value.astype(jnp.bfloat16), "dp", scatter_dimension=0, tiled=True
        ).astype(jnp.float32),
        lax.psum_scatter(
            grad_out_w.astype(jnp.bfloat16), "dp", scatter_dimension=1, tiled=True
        ).astype(jnp.float32),
        lax.psum_scatter(
            grad_gate.astype(jnp.bfloat16), "dp", scatter_dimension=0, tiled=True
        ).astype(jnp.float32),
        lax.psum_scatter(
            grad_up.astype(jnp.bfloat16), "dp", scatter_dimension=0, tiled=True
        ).astype(jnp.float32),
        lax.psum_scatter(
            grad_down.astype(jnp.bfloat16), "dp", scatter_dimension=1, tiled=True
        ).astype(jnp.float32),
    )
    return (
        output,
        input_grad,
        gain_sums[0],
        weight_sums[0],
        weight_sums[1],
        weight_sums[2],
        weight_sums[3],
        gain_sums[1],
        weight_sums[4],
        weight_sums[5],
        weight_sums[6],
    )


def solution(mesh):
    return jax.shard_map(
        on_device,
        mesh=mesh,
        in_specs=(
            P(("dp", "tensor"), None),
            P("dp", None),
            P("dp"),
            P("dp", "tensor"),
            P("dp", "tensor"),
            P("dp", "tensor"),
            P("tensor", "dp"),
            P("dp"),
            P("dp", "tensor"),
            P("dp", "tensor"),
            P("tensor", "dp"),
            P(("dp", "tensor"), None),
        ),
        out_specs=(
            P(("dp", "tensor"), None),
            P(("dp", "tensor"), None),
            P(("dp", "tensor")),
            P("dp", "tensor"),
            P("dp", "tensor"),
            P("dp", "tensor"),
            P("tensor", "dp"),
            P(("dp", "tensor")),
            P("dp", "tensor"),
            P("dp", "tensor"),
            P("tensor", "dp"),
        ),
        check_vma=False,
    )
```

profile of v0, /device:TPU:0, one launch (start us, length us, event | category | flops | bytes accessed | tf_op | source)
XLA Modules:
  0.0 1482.4 jit_solution(9569864698451217463)
XLA Ops:
  41.5 54.6 %all-gather.14.cloned.1.call-done = bf16[1024,2048]{1,0:T(8,128)(2,1)} async-done(((bf16[256,2048]{1,0:T(8,128)(2,1)}), bf16[1024,2048]{1,0:T(8,128)(2,1)}) %all-gather.14.cloned.1.call-update) | async-done | bytes 4194320 | tf_op jit(solution)/shard_map/all_gather | solution.py:119
  101.3 25.5 %all-gather.16.cloned.1.call-done = bf16[2048,512]{1,0:T(8,128)(2,1)} async-done(((bf16[256,512]{1,0:T(8,128)(2,1)}), bf16[2048,512]{1,0:T(8,128)(2,1)}) %all-gather.16.cloned.1.call-update) | async-done | bytes 2097168 | tf_op jit(solution)/shard_map/all_gather | solution.py:110
  134.0 23.0 %all-gather.20.cloned.1.call-done = bf16[2048,512]{1,0:T(8,128)(2,1)} async-done(((bf16[256,512]{1,0:T(8,128)(2,1)}), bf16[2048,512]{1,0:T(8,128)(2,1)}) %all-gather.20.cloned.1.call-update) | async-done | bytes 2097168 | tf_op jit(solution)/shard_map/all_gather | solution.py:112
  162.2 34.1 %while.43 = (s32[]{:T(128)}, bf16[2,512,8,64]{1,3,2,0:T(8,128)(2,1)S(1)}, f32[2,8,512]{2,1,0:T(8,128)S(1)}, s32[2]{0:T(128)S(1)}, s32[1,1024]{1,0:T(1,128)S(1)},...) while((s32[]{:T(128)}, ...), condition=%wide.region_7.8_spmd, body=%wide.region_4.7_spmd.sunk | while | flops 1125904896 | bytes 55720256 | solution.py:167
  216.5 74.9 %reduce-scatter.15.cloned.1.call-done = f32[256,2048]{1,0:T(8,128)} async-done(((f32[1024,2048]{1,0:T(8,128)}), f32[256,2048]{1,0:T(8,128)}) %reduce-scatter.15.cloned.1.call-update) | async-done | bytes 2097168 | tf_op jit(solution)/shard_map/reduce_scatter | solution.py:172
  296.9 78.2 %all-gather.28.cloned.1.call-done = bf16[2048,2048]{1,0:T(8,128)(2,1)} async-done(((bf16[256,2048]{1,0:T(8,128)(2,1)}), bf16[2048,2048]{1,0:T(8,128)(2,1)}) %all-gather.28.cloned.1.call-update) | async-done | bytes 8388624 | tf_op jit(solution)/shard_map/all_gather | solution.py:182
  375.2 53.8 %all-gather.24.cloned.1.call-done = bf16[1024,2048]{1,0:T(8,128)(2,1)} async-done(((bf16[256,2048]{1,0:T(8,128)(2,1)}), bf16[1024,2048]{1,0:T(8,128)(2,1)}) %all-gather.24.cloned.1.call-update) | async-done | bytes 4194320 | tf_op jit(solution)/shard_map/all_gather | solution.py:188
  443.8 69.0 %all-gather.26.cloned.1.call-done = bf16[2048,2048]{1,0:T(8,128)(2,1)} async-done(((bf16[256,2048]{1,0:T(8,128)(2,1)}), bf16[2048,2048]{1,0:T(8,128)(2,1)}) %all-gather.26.cloned.1.call-update) | async-done | bytes 8388624 | tf_op jit(solution)/shard_map/all_gather | solution.py:181
  527.2 38.7 %all-gather.32.cloned.1.call-done = bf16[1024,2048]{1,0:T(8,128)(2,1)} async-done(((bf16[256,2048]{1,0:T(8,128)(2,1)}), bf16[1024,2048]{1,0:T(8,128)(2,1)}) %all-gather.32.cloned.1.call-update) | async-done | bytes 4194320 | tf_op jit(solution)/shard_map/all_gather | solution.py:209
  565.9 84.2 %all-gather.30.cloned.1.call-done = bf16[2048,2048]{1,0:T(8,128)(2,1)} async-done(((bf16[2048,256]{1,0:T(8,128)(2,1)}), bf16[2048,2048]{1,0:T(8,128)(2,1)}) %all-gather.30.cloned.1.call-update) | async-done | bytes 8388624 | tf_op jit(solution)/shard_map/all_gather | solution.py:183
  650.1 21.8 %multiply_convert_fusion.1 = (bf16[1024,2048]{1,0:T(8,128)(2,1)}, bf16[1024,2048]{1,0:T(8,128)(2,1)}, bf16[1024,2048]{1,0:T(8,128)(2,1)}) fusion(f32[1024,2048]{1,0:T(8,128)} %fusion.79, f32[1024,2048]{1,0:T(8,128)} %fusion.80, bf16[1024,2048]{1,0:T(8,128)(2,1)} %all-gather.32.cloned.1.call-done, bf16[2048,2048]{1,0:T(8,128)(2,1)} %all-gather.30.cloned.1.call-done), kind=kOutput, calls=%fused_computation.60 | convolution fusion | flops 8621391872 | bytes 41943040 | tf_op jit(solution)/shard_map/dot_general | solution.py:67
  697.7 51.0 %reduce-scatter.19.cloned.1.call-done = bf16[256,2048]{1,0:T(8,128)(2,1)} async-done(((bf16[1024,2048]{1,0:T(8,128)(2,1)}), bf16[256,2048]{1,0:T(8,128)(2,1)}) %reduce-scatter.19.cloned.1.call-update) | async-done | bytes 1048592 | tf_op jit(solution)/shard_map/reduce_scatter | solution.py:218
  820.7 196.1 %while.44 = (s32[]{:T(128)}, f32[1024,8,64]{0,2,1:T(8,128)}, f32[1024,8,64]{0,2,1:T(8,128)}, f32[2,512,8,64]{1,0,3,2:T(2,128)}, s32[2]{0:T(128)S(1)}, /*index=5*...) while((s32[]{:T(128)}, f32[1024,8,64]{0,2,1:T(8,128)}, ...), condition=%wide.region_15.16_spmd.clone, body=%wide.region_13.15_spmd.clone.sunk | while | flops 2746755584 | bytes 238090560 | solution.py:275
  846.3 26.0 %fusion.162 = f32[1,512,8,64]{1,3,2,0:T(8,128)} fusion(f32[8,512,1024]{2,1,0:T(8,128)} %copy-done, f32[8,512,1024]{2,1,0:T(8,128)} %fusion.161, bf16[1,1024,8,64]{1,3,2,0:T(8,128)(2,1)S(1)} %get-tuple-element.629), kind=kOutput, calls=%fused_computation.37.clone.1 | convolution fusion | flops 557847552 | bytes 35651584 | tf_op jit(solution)/shard_map/while/body/eval_jaxpr/while/body/eval_jaxpr/hqk,khc->qhc/dot_general | solution.py:266
  872.3 23.8 %bitcast_add_fusion.4 = f32[1024,8,64]{0,2,1:T(8,128)} fusion(f32[1024,8,64]{0,2,1:T(8,128)} %get-tuple-element.607, f32[8,512,1024]{2,1,0:T(8,128)} %copy-done, f32[8,512,1024]{2,1,0:T(8,128)} %fusion.161, pred[]{:T(512)S(6)} %compare.6, bf16[1,1024,8,64]{1,3,2,0:T(8,128)(2,1)} %get-tuple-element.627, s32[]{:T(128)S(6)} %select_n.113), kind=kOutput, calls=%fused_computation.34.clone.1 | convolution fusion | flops 558896128 | bytes 71827464 | tf_op jit(solution)/shard_map/while/body/eval_jaxpr/while/body/eval_jaxpr/hqk,qhc->khc/dot_general | solution.py:269
  944.2 26.0 %fusion.162 = f32[1,512,8,64]{1,3,2,0:T(8,128)} fusion(f32[8,512,1024]{2,1,0:T(8,128)} %copy-done, f32[8,512,1024]{2,1,0:T(8,128)} %fusion.161, bf16[1,1024,8,64]{1,3,2,0:T(8,128)(2,1)S(1)} %get-tuple-element.629), kind=kOutput, calls=%fused_computation.37.clone.1 | convolution fusion | flops 557847552 | bytes 35651584 | tf_op jit(solution)/shard_map/while/body/eval_jaxpr/while/body/eval_jaxpr/hqk,khc->qhc/dot_general | solution.py:266
  970.2 24.4 %bitcast_add_fusion.4 = f32[1024,8,64]{0,2,1:T(8,128)} fusion(f32[1024,8,64]{0,2,1:T(8,128)} %get-tuple-element.607, f32[8,512,1024]{2,1,0:T(8,128)} %copy-done, f32[8,512,1024]{2,1,0:T(8,128)} %fusion.161, pred[]{:T(512)S(6)} %compare.6, bf16[1,1024,8,64]{1,3,2,0:T(8,128)(2,1)} %get-tuple-element.627, s32[]{:T(128)S(6)} %select_n.113), kind=kOutput, calls=%fused_computation.34.clone.1 | convolution fusion | flops 558896128 | bytes 71827464 | tf_op jit(solution)/shard_map/while/body/eval_jaxpr/while/body/eval_jaxpr/hqk,qhc->khc/dot_general | solution.py:269
  1082.4 33.6 %reduce-scatter.29.cloned.1.call-done = bf16[512,256]{1,0:T(8,128)(2,1)} async-done(((bf16[512,2048]{1,0:T(8,128)(2,1)}), bf16[512,256]{1,0:T(8,128)(2,1)}) %reduce-scatter.29.cloned.1.call-update) | async-done | bytes 262160 | tf_op jit(solution)/shard_map/reduce_scatter | solution.py:324
  1117.8 34.8 %reduce-scatter.27.cloned.1.call-done = bf16[256,512]{1,0:T(8,128)(2,1)} async-done(((bf16[2048,512]{1,0:T(8,128)(2,1)}), bf16[256,512]{1,0:T(8,128)(2,1)}) %reduce-scatter.27.cloned.1.call-update) | async-done | bytes 262160 | tf_op jit(solution)/shard_map/reduce_scatter | solution.py:321
  1154.4 34.9 %reduce-scatter.23.cloned.1.call-done = bf16[256,512]{1,0:T(8,128)(2,1)} async-done(((bf16[2048,512]{1,0:T(8,128)(2,1)}), bf16[256,512]{1,0:T(8,128)(2,1)}) %reduce-scatter.23.cloned.1.call-update) | async-done | bytes 262160 | tf_op jit(solution)/shard_map/reduce_scatter | solution.py:315
  1191.1 34.8 %reduce-scatter.25.cloned.1.call-done = bf16[256,512]{1,0:T(8,128)(2,1)} async-done(((bf16[2048,512]{1,0:T(8,128)(2,1)}), bf16[256,512]{1,0:T(8,128)(2,1)}) %reduce-scatter.25.cloned.1.call-update) | async-done | bytes 262160 | tf_op jit(solution)/shard_map/reduce_scatter | solution.py:318
  1227.7 52.5 %reduce-scatter.21.cloned.1.call-done = bf16[256,2048]{1,0:T(8,128)(2,1)} async-done(((bf16[1024,2048]{1,0:T(8,128)(2,1)}), bf16[256,2048]{1,0:T(8,128)(2,1)}) %reduce-scatter.21.cloned.1.call-update) | async-done | bytes 1048592 | tf_op jit(solution)/shard_map/reduce_scatter | solution.py:297
  1283.5 52.7 %reduce-scatter.17.cloned.1.call-done = bf16[256,2048]{1,0:T(8,128)(2,1)} async-done(((bf16[1024,2048]{1,0:T(8,128)(2,1)}), bf16[256,2048]{1,0:T(8,128)(2,1)}) %reduce-scatter.17.cloned.1.call-update) | async-done | bytes 1048592 | tf_op jit(solution)/shard_map/reduce_scatter | solution.py:195
  1341.5 131.8 %reduce-scatter.37.cloned.1.call-done = f32[64,2]{1,0:T(8,128)} async-done(((f32[2048,2]{1,0:T(8,128)}), f32[64,2]{1,0:T(8,128)}) %reduce-scatter.37.cloned.1.call-update) | async-done | bytes 528
  (239 shorter events, 407.1 us)
Async XLA Ops:
  7.2 34.3 %all-gather.18.cloned.1.call-start = ((), (), s32[]{:S(2)}) async-start(), calls=%async_computation.14 | async-start | bytes 2359296 | tf_op jit(solution)/shard_map/all_gather | solution.py:111
  7.9 88.2 %all-gather.14.cloned.1.call-start = ((), (), s32[]{:S(2)}) async-start(), calls=%async_computation.12 | async-start | bytes 5242880 | tf_op jit(solution)/shard_map/all_gather | solution.py:119
  26.7 100.1 %all-gather.16.cloned.1.call-start = ((), (), s32[]{:S(2)}) async-start(), calls=%async_computation.13 | async-start | bytes 2359296 | tf_op jit(solution)/shard_map/all_gather | solution.py:110
  27.4 129.5 %all-gather.20.cloned.1.call-start = ((), (), s32[]{:S(2)}) async-start(), calls=%async_computation.15 | async-start | bytes 2359296 | tf_op jit(solution)/shard_map/all_gather | solution.py:112
  28.0 169.7 %all-gather.22.cloned.1.call-start = ((), (), s32[]{:S(2)}) async-start(), calls=%async_computation.16 | async-start | bytes 2359296 | tf_op jit(solution)/shard_map/all_gather | solution.py:113
  28.6 262.8 %reduce-scatter.15.cloned.1.call-start = ((), (), s32[]{:S(2)}) async-start(), calls=%async_computation.17 | async-start | bytes 10485760 | tf_op jit(solution)/shard_map/reduce_scatter | solution.py:172
  205.3 169.8 %all-gather.28.cloned.1.call-start = ((), (), s32[]{:S(2)}) async-start(), calls=%async_computation.20 | async-start | bytes 9437184 | tf_op jit(solution)/shard_map/all_gather | solution.py:182
  206.1 222.9 %all-gather.24.cloned.1.call-start = ((), (), s32[]{:S(2)}) async-start(), calls=%async_computation.18 | async-start | bytes 5242880 | tf_op jit(solution)/shard_map/all_gather | solution.py:188
  216.5 534.7 %copy-start.21 = (f32[8,1,256]{2,1,0:T(1,128)}, f32[8,1,256]{2,1,0:T(1,128)S(1)}, u32[]{:S(2)}) copy-start(f32[8,1,256]{2,1,0:T(1,128)S(1)} %convert_element_type.222) | copy-start | bytes 24580
  294.8 218.0 %all-gather.26.cloned.1.call-start = ((), (), s32[]{:S(2)}) async-start(), calls=%async_computation.19 | async-start | bytes 9437184 | tf_op jit(solution)/shard_map/all_gather | solution.py:181
  295.6 270.3 %all-gather.32.cloned.1.call-start = ((), (), s32[]{:S(2)}) async-start(), calls=%async_computation.23 | async-start | bytes 5242880 | tf_op jit(solution)/shard_map/all_gather | solution.py:209
  296.1 354.0 %all-gather.30.cloned.1.call-start = ((), (), s32[]{:S(2)}) async-start(), calls=%async_computation.21 | async-start | bytes 9437184 | tf_op jit(solution)/shard_map/all_gather | solution.py:183
  296.9 451.8 %reduce-scatter.19.cloned.1.call-start = ((), (), s32[]{:S(2)}) async-start(), calls=%async_computation.24 | async-start | bytes 5242880 | tf_op jit(solution)/shard_map/reduce_scatter | solution.py:218
  697.7 110.0 %all-gather.34.cloned.1.call-start = ((), (), s32[]{:S(2)}) async-start(), calls=%async_computation.25 | async-start | bytes 5242880 | tf_op jit(solution)/shard_map/all_gather | solution.py:238
  754.8 315.3 %reduce-scatter.33.cloned.1.call-start = ((), (), s32[]{:S(2)}) async-start(), calls=%async_computation.32 | async-start | bytes 9437184 | tf_op jit(solution)/shard_map/reduce_scatter | solution.py:330
  769.1 303.7 %reduce-scatter.31.cloned.1.call-start = ((), (), s32[]{:S(2)}) async-start(), calls=%async_computation.31 | async-start | bytes 9437184 | tf_op jit(solution)/shard_map/reduce_scatter | solution.py:327
  783.2 296.5 %reduce-scatter.35.cloned.1.call-start = ((), (), s32[]{:S(2)}) async-start(), calls=%async_computation.33 | async-start | bytes 9437184 | tf_op jit(solution)/shard_map/reduce_scatter | solution.py:333
  797.7 318.3 %reduce-scatter.29.cloned.1.call-start = ((), (), s32[]{:S(2)}) async-start(), calls=%async_computation.30 | async-start | bytes 2359296 | tf_op jit(solution)/shard_map/reduce_scatter | solution.py:324
  813.6 339.0 %reduce-scatter.27.cloned.1.call-start = ((), (), s32[]{:S(2)}) async-start(), calls=%async_computation.29 | async-start | bytes 2359296 | tf_op jit(solution)/shard_map/reduce_scatter | solution.py:321
  1024.6 164.7 %reduce-scatter.23.cloned.1.call-start = ((), (), s32[]{:S(2)}) async-start(), calls=%async_computation.27 | async-start | bytes 2359296 | tf_op jit(solution)/shard_map/reduce_scatter | solution.py:315
  1035.1 190.8 %reduce-scatter.25.cloned.1.call-start = ((), (), s32[]{:S(2)}) async-start(), calls=%async_computation.28 | async-start | bytes 2359296 | tf_op jit(solution)/shard_map/reduce_scatter | solution.py:318
  1042.3 237.8 %reduce-scatter.21.cloned.1.call-start = ((), (), s32[]{:S(2)}) async-start(), calls=%async_computation.26 | async-start | bytes 5242880 | tf_op jit(solution)/shard_map/reduce_scatter | solution.py:297
  1055.7 280.5 %reduce-scatter.17.cloned.1.call-start = ((), (), s32[]{:S(2)}) async-start(), calls=%async_computation.22 | async-start | bytes 5242880 | tf_op jit(solution)/shard_map/reduce_scatter | solution.py:195
  1069.7 403.6 %reduce-scatter.37.cloned.1.call-start = ((), (), s32[]{:S(2)}) async-start(), calls=%async_computation.34 | async-start | bytes 1081344
  (39 other events, 3261.0 us)
Sparse Core Ops, SparseCore 0:
  9.6 31.7 all-gather.17
  43.9 52.1 all-gather.13
  97.7 29.0 all-gather.15
  128.3 28.5 all-gather.19
  158.4 30.2 all-gather.21
  205.4 85.9 reduce-scatter.14
  293.1 82.0 all-gather.27
  377.7 51.2 all-gather.23
  430.7 82.0 all-gather.25
  514.6 51.2 all-gather.31
  567.6 82.4 all-gather.29
  697.8 50.8 reduce-scatter.18
  754.9 52.6 all-gather.33
  809.8 89.5 reduce-scatter.32
  901.6 87.9 reduce-scatter.30
  991.7 87.9 reduce-scatter.34
  1081.8 34.1 reduce-scatter.28
  1118.2 34.3 reduce-scatter.26
  1154.9 34.3 reduce-scatter.22
  1191.4 34.4 reduce-scatter.24
  1228.8 51.2 reduce-scatter.20
  1283.4 52.6 reduce-scatter.16
  1338.4 134.8 reduce-scatter.36
where the time goes:
time: 1490 us; the launch traced here: 1480 us
  waiting for transfers between devices  959 us (64%)
  matrix products  359 us (24%)
  local copies, waits for them, and re-layouts  59.1 us (4%)
  other arithmetic  54.6 us (4%)
  blocking collectives  23.8 us (2%)
  between operations  15.2 us (1%)
    unnamed x24, waiting for transfers between devices  137 us
    all_gather x1, waiting for transfers between devices, on_device(): lax.all_gather(w_down, 'dp', axis=1, tiled=True)  84.2 us
    all_gather x1, waiting for transfers between devices, on_device(): lax.all_gather(w_up, 'dp', axis=0, tiled=True)  78.2 us
    reduce_scatter x1, waiting for transfers between devices, on_device(): lax.psum_scatter(jnp.dot(piece, out_w, preferred_element_type=jnp.float32...  74.9 us
    all_gather x1, waiting for transfers between devices, on_device(): lax.all_gather(w_gate, 'dp', axis=0, tiled=True)  69 us
    dot_general x7, matrix products, contract_cols(): lax.dot_general(left, right, (((1,), (1,)), ((), ())), preferred_element_...  67.5 us
    dot_general x7, matrix products, contract_rows(): lax.dot_general(left, right, (((0,), (0,)), ((), ())), preferred_element_...  64.4 us
    all_gather x1, waiting for transfers between devices, on_device(): normed_all = lax.all_gather(normed, 'tensor', axis=0, tiled=True)  54.6 us
  transfers between devices with their start and end apart: 23, of which 20 were waited for; matrix products, arithmetic and copies ran while one was open for 27% of the time, Pallas kernels for 0%

commit v1 on v0

v1 whole, which is shorter than its diff:
```python
import functools

import jax
import jax.numpy as jnp
from jax import lax
from jax.experimental import pallas as pl
from jax.experimental.pallas import tpu as pltpu
from jax.sharding import PartitionSpec as P

HEAD_DIM = 64
LEN = 1024
MOST = 512
EPSILON = 1e-05
ROPE_BASE = 130000.0
NEG = -1e30
GROUP = 256
FF_BLOCKS = 4
F32 = jnp.float32
BF16 = jnp.bfloat16
VMEM_BYTES = 56 * 1024 * 1024


def dot_nn(a, b):
    return jnp.dot(a, b, preferred_element_type=F32)


def dot_tn(a, b):
    return lax.dot_general(a, b, (((0,), (0,)), ((), ())), preferred_element_type=F32)


def dot_nt(a, b):
    return lax.dot_general(a, b, (((1,), (1,)), ((), ())), preferred_element_type=F32)


def norm_factor(values):
    return lax.rsqrt(jnp.mean(values * values, axis=-1, keepdims=True) + EPSILON)


def norm_back(values, factor, gain, grads):
    scaled = grads * gain
    grad_in = factor * scaled - values * factor * factor * factor * jnp.mean(
        scaled * values, axis=-1, keepdims=True
    )
    return grad_in, jnp.sum(grads * values * factor, axis=0)


def doc_tables(doc_lengths, tokens):
    ends = jnp.cumsum(doc_lengths, axis=1)[0]
    passed = tokens[:, None] >= ends[None, :]
    segment = jnp.sum(passed.astype(jnp.int32), axis=1)
    start = jnp.sum(jnp.where(passed, doc_lengths, 0), axis=1)
    return segment, tokens - start


def rotary_tables(position):
    half = HEAD_DIM // 2
    inverse = jnp.power(ROPE_BASE, -jnp.arange(half, dtype=F32) * 2.0 / HEAD_DIM)
    angles = position.astype(F32)[:, None] * inverse
    cosine, sine = jnp.cos(angles), jnp.sin(angles)
    heads = GROUP // HEAD_DIM
    return (
        jnp.tile(jnp.concatenate([cosine, cosine], axis=1), (1, heads)),
        jnp.tile(jnp.concatenate([-sine, sine], axis=1), (1, heads)),
    )


def swap_halves(v):
    half, width = HEAD_DIM // 2, v.shape[1]
    lane = lax.broadcasted_iota(jnp.int32, v.shape, 1)
    ahead = pltpu.roll(v, width - half, 1)
    behind = pltpu.roll(v, half, 1)
    return jnp.where(lane % HEAD_DIM < half, ahead, behind)


def key_blocks(i, rows):
    reach = -(-(MOST - 1) // rows)
    return list(range(max(0, i - reach), i + 1))


def fill_bias(bias_ref, seg_col, seg_ref, i, places):
    rows = seg_col.shape[0]
    for n, (j, place) in enumerate(places):
        same = seg_col == seg_ref[place][0:1, :]
        if j == i:
            row = lax.broadcasted_iota(jnp.int32, (rows, rows), 0)
            col = lax.broadcasted_iota(jnp.int32, (rows, rows), 1)
            same = same & (col <= row)
        bias_ref[n] = jnp.where(same, 0.0, NEG)


def attn_forward_kernel(
    blocks, key_ref, x_ref, qo, qs, ko, ks, vo, vs, cos_ref, sin_ref, segc_ref, segr_ref,
    q_ref, k_ref, v_ref, mixed_ref, lse_ref, bias_ref,
):
    rows = LEN // blocks
    half = x_ref.shape[1] // 2
    key = key_ref[0]

    @pl.loop(0, blocks)
    def _(b):
        at = pl.ds(pl.multiple_of(b * rows, rows), rows)
        left, right = x_ref[at, :half], x_ref[at, half:]
        cosine, sine = cos_ref[at, :], sin_ref[at, :]
        query = dot_nn(left, qo[...]) + dot_nn(right, qs[...])
        q_ref[at, :] = (query * cosine + swap_halves(query) * sine).astype(BF16)
        keys = dot_nn(left, ko[...]) + dot_nn(right, ks[...])
        k_ref[at, :] = (keys * cosine + swap_halves(keys) * sine).astype(BF16)
        v_ref[at, :] = (dot_nn(left, vo[...]) + dot_nn(right, vs[...])).astype(BF16)

    head_lane = lax.broadcasted_iota(jnp.int32, (rows, 128), 1)
    for i in range(blocks):
        places = [(j, j ^ key) for j in key_blocks(i, rows)]
        at = pl.ds(pl.multiple_of((i ^ key) * rows, rows), rows)
        fill_bias(bias_ref, segc_ref[at, 0:1], segr_ref, i, places)
        spots = [pl.ds(pl.multiple_of(p * rows, rows), rows) for _, p in places]

        @pl.loop(0, GROUP // 128)
        def _(pair, at=at, spots=spots):
            lanes = pl.ds(pl.multiple_of(pair * 128, 128), 128)
            query = q_ref[at, lanes]
            outs, stats = [], []
            for h in range(2):
                mine = (head_lane < HEAD_DIM) if h == 0 else (head_lane >= HEAD_DIM)
                qm = jnp.where(mine, query, 0) * jnp.asarray(HEAD_DIM**-0.5, BF16)
                scores = [
                    dot_nt(qm, k_ref[s, lanes]) + bias_ref[n] for n, s in enumerate(spots)
                ]
                top = functools.reduce(
                    jnp.maximum, [jnp.max(s, axis=1, keepdims=True) for s in scores]
                )
                weights = [jnp.exp(s - top) for s in scores]
                total = sum(jnp.sum(w, axis=1, keepdims=True) for w in weights)
                out = sum(
                    dot_nn(w.astype(BF16), v_ref[s, lanes]) for w, s in zip(weights, spots)
                )
                outs.append(out / total)
                stats.append(top + jnp.log(total))
            mixed_ref[at, lanes] = jnp.where(head_lane < HEAD_DIM, outs[0], outs[1]).astype(BF16)
            kept = jnp.where(pair == 0, 0.0, lse_ref[at, :])
            for h in range(2):
                kept = jnp.where(head_lane == pair * 2 + h, stats[h], kept)
            lse_ref[at, :] = kept


def attn_forward(blocks, key, x, own, sib, cosine, sine, segc, segr):
    d = x.shape[1]
    cols = own.shape[1] // 4
    steps = cols // GROUP
    rows = LEN // blocks

    def weight(part):
        return pl.BlockSpec((d // 2, GROUP), lambda i, part=part: (0, part * steps + i))

    def whole(shape):
        return pl.BlockSpec(shape, lambda i: (0,) * len(shape))

    col_block = pl.BlockSpec((LEN, GROUP), lambda i: (0, i))
    slab = jax.ShapeDtypeStruct((LEN, cols), BF16)
    return pl.pallas_call(
        functools.partial(attn_forward_kernel, blocks),
        grid=(steps,),
        in_specs=[pl.BlockSpec(memory_space=pltpu.SMEM), whole((LEN, d))]
        + [weight(p) for p in (0, 0, 1, 1, 2, 2)]
        + [whole((LEN, GROUP))] * 2
        + [whole((LEN, 128)), whole(segr.shape)],
        out_specs=[col_block] * 4 + [pl.BlockSpec((LEN, 128), lambda i: (0, i))],
        out_shape=[slab] * 4 + [jax.ShapeDtypeStruct((LEN, 128 * steps), F32)],
        scratch_shapes=[pltpu.VMEM((blocks, rows, rows), F32)],
        compiler_params=pltpu.CompilerParams(vmem_limit_bytes=VMEM_BYTES),
        name="attn_forward",
    )(key, x, own, sib, own, sib, own, sib, cosine, sine, segc, segr)


def attn_backward_kernel(
    blocks, key_ref, g_ref, wo, ws, q_ref, k_ref, v_ref, lse_ref, cos_ref, sin_ref, segc_ref,
    segr_ref, dq_ref, dk_ref, dv_ref, dm_ref, dqa_ref, dka_ref, dva_ref, bias_ref,
):
    rows = LEN // blocks
    half = g_ref.shape[1] // 2
    key = key_ref[0]

    @pl.loop(0, blocks)
    def _(b):
        at = pl.ds(pl.multiple_of(b * rows, rows), rows)
        dm_ref[at, :] = (dot_nn(g_ref[at, :half], wo[...]) + dot_nn(g_ref[at, half:], ws[...])).astype(BF16)
        dka_ref[at, :] = jnp.zeros((rows, GROUP), F32)
        dva_ref[at, :] = jnp.zeros((rows, GROUP), F32)

    head_lane = lax.broadcasted_iota(jnp.int32, (rows, 128), 1)
    scale = HEAD_DIM**-0.5
    for i in range(blocks):
        places = [(j, j ^ key) for j in key_blocks(i, rows)]
        at = pl.ds(pl.multiple_of((i ^ key) * rows, rows), rows)
        fill_bias(bias_ref, segc_ref[at, 0:1], segr_ref, i, places)
        spots = [pl.ds(pl.multiple_of(p * rows, rows), rows) for _, p in places]

        @pl.loop(0, GROUP // 128)
        def _(pair, at=at, spots=spots):
            lanes = pl.ds(pl.multiple_of(pair * 128, 128), 128)
            query, grad = q_ref[at, lanes], dm_ref[at, lanes]
            logs = lse_ref[at, :]
            outs = []
            for h in range(2):
                mine = (head_lane < HEAD_DIM) if h == 0 else (head_lane >= HEAD_DIM)
                qm = jnp.where(mine, query, 0) * jnp.asarray(scale, BF16)
                gm = jnp.where(mine, grad, 0)
                log = jnp.sum(
                    jnp.where(head_lane == pair * 2 + h, logs, 0.0), axis=1, keepdims=True
                )
                weights = [
                    jnp.exp(dot_nt(qm, k_ref[s, lanes]) + bias_ref[n] - log)
                    for n, s in enumerate(spots)
                ]
                grads = [dot_nt(gm, v_ref[s, lanes]) for s in spots]
                inner = sum(
                    jnp.sum(w * g, axis=1, keepdims=True) for w, g in zip(weights, grads)
                )
                dq = jnp.zeros((rows, 128), F32)
                for w, g, s in zip(weights, grads, spots):
                    ds = (w * (g - inner)).astype(BF16)
                    dva_ref[s, lanes] += dot_tn(w.astype(BF16), gm)
                    dka_ref[s, lanes] += dot_tn(ds, qm)
                    dq = dq + dot_nn(ds, k_ref[s, lanes])
                outs.append(dq)
            dqa_ref[at, lanes] = jnp.where(head_lane < HEAD_DIM, outs[0], outs[1]) * scale

    @pl.loop(0, blocks)
    def _(b):
        at = pl.ds(pl.multiple_of(b * rows, rows), rows)
        cosine, sine = cos_ref[at, :], sin_ref[at, :]
        dq = dqa_ref[at, :]
        dq_ref[at, :] = (dq * cosine - swap_halves(dq) * sine).astype(BF16)
        dk = dka_ref[at, :]
        dk_ref[at, :] = (dk * cosine - swap_halves(dk) * sine).astype(BF16)
        dv_ref[at, :] = dva_ref[at, :].astype(BF16)


def attn_backward(blocks, key, g, own, sib, q, k, v, lse, cosine, sine, segc, segr):
    d = g.shape[1]
    cols = q.shape[1]
    steps = cols // GROUP
    rows = LEN // blocks

    def whole(shape):
        return pl.BlockSpec(shape, lambda i: (0,) * len(shape))

    col_block = pl.BlockSpec((LEN, GROUP), lambda i: (0, i))
    weight = pl.BlockSpec((d // 2, GROUP), lambda i: (0, 3 * steps + i))
    slab = jax.ShapeDtypeStruct((LEN, cols), BF16)
    return pl.pallas_call(
        functools.partial(attn_backward_kernel, blocks),
        grid=(steps,),
        in_specs=[pl.BlockSpec(memory_space=pltpu.SMEM), whole((LEN, d)), weight, weight]
        + [col_block] * 3
        + [pl.BlockSpec((LEN, 128), lambda i: (0, i))]
        + [whole((LEN, GROUP))] * 2
        + [whole((LEN, 128)), whole(segr.shape)],
        out_specs=[col_block] * 3,
        out_shape=[slab] * 3,
        scratch_shapes=[
            pltpu.VMEM((LEN, GROUP), BF16),
            pltpu.VMEM((LEN, GROUP), F32),
            pltpu.VMEM((LEN, GROUP), F32),
            pltpu.VMEM((LEN, GROUP), F32),
            pltpu.VMEM((blocks, rows, rows), F32),
        ],
        compiler_params=pltpu.CompilerParams(vmem_limit_bytes=VMEM_BYTES),
        name="attn_backward",
    )(key, g, own, sib, q, k, v, lse, cosine, sine, segc, segr)


def on_device(
    dp, tensor, hidden_in, doc_lengths, gain_attn, w_query, w_key, w_value, w_out, gain_mlp,
    w_gate, w_up, w_down, cotangent,
):
    line = dp // 2
    core = lax.axis_index("dp") % 2
    place = lax.axis_index("tensor")
    square = tensor == 4
    same_core = [[c + 2 * z for z in range(line)] for c in range(2)]
    sibling = [(i, i ^ 1) for i in range(dp)]
    d = hidden_in.shape[1]
    local = hidden_in.shape[0]

    def own_first(a):
        s = a.reshape(a.shape[:-1] + (line, 2, d // dp))
        even, odd = s[..., 0, :], s[..., 1, :]
        out = jnp.concatenate(
            [jnp.where(core == 0, even, odd), jnp.where(core == 0, odd, even)], axis=-2
        )
        return out.reshape(a.shape)

    def true_order(a):
        s = a.reshape(a.shape[:-1] + (2, line, d // dp))
        first, second = s[..., 0, :, :], s[..., 1, :, :]
        out = jnp.stack(
            [jnp.where(core == 0, first, second), jnp.where(core == 0, second, first)], axis=-2
        )
        return out.reshape(a.shape)

    def hop(a, step):
        return lax.ppermute(a, "tensor", [(i, i ^ step) for i in range(tensor)])

    def gather_rows(a):
        if not square:
            return lax.all_gather(a, "tensor", axis=0, tiled=True)
        half = a.shape[0] // 2
        from_x, from_y = hop(a, 1), hop(a, 2)
        top, bottom = hop(from_x[:half], 2), hop(from_y[half:], 1)
        return jnp.concatenate([a, from_x, from_y, top, bottom], axis=0)

    def scatter_rows(a):
        if not square:
            return lax.psum_scatter(a, "tensor", scatter_dimension=0, tiled=True).astype(F32)
        n = a.shape[0] // 4
        half = n // 2
        top = hop(a[3 * n : 3 * n + half], 2)
        bottom = hop(a[3 * n + half :], 1)
        for_x = jnp.concatenate([a[n : n + half] + top, a[n + half : 2 * n]], axis=0)
        for_y = jnp.concatenate([a[2 * n : 2 * n + half], a[2 * n + half : 3 * n] + bottom], axis=0)
        return (a[:n].astype(F32) + hop(for_x, 1).astype(F32)) + hop(for_y, 2).astype(F32)

    def line_gather(a):
        own = lax.all_gather(a, "dp", axis=0, axis_index_groups=same_core, tiled=True)
        return own, lax.ppermute(own, "dp", sibling)

    def line_scatter(own, sib):
        mine = own + lax.ppermute(sib, "dp", sibling)
        return lax.psum_scatter(
            mine, "dp", scatter_dimension=0, axis_index_groups=same_core, tiled=True
        ).astype(F32)

    blocks = 4
    rows = LEN // blocks
    key = place if square else jnp.zeros((), jnp.int32)
    tokens = (
        (jnp.arange(blocks, dtype=jnp.int32) ^ key)[:, None] * rows
        + jnp.arange(rows, dtype=jnp.int32)[None, :]
    ).reshape(LEN)
    segment, position = doc_tables(doc_lengths, tokens)
    cosine, sine = rotary_tables(position)
    segc = jnp.broadcast_to(segment[:, None], (LEN, 128))
    segr = jnp.broadcast_to(segment.reshape(blocks, 1, rows), (blocks, 8, rows))
    key = key.reshape(1)

    gains = lax.all_gather(jnp.stack([gain_attn, gain_mlp]), "dp", axis=0)
    gains = own_first(jnp.moveaxis(gains, 0, 1).reshape(2, d)).astype(F32)
    gain_one, gain_two = gains[0], gains[1]

    ff = w_gate.shape[1]
    fb = ff // FF_BLOCKS
    attn_own, attn_sib = line_gather(
        jnp.concatenate([w_query, w_key, w_value, w_out.T], axis=1)
    )
    down_t = w_down.T
    ff_sets = []
    for b in range(FF_BLOCKS):
        cut = slice(b * fb, (b + 1) * fb)
        own, sib = line_gather(
            jnp.concatenate([w_gate[:, cut], w_up[:, cut], down_t[:, cut]], axis=1)
        )
        ff_sets.append(jnp.concatenate([own, sib], axis=0))

    inputs = own_first(hidden_in).astype(F32)
    g_local = own_first(cotangent)
    factor_one = norm_factor(inputs)
    normed = gather_rows((inputs * factor_one * gain_one).astype(BF16))
    g_all = gather_rows(g_local)

    query, keys, values, mixed, lse = attn_forward(
        blocks, key, normed, attn_own, attn_sib, cosine, sine, segc, segr
    )
    cols = query.shape[1]
    out_own, out_sib = attn_own[:, 3 * cols :], attn_sib[:, 3 * cols :]
    attended = jnp.concatenate(
        [dot_nt(mixed, out_own).astype(BF16), dot_nt(mixed, out_sib).astype(BF16)], axis=1
    )
    middle = inputs + scatter_rows(attended)
    factor_two = norm_factor(middle)
    normed_mlp = gather_rows((middle * factor_two * gain_two).astype(BF16))

    down_sum = jnp.zeros((LEN, d), F32)
    back_sum = jnp.zeros((LEN, d), F32)
    ff_grads = []
    for b in range(FF_BLOCKS):
        gate_w, up_w, down_w = jnp.split(ff_sets[b], 3, axis=1)
        gate_pre = dot_nn(normed_mlp, gate_w)
        upward = dot_nn(normed_mlp, up_w)
        grad_hidden = dot_nn(g_all, down_w)
        sig = jax.nn.sigmoid(gate_pre)
        activated = gate_pre * sig
        hidden = (activated * upward).astype(BF16)
        grad_gate_pre = (grad_hidden * upward * sig * (1.0 + gate_pre * (1.0 - sig))).astype(BF16)
        grad_upward = (grad_hidden * activated).astype(BF16)
        down_sum = down_sum + dot_nt(hidden, down_w)
        back_sum = back_sum + dot_nt(grad_gate_pre, gate_w) + dot_nt(grad_upward, up_w)
        grad = jnp.concatenate(
            [
                dot_tn(normed_mlp, grad_gate_pre).astype(BF16),
                dot_tn(normed_mlp, grad_upward).astype(BF16),
                dot_tn(g_all, hidden).astype(BF16),
            ],
            axis=1,
        )
        ff_grads.append(line_scatter(grad[: d // 2], grad[d // 2 :]))
    grad_norm_two = scatter_rows(back_sum.astype(BF16))
    output = true_order((middle + scatter_rows(down_sum.astype(BF16))).astype(BF16))
    grad_mid_norm, gain_two_part = norm_back(middle, factor_two, gain_two, grad_norm_two)
    grad_middle = g_local.astype(F32) + grad_mid_norm
    grad_mid_all = gather_rows(grad_middle.astype(BF16))

    dq, dk, dv = attn_backward(
        blocks, key, grad_mid_all, attn_own, attn_sib, query, keys, values, lse, cosine, sine,
        segc, segr,
    )
    grad = jnp.concatenate(
        [dot_tn(normed, dq), dot_tn(normed, dk), dot_tn(normed, dv), dot_tn(grad_mid_all, mixed)],
        axis=1,
    ).astype(BF16)
    attn_grads = line_scatter(grad[: d // 2], grad[d // 2 :])
    rows_grad = jnp.concatenate([dq, dk, dv], axis=1)
    back = jnp.concatenate(
        [
            dot_nt(rows_grad, attn_own[:, : 3 * cols]).astype(BF16),
            dot_nt(rows_grad, attn_sib[:, : 3 * cols]).astype(BF16),
        ],
        axis=1,
    )
    grad_in_norm, gain_one_part = norm_back(inputs, factor_one, gain_one, scatter_rows(back))
    input_grad = true_order(grad_middle + grad_in_norm)

    parts = true_order(jnp.stack([gain_one_part, gain_two_part])).reshape(2 * d)
    shares = lax.all_gather(parts, ("dp", "tensor"), axis=0)
    gain_sum = jnp.sum(shares, axis=0).reshape(2, d)
    share = d // (dp * tensor)
    first = (lax.axis_index("dp") * tensor + place) * share
    gain_sum = lax.dynamic_slice_in_dim(gain_sum, first, share, 1)

    return (
        output,
        input_grad,
        gain_sum[0],
        attn_grads[:, :cols],
        attn_grads[:, cols : 2 * cols],
        attn_grads[:, 2 * cols : 3 * cols],
        attn_grads[:, 3 * cols :].T,
        gain_sum[1],
        jnp.concatenate([g[:, :fb] for g in ff_grads], axis=1),
        jnp.concatenate([g[:, fb : 2 * fb] for g in ff_grads], axis=1),
        jnp.concatenate([g[:, 2 * fb :] for g in ff_grads], axis=1).T,
    )


def solution(mesh):
    shape = dict(mesh.shape)
    return jax.shard_map(
        functools.partial(on_device, shape["dp"], shape["tensor"]),
        mesh=mesh,
        in_specs=(
            P(("dp", "tensor"), None),
            P("dp", None),
            P("dp"),
            P("dp", "tensor"),
            P("dp", "tensor"),
            P("dp", "tensor"),
            P("tensor", "dp"),
            P("dp"),
            P("dp", "tensor"),
            P("dp", "tensor"),
            P("tensor", "dp"),
            P(("dp", "tensor"), None),
        ),
        out_specs=(
            P(("dp", "tensor"), None),
            P(("dp", "tensor"), None),
            P(("dp", "tensor")),
            P("dp", "tensor"),
            P("dp", "tensor"),
            P("dp", "tensor"),
            P("tensor", "dp"),
            P(("dp", "tensor")),
            P("dp", "tensor"),
            P("dp", "tensor"),
            P("tensor", "dp"),
        ),
        check_vma=False,
    )
```

time: 1490 us -> 1100 us (0.74)
  waiting for transfers between devices: 959 us -> 384 us
  matrix products: 359 us -> 272 us
  Pallas kernels: 0 us -> 67.6 us
  blocking collectives: 23.8 us -> 88 us
  local copies, waits for them, and re-layouts: 59.1 us -> 120 us
  other arithmetic: 54.6 us -> 105 us
  starting transfers between devices: 1.47 us -> 37.8 us
    reduce_scatter x11 -> x5, waiting for transfers between devices: 373 us -> 0.01 us  [line_scatter(): lax.psum_scatter(mine, 'dp', scatter_dimension=0, axis_index_groups=same_...]
    all_gather x11 -> x5, waiting for transfers between devices: 449 us -> 168 us  [line_gather(): lax.all_gather(a, 'dp', axis=0, axis_index_groups=same_core, tiled=True)]
    ppermute x0 -> x42, waiting for transfers between devices: none -> 215 us  [the longest x32 215 us: hop(): return lax.ppermute(a, 'tensor', [(i, i ^ step) for i in range(tensor)])]
    unnamed x24 -> x10, waiting for transfers between devices: 137 us -> 0.16 us
    dot_general x35 -> x44, matrix products: 359 us -> 272 us  [the longest x16 116 us: dot_nt(): lax.dot_general(a, b, (((1,), (1,)), ((), ())), preferred_element_type=F32)]
    pallas_call x0 -> x2, Pallas kernels: none -> 67.6 us  [the longest x1 37.5 us: attn_backward(): pl.pallas_call(functools.partial(attn_backward_kernel, blocks), grid=(ste...]
    all_gather x2, blocking collectives: 23.8 us -> 88 us  [the longest x1 74 us: on_device(): shares = lax.all_gather(parts, ('dp', 'tensor'), axis=0)]
    unnamed x82 -> x224, local copies, waits for them, and re-layouts: 5.66 us -> 55.2 us
  transfers between devices with their start and end apart: 23 -> 52, of which waited for: 20 -> 24; matrix products, arithmetic and copies ran while one was open for 27% -> 39% of each run, Pallas kernels for 0% -> 6%
where the time goes in v1:
time: 1100 us; the launch traced here: 1090 us
  waiting for transfers between devices  384 us (35%)
  matrix products  272 us (25%)
  local copies, waits for them, and re-layouts  120 us (11%)
  other arithmetic  105 us (10%)
  blocking collectives  88 us (8%)
  Pallas kernels  67.6 us (6%)
  starting transfers between devices  37.8 us (3%)
  between operations  16.1 us (1%)
    ppermute x32, waiting for transfers between devices, hop(): return lax.ppermute(a, 'tensor', [(i, i ^ step) for i in range(tensor)])  215 us
    all_gather x5, waiting for transfers between devices, line_gather(): lax.all_gather(a, 'dp', axis=0, axis_index_groups=same_core, tiled=True)  168 us
    dot_general x16, matrix products, dot_nt(): lax.dot_general(a, b, (((1,), (1,)), ((), ())), preferred_element_type=F32)  116 us
    dot_general x16, matrix products, dot_tn(): lax.dot_general(a, b, (((0,), (0,)), ((), ())), preferred_element_type=F32)  81.3 us
    all_gather x1, blocking collectives, on_device(): shares = lax.all_gather(parts, ('dp', 'tensor'), axis=0)  74 us
    dot_general x12, matrix products, dot_nn(): return jnp.dot(a, b, preferred_element_type=F32)  73.9 us
    unnamed x224, local copies, waits for them, and re-layouts  55.2 us
    pallas_call x1, Pallas kernels, attn_backward(): pl.pallas_call(functools.partial(attn_backward_kernel, blocks), grid=(ste...  37.5 us
  transfers between devices with their start and end apart: 52, of which 24 were waited for; matrix products, arithmetic and copies ran while one was open for 39% of the time, Pallas kernels for 6%

profile of v1, /device:TPU:0, one launch (start us, length us, event | category | flops | bytes accessed | tf_op | source)
XLA Modules:
  0.0 1090.0 jit_solution(5482817322914816189)
XLA Ops:
  26.5 13.9 %all-gather.1 = bf16[8,2,256]{2,1,0:T(2,128)(2,1)S(1)} all-gather(bf16[1,2,256]{2,1,0:T(2,128)(2,1)S(1)} %maximum_bitcast_fusion.1), channel_id=2, replica_groups=mesh['dp'=8,'tensor'=4] {'dp'}, dimensions={0}, use_global_device_ids=true | all-gather | bytes 9216 | tf_op jit(solution)/shard_map/all_gather | solution.py:346
  41.8 52.6 %all-gather.9.cloned.1.call-done.qo.ko.vo.wo = bf16[1024,2048]{1,0:T(8,128)(2,1)} async-done(((bf16[256,2048]{1,0:T(8,128)(2,1)}), bf16[1024,2048]{1,0:T(8,128)(2,1)}) %all-gather.9.cloned.1.call-update) | async-done | bytes 4194320 | tf_op jit(solution)/shard_map/all_gather | solution.py:324
  127.5 17.2 %collective-permute-done.21 = bf16[256,2048]{1,0:T(8,128)(2,1)} collective-permute-done((bf16[256,2048]{1,0:T(8,128)(2,1)S(1)}, bf16[256,2048]{1,0:T(8,128)(2,1)}, u32[]{:S(2)}, u32[]{:S(2)}) %collective-permute-start.21) | collective-permute-done | bytes 1048608 | tf_op jit(solution)/shard_map/ppermute | solution.py:302
  169.6 52.1 %all-gather.13.cloned.1.call-done = bf16[1024,1536]{0,1:T(8,128)(2,1)} async-done(((bf16[256,1536]{0,1:T(8,128)(2,1)}), bf16[1024,1536]{0,1:T(8,128)(2,1)}) %all-gather.13.cloned.1.call-update) | async-done | bytes 3145744 | tf_op jit(solution)/shard_map/all_gather | solution.py:324
  221.7 63.6 %all-gather.15.cloned.1.call-done = bf16[1024,1536]{0,1:T(8,128)(2,1)} async-done(((bf16[256,1536]{0,1:T(8,128)(2,1)}), bf16[1024,1536]{0,1:T(8,128)(2,1)}) %all-gather.15.cloned.1.call-update) | async-done | bytes 3145744 | tf_op jit(solution)/shard_map/all_gather | solution.py:324
  286.9 30.0 %attn_forward.1 = (bf16[1024,512]{1,0:T(8,128)(2,1)}, bf16[1024,512]{1,0:T(8,128)(2,1)}, bf16[1024,512]{1,0:T(8,128)(2,1)}, bf16[1024,512]{1,0:T(8,128)(2,1)}, f32[1024,256]{1,0:T(8,128)}) custom-call(s32[1]{0:T(128)} %bitcast.2.key_ref, bf16[1024,2048]{1,0:T(8,128)(2,1)} %constant_dynamic-update-slice_fusion.x_ref, ...), custom_call_target="tpu_custom_call" | custom-call | tf_op jit(solution)/shard_map/attn_forward/pallas_call | solution.py:159
  342.3 10.6 collective-permute-done.7
  390.2 8.1 fusion.28
  463.7 10.1 pad_maximum_fusion.1
  496.6 10.0 pad_maximum_fusion.2
  532.0 10.2 pad_maximum_fusion.3
  588.9 8.7 multiply_convert_fusion
  597.6 12.2 %add_convert_fusion.1 = bf16[1024,2048]{1,0:T(8,128)(2,1)S(1)} fusion(f32[1024,2048]{1,0:T(8,128)} %fusion.30, f32[1024,2048]{1,0:T(8,128)} %fusion.54, f32[1024,2048]{1,0:T(8,128)} %fusion.42, bf16[1024,512]{1,0:T(8,128)(2,1)S(1)} %get-tuple-element.107, bf16[2048,1536]{0,1:T(8,128)(2,1)} %copy-done.18), kind=kOutput, calls=%fused_computation.2 | convolution fusion | flops 2155872256 | bytes 32505856 | tf_op jit(solution)/shard_map/dot_general | solution.py:32
  612.0 8.1 fusion.60
  656.0 20.9 %add_convert_fusion = bf16[1024,2048]{1,0:T(8,128)(2,1)S(1)} fusion(f32[1024,2048]{1,0:T(8,128)} %fusion.24, f32[1024,2048]{1,0:T(8,128)} %fusion.32, f32[1024,2048]{1,0:T(8,128)} %fusion.36, f32[1024,2048]{1,0:T(8,128)} %fusion.44, f32[1024,2048]{1,0:T(8,128)} %fusion.48, f32[1024,2048]{1,0:T(8,128)} %fusion.60, f32[1024,2048]{1,0:T(8,128)} %fusion.56, ...), kind=kOutput, calls=%fused_computation.1 | convolution fusion | flops 2164260864 | bytes 66060288 | tf_op jit(solution)/shard_map/dot_general | solution.py:32
  709.0 28.0 %collective-permute-done.19 = bf16[128,2048]{1,0:T(8,128)(2,1)} collective-permute-done((bf16[128,2048]{1,0:T(8,128)(2,1)}, bf16[128,2048]{1,0:T(8,128)(2,1)}, u32[]{:S(2)}, u32[]{:S(2)}) %collective-permute-start.19) | collective-permute-done | bytes 524320 | tf_op jit(solution)/shard_map/ppermute | solution.py:302
  739.7 30.6 %collective-permute-done.27 = bf16[128,2048]{1,0:T(8,128)(2,1)S(1)} collective-permute-done((bf16[128,2048]{1,0:T(8,128)(2,1)S(1)}, bf16[128,2048]{1,0:T(8,128)(2,1)S(1)}, u32[]{:S(2)}, u32[]{:S(2)}) %collective-permute-start.27) | collective-permute-done | bytes 524320 | tf_op jit(solution)/shard_map/ppermute | solution.py:302
  775.2 20.3 %collective-permute-done.28 = bf16[256,2048]{1,0:T(8,128)(2,1)S(1)} collective-permute-done((bf16[256,2048]{1,0:T(8,128)(2,1)S(1)}, bf16[256,2048]{1,0:T(8,128)(2,1)S(1)}, u32[]{:S(2)}, u32[]{:S(2)}) %collective-permute-start.28) | collective-permute-done | bytes 1048608 | tf_op jit(solution)/shard_map/ppermute | solution.py:302
  804.0 22.4 %collective-permute-done.29 = bf16[256,2048]{1,0:T(8,128)(2,1)S(1)} collective-permute-done((bf16[256,2048]{1,0:T(8,128)(2,1)S(1)}, bf16[256,2048]{1,0:T(8,128)(2,1)S(1)}, u32[]{:S(2)}, u32[]{:S(2)}) %collective-permute-start.29) | collective-permute-done | bytes 1048608 | tf_op jit(solution)/shard_map/ppermute | solution.py:302
  847.6 37.5 %attn_backward.1 = (bf16[1024,512]{1,0:T(8,128)(2,1)}, bf16[1024,512]{1,0:T(8,128)(2,1)}, bf16[1024,512]{1,0:T(8,128)(2,1)}) custom-call(s32[1]{0:T(128)} %bitcast.2.key_ref, bf16[1024,2048]{1,0:T(8,128)(2,1)} %constant_dynamic-update-slice_fusion.23.g_ref, bf16[1024,2048]{1,0:T(8,128)(2,1)} %all-gather.9.cloned.1.call-done.qo.ko.vo.wo, ...), custom_call_target="tpu_custom_call" | custom-call | tf_op jit(solution)/shard_map/attn_backward/pallas_call | solution.py:250
  916.6 10.4 collective-permute-done.33
  931.5 11.8 %collective-permute-done.35 = bf16[128,2048]{1,0:T(8,128)(2,1)S(1)} collective-permute-done((bf16[128,2048]{1,0:T(8,128)(2,1)S(1)}, bf16[128,2048]{1,0:T(8,128)(2,1)S(1)}, u32[]{:S(2)}, u32[]{:S(2)}) %collective-permute-start.35) | collective-permute-done | bytes 524320 | tf_op jit(solution)/shard_map/ppermute | solution.py:302
  956.1 7.9 collective-permute-done.34
  970.3 74.0 %all-gather.2 = f32[32,1,4096]{2,1,0:T(1,128)} all-gather(f32[1,1,4096]{2,1,0:T(1,128)S(1)} %reshape.296), channel_id=1, replica_groups=mesh['dp'=8,'tensor'=4] {'dp','tensor'}, dimensions={0}, use_global_device_ids=true | all-gather | bytes 540672 | tf_op jit(solution)/shard_map/all_gather | solution.py:433
  (501 shorter events, 502.7 us)
Async XLA Ops:
  7.2 87.2 %all-gather.9.cloned.1.call-start = ((), (), s32[]{:S(2)}) async-start(), calls=%async_computation.5 | async-start | bytes 5242880 | tf_op jit(solution)/shard_map/all_gather | solution.py:324
  10.7 158.9 %all-gather.11.cloned.1.call-start = ((), (), s32[]{:S(2)}) async-start(), calls=%async_computation.6 | async-start | bytes 3932160 | tf_op jit(solution)/shard_map/all_gather | solution.py:324
  15.7 206.0 %all-gather.13.cloned.1.call-start = ((), (), s32[]{:S(2)}) async-start(), calls=%async_computation.7 | async-start | bytes 3932160 | tf_op jit(solution)/shard_map/all_gather | solution.py:324
  17.0 268.3 %all-gather.15.cloned.1.call-start = ((), (), s32[]{:S(2)}) async-start(), calls=%async_computation.8 | async-start | bytes 3932160 | tf_op jit(solution)/shard_map/all_gather | solution.py:324
  19.3 336.3 %all-gather.17.cloned.1.call-start = ((), (), s32[]{:S(2)}) async-start(), calls=%async_computation.9 | async-start | bytes 3932160 | tf_op jit(solution)/shard_map/all_gather | solution.py:324
  94.4 190.9 %collective-permute-start.4 = (bf16[1024,2048]{1,0:T(8,128)(2,1)}, bf16[1024,2048]{1,0:T(8,128)(2,1)}, u32[]{:S(2)}, u32[]{:S(2)}) collective-permute-start(bf16[1024,2048]{1,0:T(8,128)(2,1)} %all-gather.9.cloned.1.call-done.qo.ko.vo.wo), channel_id=1, source_target_pairs={{0,4},{4,0},{8,12},{12,8},{16,20},{20,16},{24,28},{28,24},{1,5},{5... | collective-permute-start | bytes 12582920 | tf_op jit(solution)/shard_map/ppermute | solution.py:325
  100.5 46.9 %collective-permute-start.22 = (bf16[256,2048]{1,0:T(8,128)(2,1)S(1)}, bf16[256,2048]{1,0:T(8,128)(2,1)}, u32[]{:S(2)}, u32[]{:S(2)}) collective-permute-start(bf16[256,2048]{1,0:T(8,128)(2,1)S(1)} %bitcast.155), channel_id=1, source_target_pairs={{0,2},{1,3},{2,0},{3,1},{4,6},{5,7},{6,4},{7,5},{8,10},{9,11},{10,... | collective-permute-start | bytes 3145736 | tf_op jit(solution)/shard_map/ppermute | solution.py:302
  105.9 953.6 %reduce-scatter.8.cloned.1.call-start = ((), (), s32[]{:S(2)}) async-start(), calls=%async_computation.11 | async-start | bytes 3932160 | tf_op jit(solution)/shard_map/reduce_scatter | solution.py:329
  169.6 214.0 %collective-permute-start.13 = (bf16[1024,1536]{0,1:T(8,128)(2,1)}, bf16[1024,1536]{0,1:T(8,128)(2,1)}, u32[]{:S(2)}, u32[]{:S(2)}) collective-permute-start(bf16[1024,1536]{0,1:T(8,128)(2,1)} %all-gather.11.cloned.1.call-done), channel_id=1, source_target_pairs={{0,4},{4,0},{8,12},{12,8},{16,20},{20,16},{24,28},{28,24},{1,5},{5... | collective-permute-start | bytes 9437192 | tf_op jit(solution)/shard_map/ppermute | solution.py:325
  221.7 136.3 %collective-permute-start.14 = (bf16[1024,1536]{0,1:T(8,128)(2,1)}, bf16[1024,1536]{0,1:T(8,128)(2,1)}, u32[]{:S(2)}, u32[]{:S(2)}) collective-permute-start(bf16[1024,1536]{0,1:T(8,128)(2,1)} %all-gather.13.cloned.1.call-done), channel_id=1, source_target_pairs={{0,4},{4,0},{8,12},{12,8},{16,20},{20,16},{24,28},{28,24},{1,5},{5... | collective-permute-start | bytes 9437192 | tf_op jit(solution)/shard_map/ppermute | solution.py:325
  285.3 102.1 %collective-permute-start.15 = (bf16[1024,1536]{0,1:T(8,128)(2,1)}, bf16[1024,1536]{0,1:T(8,128)(2,1)}, u32[]{:S(2)}, u32[]{:S(2)}) collective-permute-start(bf16[1024,1536]{0,1:T(8,128)(2,1)} %all-gather.15.cloned.1.call-done), channel_id=1, source_target_pairs={{0,4},{4,0},{8,12},{12,8},{16,20},{20,16},{24,28},{28,24},{1,5},{5... | collective-permute-start | bytes 9437192 | tf_op jit(solution)/shard_map/ppermute | solution.py:325
  358.4 47.1 %collective-permute-start.16 = (bf16[1024,1536]{0,1:T(8,128)(2,1)S(1)}, bf16[1024,1536]{0,1:T(8,128)(2,1)S(1)}, u32[]{:S(2)}, u32[]{:S(2)}) collective-permute-start(bf16[1024,1536]{0,1:T(8,128)(2,1)S(1)} %copy-done.23), channel_id=1, source_target_pairs={{0,4},{4,0},{8,12},{12,8},{16,20},{20,16},{24,28},{28,24},{1,5},{5... | collective-permute-start | bytes 9437192 | tf_op jit(solution)/shard_map/ppermute | solution.py:325
  474.3 112.4 %collective-permute-start.38 = (bf16[1024,1536]{0,1:T(8,128)(2,1)S(1)}, bf16[1024,1536]{0,1:T(8,128)(2,1)S(1)}, u32[]{:S(2)}, u32[]{:S(2)}) collective-permute-start(bf16[1024,1536]{0,1:T(8,128)(2,1)S(1)} %slice.453), channel_id=1, source_target_pairs={{0,4},{4,0},{8,12},{12,8},{16,20},{20,16},{24,28},{28,24},{1,5},{5... | collective-permute-start | bytes 9437192 | tf_op jit(solution)/shard_map/ppermute | solution.py:328
  509.8 141.0 %collective-permute-start.39 = (bf16[1024,1536]{0,1:T(8,128)(2,1)S(1)}, bf16[1024,1536]{0,1:T(8,128)(2,1)}, u32[]{:S(2)}, u32[]{:S(2)}) collective-permute-start(bf16[1024,1536]{0,1:T(8,128)(2,1)S(1)} %slice.456), channel_id=1, source_target_pairs={{0,4},{4,0},{8,12},{12,8},{16,20},{20,16},{24,28},{28,24},{1,5},{5... | collective-permute-start | bytes 9437192 | tf_op jit(solution)/shard_map/ppermute | solution.py:328
  545.8 156.8 %collective-permute-start.40 = (bf16[1024,1536]{0,1:T(8,128)(2,1)}, bf16[1024,1536]{0,1:T(8,128)(2,1)}, u32[]{:S(2)}, u32[]{:S(2)}) collective-permute-start(bf16[1024,1536]{0,1:T(8,128)(2,1)} %slice.459), channel_id=1, source_target_pairs={{0,4},{4,0},{8,12},{12,8},{16,20},{20,16},{24,28},{28,24},{1,5},{5... | collective-permute-start | bytes 9437192 | tf_op jit(solution)/shard_map/ppermute | solution.py:328
  588.7 473.0 %reduce-scatter.10.cloned.1.call-start = ((), (), s32[]{:S(2)}) async-start(), calls=%async_computation.12 | async-start | bytes 3932160 | tf_op jit(solution)/shard_map/reduce_scatter | solution.py:329
  610.7 85.7 %collective-permute-start.17 = (bf16[128,2048]{1,0:T(8,128)(2,1)}, bf16[128,2048]{1,0:T(8,128)(2,1)}, u32[]{:S(2)}, u32[]{:S(2)}) collective-permute-start(bf16[128,2048]{1,0:T(8,128)(2,1)} %slice.408), channel_id=1, source_target_pairs={{0,2},{1,3},{2,0},{3,1},{4,6},{5,7},{6,4},{7,5},{8,10},{9,11},{10,... | collective-permute-start | bytes 1572872 | tf_op jit(solution)/shard_map/ppermute | solution.py:302
  654.8 409.1 %reduce-scatter.12.cloned.1.call-start = ((), (), s32[]{:S(2)}) async-start(), calls=%async_computation.13 | async-start | bytes 3932160 | tf_op jit(solution)/shard_map/reduce_scatter | solution.py:329
  699.5 75.6 %collective-permute-start.18 = (bf16[256,2048]{1,0:T(8,128)(2,1)}, bf16[256,2048]{1,0:T(8,128)(2,1)}, u32[]{:S(2)}, u32[]{:S(2)}) collective-permute-start(bf16[256,2048]{1,0:T(8,128)(2,1)} %pad_maximum_fusion.11), channel_id=1, source_target_pairs={{0,1},{1,0},{2,3},{3,2},{4,5},{5,4},{6,7},{7,6},{8,9},{9,8},{10,11... | collective-permute-start | bytes 3145736 | tf_op jit(solution)/shard_map/ppermute | solution.py:302
  706.6 359.6 %reduce-scatter.14.cloned.1.call-start = ((), (), s32[]{:S(2)}) async-start(), calls=%async_computation.14 | async-start | bytes 3932160 | tf_op jit(solution)/shard_map/reduce_scatter | solution.py:329
  706.9 68.2 %collective-permute-start.26 = (bf16[256,2048]{1,0:T(8,128)(2,1)S(1)}, bf16[256,2048]{1,0:T(8,128)(2,1)S(1)}, u32[]{:S(2)}, u32[]{:S(2)}) collective-permute-start(bf16[256,2048]{1,0:T(8,128)(2,1)S(1)} %pad_maximum_fusion.15), channel_id=1, source_target_pairs={{0,1},{1,0},{2,3},{3,2},{4,5},{5,4},{6,7},{7,6},{8,9},{9,8},{10,11... | collective-permute-start | bytes 3145736 | tf_op jit(solution)/shard_map/ppermute | solution.py:302
  707.6 62.7 %collective-permute-start.27 = (bf16[128,2048]{1,0:T(8,128)(2,1)S(1)}, bf16[128,2048]{1,0:T(8,128)(2,1)S(1)}, u32[]{:S(2)}, u32[]{:S(2)}) collective-permute-start(bf16[128,2048]{1,0:T(8,128)(2,1)S(1)} %copy-done.45), channel_id=1, source_target_pairs={{0,1},{1,0},{2,3},{3,2},{4,5},{5,4},{6,7},{7,6},{8,9},{9,8},{10,11... | collective-permute-start | bytes 1572872 | tf_op jit(solution)/shard_map/ppermute | solution.py:302
  775.0 53.3 %collective-permute-start.41 = (bf16[1024,1536]{0,1:T(8,128)(2,1)S(1)}, bf16[1024,1536]{0,1:T(8,128)(2,1)S(1)}, u32[]{:S(2)}, u32[]{:S(2)}) collective-permute-start(bf16[1024,1536]{0,1:T(8,128)(2,1)S(1)} %slice.462), channel_id=1, source_target_pairs={{0,4},{4,0},{8,12},{12,8},{16,20},{20,16},{24,28},{28,24},{1,5},{5... | collective-permute-start | bytes 9437192 | tf_op jit(solution)/shard_map/ppermute | solution.py:328
  830.4 247.2 %reduce-scatter.6.cloned.1.call-start = ((), (), s32[]{:S(2)}) async-start(), calls=%async_computation.10 | async-start | bytes 5242880 | tf_op jit(solution)/shard_map/reduce_scatter | solution.py:329
  (121 other events, 2654.4 us)
Sparse Core Ops, SparseCore 0:
  10.8 83.5 all-gather.8
  96.0 61.8 all-gather.10
  160.0 61.5 all-gather.12
  223.7 61.5 all-gather.14
  287.3 61.5 all-gather.16
  588.8 57.8 reduce-scatter.7
  654.9 57.3 reduce-scatter.9
  714.6 60.2 reduce-scatter.11
  830.5 56.8 reduce-scatter.13
  916.7 74.9 reduce-scatter.5

commit v2 on v1

--- a/solution.py
+++ b/solution.py
@@ -15,6 +15,7 @@
 NEG = -1e30
 GROUP = 256
 FF_BLOCKS = 4
+FF_EARLY = 2
 F32 = jnp.float32
 BF16 = jnp.bfloat16
 VMEM_BYTES = 56 * 1024 * 1024
@@ -116,35 +117,13 @@
 
         @pl.loop(0, GROUP // 128)
         def _(pair, at=at, spots=spots):
-            lanes = pl.ds(pl.multiple_of(pair * 128, 128), 128)
-            query = q_ref[at, lanes]
-            outs, stats = [], []
-            for h in range(2):
-                mine = (head_lane < HEAD_DIM) if h == 0 else (head_lane >= HEAD_DIM)
-                qm = jnp.where(mine, query, 0) * jnp.asarray(HEAD_DIM**-0.5, BF16)
-                scores = [
-                    dot_nt(qm, k_ref[s, lanes]) + bias_ref[n] for n, s in enumerate(spots)
-                ]
-                top = functools.reduce(
-                    jnp.maximum, [jnp.max(s, axis=1, keepdims=True) for s in scores]
-                )
-                weights = [jnp.exp(s - top) for s in scores]
-                total = sum(jnp.sum(w, axis=1, keepdims=True) for w in weights)
-                out = sum(
-                    dot_nn(w.astype(BF16), v_ref[s, lanes]) for w, s in zip(weights, spots)
-                )
-                outs.append(out / total)
-                stats.append(top + jnp.log(total))
-            mixed_ref[at, lanes] = jnp.where(head_lane < HEAD_DIM, outs[0], outs[1]).astype(BF16)
-            kept = jnp.where(pair == 0, 0.0, lse_ref[at, :])
-            for h in range(2):
-                kept = jnp.where(head_lane == pair * 2 + h, stats[h], kept)
-            lse_ref[at, :] = kept
+            first = pl.program_id(0) * (GROUP // HEAD_DIM)
+            attend(pair, first, at, spots, head_lane, q_ref, k_ref, v_ref, mixed_ref, lse_ref, bias_ref)
 
 
 def attn_forward(blocks, key, x, own, sib, cosine, sine, segc, segr):
     d = x.shape[1]
-    cols = own.shape[1] // 4
+    cols = own.shape[1] // 3
     steps = cols // GROUP
     rows = LEN // blocks
 
@@ -163,8 +142,8 @@
         + [weight(p) for p in (0, 0, 1, 1, 2, 2)]
         + [whole((LEN, GROUP))] * 2
         + [whole((LEN, 128)), whole(segr.shape)],
-        out_specs=[col_block] * 4 + [pl.BlockSpec((LEN, 128), lambda i: (0, i))],
-        out_shape=[slab] * 4 + [jax.ShapeDtypeStruct((LEN, 128 * steps), F32)],
+        out_specs=[col_block] * 4 + [whole((LEN, 128))],
+        out_shape=[slab] * 4 + [jax.ShapeDtypeStruct((LEN, 128), F32)],
         scratch_shapes=[pltpu.VMEM((blocks, rows, rows), F32)],
         compiler_params=pltpu.CompilerParams(vmem_limit_bytes=VMEM_BYTES),
         name="attn_forward",
@@ -197,6 +176,7 @@
         @pl.loop(0, GROUP // 128)
         def _(pair, at=at, spots=spots):
             lanes = pl.ds(pl.multiple_of(pair * 128, 128), 128)
+            first = pl.program_id(0) * (GROUP // HEAD_DIM)
             query, grad = q_ref[at, lanes], dm_ref[at, lanes]
             logs = lse_ref[at, :]
             outs = []
@@ -205,7 +185,7 @@
                 qm = jnp.where(mine, query, 0) * jnp.asarray(scale, BF16)
                 gm = jnp.where(mine, grad, 0)
                 log = jnp.sum(
-                    jnp.where(head_lane == pair * 2 + h, logs, 0.0), axis=1, keepdims=True
+                    jnp.where(head_lane == first + pair * 2 + h, logs, 0.0), axis=1, keepdims=True
                 )
                 weights = [
                     jnp.exp(dot_nt(qm, k_ref[s, lanes]) + bias_ref[n] - log)
@@ -245,14 +225,14 @@
         return pl.BlockSpec(shape, lambda i: (0,) * len(shape))
 
     col_block = pl.BlockSpec((LEN, GROUP), lambda i: (0, i))
-    weight = pl.BlockSpec((d // 2, GROUP), lambda i: (0, 3 * steps + i))
+    weight = pl.BlockSpec((d // 2, GROUP), lambda i: (0, i))
     slab = jax.ShapeDtypeStruct((LEN, cols), BF16)
     return pl.pallas_call(
         functools.partial(attn_backward_kernel, blocks),
         grid=(steps,),
         in_specs=[pl.BlockSpec(memory_space=pltpu.SMEM), whole((LEN, d)), weight, weight]
         + [col_block] * 3
-        + [pl.BlockSpec((LEN, 128), lambda i: (0, i))]
+        + [whole((LEN, 128))]
         + [whole((LEN, GROUP))] * 2
         + [whole((LEN, 128)), whole(segr.shape)],
         out_specs=[col_block] * 3,
@@ -269,6 +249,430 @@
     )(key, g, own, sib, q, k, v, lse, cosine, sine, segc, segr)
 
 
+class LineGather:
+    def __init__(self, me, src, full, sems):
+        self.me, self.src, self.full, self.sems = me, src, full, sems
+        self.rows = src.shape[0]
+
+    def spot(self, side, s):
+        return self.full.at[side, pl.ds(pl.multiple_of(s * self.rows, self.rows), self.rows)]
+
+    def to_line(self, src, s, way):
+        device = self.me.up if way == 0 else self.me.down
+        return remote(src, self.spot(0, s), self.sems.at[way, s], self.sems.at[3, s], device)
+
+    def to_core(self, src, s):
+        return remote(src, self.spot(1, s), self.sems.at[2, s], self.sems.at[4, s], self.me.other)
+
+    def keep(self):
+        return pltpu.make_async_copy(self.src, self.spot(0, self.me.z), self.sems.at[5, 0])
+
+    def start(self):
+        z, line = self.me.z, self.me.line
+
+        @pl.when(z + 1 < line)
+        def _():
+            self.to_line(self.src, z, 0).start()
+
+        @pl.when(z >= 1)
+        def _():
+            self.to_line(self.src, z, 1).start()
+
+        self.to_core(self.src, z).start()
+        self.keep().start()
+
+    def hop(self, h):
+        z, line = self.me.z, self.me.line
+        for s, arrives, goes_on, way in (
+            (z - h, z >= h, z + 1 < line, 0),
+            (z + h, z + h < line, z >= 1, 1),
+        ):
+
+            @pl.when(arrives)
+            def _(s=s, goes_on=goes_on, way=way):
+                here = self.spot(0, s)
+                self.to_line(here, s, way).wait_recv()
+
+                @pl.when(goes_on)
+                def _():
+                    self.to_line(here, s, way).start()
+
+                self.to_core(here, s).start()
+
+    def arrived(self):
+        self.keep().wait()
+        for s in range(self.me.line):
+            self.to_core(self.spot(0, s), s).wait_recv()
+
+    def done(self):
+        z, line = self.me.z, self.me.line
+        for s in range(line):
+            here = self.spot(0, s)
+            self.to_core(here, s).wait_send()
+
+            @pl.when((s <= z) & (z + 1 < line))
+            def _(s=s, here=here):
+                self.to_line(here, s, 0).wait_send()
+
+            @pl.when((s >= z) & (z >= 1))
+            def _(s=s, here=here):
+                self.to_line(here, s, 1).wait_send()
+
+
+class SquareGather:
+    def __init__(self, me, full, sems):
+        self.me, self.full, self.sems = me, full, sems
+        self.half = full.shape[1] // 2
+
+    def copies(self):
+        me, full, sems, half = self.me, self.full, self.sems, self.half
+        top, bottom = pl.ds(0, half), pl.ds(half, half)
+        return (
+            remote(full.at[0], full.at[1], sems.at[0], sems.at[1], me.x),
+            remote(full.at[0], full.at[2], sems.at[2], sems.at[3], me.y),
+            remote(full.at[1, top], full.at[3, top], sems.at[4], sems.at[5], me.y),
+            remote(full.at[2, bottom], full.at[3, bottom], sems.at[6], sems.at[7], me.x),
+        )
+
+    def start(self):
+        x, y, _, _ = self.copies()
+        x.start()
+        y.start()
+
+    def forward(self):
+        x, y, top, bottom = self.copies()
+        x.wait_recv()
+        top.start()
+        y.wait_recv()
+        bottom.start()
+
+    def arrived(self):
+        _, _, top, bottom = self.copies()
+        top.wait_recv()
+        bottom.wait_recv()
+
+    def done(self):
+        for copy in self.copies():
+            copy.wait_send()
+
+
+class SquareScatter:
+    def __init__(self, me, stage, landed, sems):
+        self.me, self.stage, self.landed, self.sems = me, stage, landed, sems
+        self.half = stage.shape[1] // 2
+        self.top, self.bottom = pl.ds(0, self.half), pl.ds(self.half, self.half)
+
+    def copies(self):
+        me, stage, landed, sems = self.me, self.stage, self.landed, self.sems
+        top, bottom = self.top, self.bottom
+        return (
+            remote(stage.at[2, top], landed.at[2, top], sems.at[0], sems.at[1], me.y),
+            remote(stage.at[2, bottom], landed.at[2, bottom], sems.at[2], sems.at[3], me.x),
+            remote(stage.at[0, bottom], landed.at[0, bottom], sems.at[4], sems.at[5], me.x),
+            remote(stage.at[1, top], landed.at[1, top], sems.at[6], sems.at[7], me.y),
+            remote(stage.at[0, top], landed.at[0, top], sems.at[8], sems.at[9], me.x),
+            remote(stage.at[1, bottom], landed.at[1, bottom], sems.at[10], sems.at[11], me.y),
+        )
+
+    def diagonal_ready(self):
+        copies = self.copies()
+        copies[0].start()
+        copies[1].start()
+
+    def sides_ready(self):
+        copies = self.copies()
+        copies[2].start()
+        copies[3].start()
+
+    def combine(self):
+        copies = self.copies()
+        for n, slot, at in ((0, 0, self.top), (1, 1, self.bottom)):
+            copies[n].wait_recv()
+            add_rows(self.stage, slot, at, self.landed)
+            copies[4 + n].start()
+
+    def arrived(self):
+        for copy in self.copies()[2:]:
+            copy.wait_recv()
+
+    def done(self):
+        for copy in self.copies():
+            copy.wait_send()
+
+
+def add_rows(stage, slot, at, landed):
+    step = 32
+
+    @pl.loop(0, at.size // step)
+    def _(n):
+        here = pl.ds(pl.multiple_of(at.start + n * step, step), step)
+        total = stage[slot, here, :].astype(F32) + landed[2, here, :].astype(F32)
+        stage[slot, here, :] = total.astype(BF16)
+
+
+def remote(src, dst, send_sem, recv_sem, device):
+    return pltpu.make_async_remote_copy(
+        src_ref=src, dst_ref=dst, send_sem=send_sem, recv_sem=recv_sem, device_id=device,
+        device_id_type=pl.DeviceIdType.MESH,
+    )
+
+
+class Place:
+    def __init__(self, dp):
+        index = lax.axis_index("dp")
+        self.line = dp // 2
+        self.z, self.core = index // 2, index % 2
+        self.t = lax.axis_index("tensor")
+        tx, ty = self.t % 2, self.t // 2
+        self.other = {"dp": index + 1 - 2 * self.core}
+        self.up, self.down = {"dp": index + 2}, {"dp": index - 2}
+        self.x = {"tensor": self.t + 1 - 2 * tx}
+        self.y = {"tensor": self.t + 2 - 4 * ty}
+        self.spots = [
+            (tx if i % 2 == 0 else 1 - tx) + 2 * (ty if i // 2 == 0 else 1 - ty) for i in range(4)
+        ]
+
+    def greet(self):
+        barrier = pltpu.get_barrier_semaphore()
+
+        def signal(device):
+            pl.semaphore_signal(
+                barrier, inc=1, device_id=device, device_id_type=pl.DeviceIdType.MESH
+            )
+
+        for device in (self.other, self.x, self.y):
+            signal(device)
+        pl.when(self.z + 1 < self.line)(lambda: signal(self.up))
+        pl.when(self.z >= 1)(lambda: signal(self.down))
+        ends = (self.z == 0) | (self.z == self.line - 1)
+        pl.when(ends)(lambda: pl.semaphore_wait(barrier, 4))
+        pl.when(jnp.logical_not(ends))(lambda: pl.semaphore_wait(barrier, 5))
+
+
+def norm_rows(count, body, step=32):
+    @pl.loop(0, count // step)
+    def _(n):
+        body(pl.ds(pl.multiple_of(n * step, step), step))
+
+
+def forward_kernel(
+    dp, x_ref, wa_ref, wo_ref, wf_ref, g_ref, gain_ref, cos_ref, sin_ref, segc_ref, segr_ref,
+    normed_ref, gall_ref, normed_mlp_ref, q_ref, k_ref, v_ref, mixed_ref, lse_ref, middle_ref,
+    wa_full, wo_full, wf_full, gains_ref,
+    bias_ref, local_ref, stage_ref, landed_ref,
+    sem_gain, sem_a, sem_o, sem_f, sem_n, sem_g, sem_s, sem_m, sem_c,
+):
+    me = Place(dp)
+    me.greet()
+    nf = wf_ref.shape[0]
+    gain = LineGather(me, gain_ref, gains_ref, sem_gain)
+    wa = LineGather(me, wa_ref, wa_full, sem_a)
+    wo = LineGather(me, wo_ref, wo_full, sem_o)
+    wf = [LineGather(me, wf_ref.at[b], wf_full.at[b], sem_f.at[b]) for b in range(nf)]
+    normed = SquareGather(me, normed_ref, sem_n)
+    grads = SquareGather(me, gall_ref, sem_g)
+    normed_mlp = SquareGather(me, normed_mlp_ref, sem_m)
+    hops = range(1, me.line)
+
+    gain.start()
+    wa.start()
+    keep_g = pltpu.make_async_copy(g_ref, gall_ref.at[0], sem_c.at[0])
+    keep_g.start()
+    for h in hops:
+        gain.hop(h)
+    gain.arrived()
+
+    half = x_ref.shape[1] // 2
+    shard = gain_ref.shape[1]
+
+    def gain_row(which, width):
+        return jnp.concatenate(
+            [
+                gains_ref[side, pl.ds(s * 16 + which, 1), :].astype(F32)
+                for side in range(2)
+                for s in range(me.line)
+            ],
+            axis=1,
+        )
+
+    gain_one, gain_two = gain_row(0, shard), gain_row(1, shard)
+
+    def first_norm(at):
+        values = x_ref[at, :].astype(F32)
+        normed_ref[0, at, :] = (values * norm_factor(values) * gain_one).astype(BF16)
+
+    norm_rows(x_ref.shape[0], first_norm)
+    normed.start()
+    wa.hop(1)
+    normed.forward()
+    wa.hop(2)
+    grads_started = False
+    for h in range(3, me.line):
+        wa.hop(h)
+    wo.start()
+    keep_g.wait()
+    grads.start()
+    normed.arrived()
+    wa.arrived()
+    wf[0].start()
+
+    rows = LEN // 4
+    cols = q_ref.shape[1]
+    groups = cols // GROUP
+
+    @pl.loop(0, 4 * groups)
+    def _(n):
+        b, group = n // groups, n % groups
+        at = pl.ds(pl.multiple_of(b * rows, rows), rows)
+        lanes = pl.ds(pl.multiple_of(group * GROUP, GROUP), GROUP)
+        left, right = normed_ref[b, :, :half], normed_ref[b, :, half:]
+        cosine, sine = cos_ref[at, :], sin_ref[at, :]
+
+        def product(part):
+            here = pl.ds(pl.multiple_of(part * cols + group * GROUP, GROUP), GROUP)
+            return dot_nn(left, wa_full[0, :, here]) + dot_nn(right, wa_full[1, :, here])
+
+        query = product(0)
+        q_ref[at, lanes] = (query * cosine + swap_halves(query) * sine).astype(BF16)
+        keys = product(1)
+        k_ref[at, lanes] = (keys * cosine + swap_halves(keys) * sine).astype(BF16)
+        v_ref[at, lanes] = product(2).astype(BF16)
+
+    wo.hop(1)
+    head_lane = lax.broadcasted_iota(jnp.int32, (rows, 128), 1)
+    for i in range(4):
+        places = [(j, me.spots[j]) for j in key_blocks(i, rows)]
+        at = pl.ds(pl.multiple_of(me.spots[i] * rows, rows), rows)
+        fill_bias(bias_ref, segc_ref[at, 0:1], segr_ref, i, places)
+        spots = [pl.ds(pl.multiple_of(p * rows, rows), rows) for _, p in places]
+
+        @pl.loop(0, cols // 128)
+        def _(pair, at=at, spots=spots):
+            attend(pair, 0, at, spots, head_lane, q_ref, k_ref, v_ref, mixed_ref, lse_ref, bias_ref)
+
+        if i == 0:
+            wo.hop(2)
+        if i == 1:
+            for h in range(3, me.line):
+                wo.hop(h)
+            grads.forward()
+        if i == 2:
+            wf[0].hop(1)
+
+    wo.arrived()
+    scatter = SquareScatter(me, stage_ref, landed_ref, sem_s)
+
+    def out_rows(b, slot):
+        at = pl.ds(b * rows, rows)
+
+        @pl.loop(0, 2)
+        def _(side):
+            @pl.loop(0, half // GROUP)
+            def _(n):
+                here = pl.ds(pl.multiple_of(n * GROUP, GROUP), GROUP)
+                there = pl.ds(pl.multiple_of(side * half + n * GROUP, GROUP), GROUP)
+                total = dot_nt(mixed_ref[at, :], wo_full[side, here, :])
+                if slot is None:
+                    middle_ref[:, there] = total
+                else:
+                    stage_ref[slot, :, there] = total.astype(BF16)
+
+    out_rows(3, 2)
+    scatter.diagonal_ready()
+    out_rows(1, 0)
+    out_rows(2, 1)
+    scatter.sides_ready()
+    out_rows(0, None)
+    wf[0].hop(2)
+    scatter.combine()
+    for h in range(3, me.line):
+        wf[0].hop(h)
+    if nf > 1:
+        wf[1].start()
+    scatter.arrived()
+
+    def second_norm(at):
+        total = middle_ref[at, :] + landed_ref[0, at, :].astype(F32)
+        total = total + landed_ref[1, at, :].astype(F32)
+        middle = x_ref[at, :].astype(F32) + total
+        middle_ref[at, :] = middle
+        local_ref[at, :] = (middle * norm_factor(middle) * gain_two).astype(BF16)
+
+    norm_rows(x_ref.shape[0], second_norm)
+    keep_m = pltpu.make_async_copy(local_ref, normed_mlp_ref.at[0], sem_c.at[1])
+    keep_m.start()
+    keep_m.wait()
+    normed_mlp.start()
+    if nf > 1:
+        wf[1].hop(1)
+    normed_mlp.forward()
+    if nf > 1:
+        for h in range(2, me.line):
+            wf[1].hop(h)
+    normed_mlp.arrived()
+    grads.arrived()
+    for one in wf:
+        one.arrived()
+    for one in (gain, wa, wo, *wf, normed, grads, normed_mlp, scatter):
+        one.done()
+
+
+def attend(pair, first, at, spots, head_lane, q_ref, k_ref, v_ref, mixed_ref, lse_ref, bias_ref):
+    lanes = pl.ds(pl.multiple_of(pair * 128, 128), 128)
+    query = q_ref[at, lanes]
+    outs, stats = [], []
+    for h in range(2):
+        mine = (head_lane < HEAD_DIM) if h == 0 else (head_lane >= HEAD_DIM)
+        qm = jnp.where(mine, query, 0) * jnp.asarray(HEAD_DIM**-0.5, BF16)
+        scores = [dot_nt(qm, k_ref[s, lanes]) + bias_ref[n] for n, s in enumerate(spots)]
+        top = functools.reduce(jnp.maximum, [jnp.max(s, axis=1, keepdims=True) for s in scores])
+        weights = [jnp.exp(s - top) for s in scores]
+        total = sum(jnp.sum(w, axis=1, keepdims=True) for w in weights)
+        out = sum(dot_nn(w.astype(BF16), v_ref[s, lanes]) for w, s in zip(weights, spots))
+        outs.append(out / total)
+        stats.append(top + jnp.log(total))
+    mixed_ref[at, lanes] = jnp.where(head_lane < HEAD_DIM, outs[0], outs[1]).astype(BF16)
+    kept = jnp.where(pair + first == 0, 0.0, lse_ref[at, :])
+    for h in range(2):
+        kept = jnp.where(head_lane == first + pair * 2 + h, stats[h], kept)
+    lse_ref[at, :] = kept
+
+
+def forward(dp, x, wa, wo, wf, g, gains, cosine, sine, segc, segr):
+    line = dp // 2
+    local, d = x.shape
+    cols = wo.shape[1]
+    nf, _, fcols = wf.shape
+    vmem, hbm = pl.BlockSpec(memory_space=pltpu.VMEM), pl.BlockSpec(memory_space=pl.ANY)
+    S = jax.ShapeDtypeStruct
+    slab = S((LEN, cols), BF16)
+    rows = LEN // 4
+    dma = pltpu.SemaphoreType.DMA
+    return pl.pallas_call(
+        functools.partial(forward_kernel, dp),
+        in_specs=[vmem, vmem, vmem, hbm, hbm, vmem, vmem, vmem, vmem, vmem],
+        out_specs=[vmem, hbm, hbm, vmem, vmem, vmem, vmem, vmem, vmem, vmem, vmem, hbm, vmem],
+        out_shape=[
+            S((4, local, d), BF16), S((4, local, d), BF16), S((4, local, d), BF16),
+            slab, slab, slab, slab, S((LEN, 128), F32), S((local, d), F32),
+            S((2, d // 2, 3 * cols), BF16), S((2, d // 2, cols), BF16),
+            S((nf, 2, d // 2, fcols), BF16), S((2, line * 16, d // dp), BF16),
+        ],
+        scratch_shapes=[
+            pltpu.VMEM((3, rows, rows), F32),
+            pltpu.VMEM((local, d), BF16),
+            pltpu.VMEM((3, local, d), BF16),
+            pltpu.VMEM((3, local, d), BF16),
+            dma((6, line)), dma((6, line)), dma((6, line)), dma((nf, 6, line)),
+            dma((8,)), dma((8,)), dma((12,)), dma((8,)), dma((2,)),
+        ],
+        compiler_params=pltpu.CompilerParams(
+            vmem_limit_bytes=VMEM_BYTES, collective_id=0, has_side_effects=True
+        ),
+        name="forward",
+    )(x, wa, wo, wf, g, gains, cosine, sine, segc, segr)
+
+
 def on_device(
     dp, tensor, hidden_in, doc_lengths, gain_attn, w_query, w_key, w_value, w_out, gain_mlp,
     w_gate, w_up, w_down, cotangent,
@@ -343,41 +747,54 @@
     segr = jnp.broadcast_to(segment.reshape(blocks, 1, rows), (blocks, 8, rows))
     key = key.reshape(1)
 
-    gains = lax.all_gather(jnp.stack([gain_attn, gain_mlp]), "dp", axis=0)
-    gains = own_first(jnp.moveaxis(gains, 0, 1).reshape(2, d)).astype(F32)
-    gain_one, gain_two = gains[0], gains[1]
-
     ff = w_gate.shape[1]
     fb = ff // FF_BLOCKS
-    attn_own, attn_sib = line_gather(
-        jnp.concatenate([w_query, w_key, w_value, w_out.T], axis=1)
-    )
     down_t = w_down.T
-    ff_sets = []
-    for b in range(FF_BLOCKS):
-        cut = slice(b * fb, (b + 1) * fb)
-        own, sib = line_gather(
-            jnp.concatenate([w_gate[:, cut], w_up[:, cut], down_t[:, cut]], axis=1)
+    shards = [
+        jnp.concatenate([w[:, b * fb : (b + 1) * fb] for w in (w_gate, w_up, down_t)], axis=1)
+        for b in range(FF_BLOCKS)
+    ]
+    qkv_shard = jnp.concatenate([w_query, w_key, w_value], axis=1)
+    cols = w_query.shape[1]
+    hidden_mine = own_first(hidden_in)
+    g_local = own_first(cotangent)
+    inputs = hidden_mine.astype(F32)
+    factor_one = norm_factor(inputs)
+    early = FF_EARLY if square else 0
+    ff_sets = [jnp.concatenate(line_gather(shard), axis=0) for shard in shards[early:]]
+    if square:
+        gain_rows = jnp.pad(jnp.stack([gain_attn, gain_mlp]), ((0, 14), (0, 0)))
+        (
+            normed, g_all, normed_mlp, query, keys, values, mixed, lse, middle, qkv_full,
+            out_full, ff_full, gains,
+        ) = forward(
+            dp, hidden_mine, qkv_shard, w_out.T, jnp.stack(shards[:early]), g_local, gain_rows,
+            cosine, sine, segc, segr,
         )
-        ff_sets.append(jnp.concatenate([own, sib], axis=0))
-
-    inputs = own_first(hidden_in).astype(F32)
-    g_local = own_first(cotangent)
-    factor_one = norm_factor(inputs)
-    normed = gather_rows((inputs * factor_one * gain_one).astype(BF16))
-    g_all = gather_rows(g_local)
-
-    query, keys, values, mixed, lse = attn_forward(
-        blocks, key, normed, attn_own, attn_sib, cosine, sine, segc, segr
-    )
-    cols = query.shape[1]
-    out_own, out_sib = attn_own[:, 3 * cols :], attn_sib[:, 3 * cols :]
-    attended = jnp.concatenate(
-        [dot_nt(mixed, out_own).astype(BF16), dot_nt(mixed, out_sib).astype(BF16)], axis=1
-    )
-    middle = inputs + scatter_rows(attended)
-    factor_two = norm_factor(middle)
-    normed_mlp = gather_rows((middle * factor_two * gain_two).astype(BF16))
+        normed, g_all, normed_mlp = (a.reshape(LEN, d) for a in (normed, g_all, normed_mlp))
+        qkv_own, qkv_sib = qkv_full[0], qkv_full[1]
+        out_own, out_sib = out_full[0], out_full[1]
+        ff_sets = [ff_full[b].reshape(d, 3 * fb) for b in range(early)] + ff_sets
+        gains = gains.reshape(2 * line, 16, d // dp)[:, :2].astype(F32)
+        gain_one, gain_two = gains[:, 0].reshape(d), gains[:, 1].reshape(d)
+        factor_two = norm_factor(middle)
+    else:
+        gains = lax.all_gather(jnp.stack([gain_attn, gain_mlp]), "dp", axis=0)
+        gains = own_first(jnp.moveaxis(gains, 0, 1).reshape(2, d)).astype(F32)
+        gain_one, gain_two = gains[0], gains[1]
+        qkv_own, qkv_sib = line_gather(qkv_shard)
+        out_own, out_sib = line_gather(w_out.T)
+        normed = gather_rows((inputs * factor_one * gain_one).astype(BF16))
+        g_all = gather_rows(g_local)
+        query, keys, values, mixed, lse = attn_forward(
+            blocks, key, normed, qkv_own, qkv_sib, cosine, sine, segc, segr
+        )
+        attended = jnp.concatenate(
+            [dot_nt(mixed, out_own).astype(BF16), dot_nt(mixed, out_sib).astype(BF16)], axis=1
+        )
+        middle = inputs + scatter_rows(attended)
+        factor_two = norm_factor(middle)
+        normed_mlp = gather_rows((middle * factor_two * gain_two).astype(BF16))
 
     down_sum = jnp.zeros((LEN, d), F32)
     back_sum = jnp.zeros((LEN, d), F32)
@@ -410,7 +827,7 @@
     grad_mid_all = gather_rows(grad_middle.astype(BF16))
 
     dq, dk, dv = attn_backward(
-        blocks, key, grad_mid_all, attn_own, attn_sib, query, keys, values, lse, cosine, sine,
+        blocks, key, grad_mid_all, out_own, out_sib, query, keys, values, lse, cosine, sine,
         segc, segr,
     )
     grad = jnp.concatenate(
@@ -421,8 +838,8 @@
     rows_grad = jnp.concatenate([dq, dk, dv], axis=1)
     back = jnp.concatenate(
         [
-            dot_nt(rows_grad, attn_own[:, : 3 * cols]).astype(BF16),
-            dot_nt(rows_grad, attn_sib[:, : 3 * cols]).astype(BF16),
+            dot_nt(rows_grad, qkv_own).astype(BF16),
+            dot_nt(rows_grad, qkv_sib).astype(BF16),
         ],
         axis=1,
     )

time: 1100 us -> 934 us (0.85)
  Pallas kernels: 67.6 us -> 320 us
  waiting for transfers between devices: 384 us -> 133 us
  matrix products: 272 us -> 192 us
  local copies, waits for them, and re-layouts: 120 us -> 85 us
  blocking collectives: 88 us -> 69.5 us
  starting transfers between devices: 37.8 us -> 19.5 us
  other arithmetic: 105 us -> 92.3 us
    pallas_call x1, Pallas kernels: 30 us -> 282 us  [forward(): pl.pallas_call(functools.partial(forward_kernel, dp), in_specs=[vmem, vme...]
    all_gather x5 -> x2, waiting for transfers between devices: 168 us -> 0.01 us  [line_gather(): lax.all_gather(a, 'dp', axis=0, axis_index_groups=same_core, tiled=True)]
    ppermute x32 -> x16, waiting for transfers between devices: 215 us -> 133 us  [hop(): return lax.ppermute(a, 'tensor', [(i, i ^ step) for i in range(tensor)])]
    dot_general x12, matrix products: 73.9 us -> 35 us  [dot_nn(): return jnp.dot(a, b, preferred_element_type=F32)]
    dot_general x16, matrix products: 81.3 us -> 51.1 us  [dot_tn(): lax.dot_general(a, b, (((0,), (0,)), ((), ())), preferred_element_type=F32)]
    unnamed x224 -> x171, local copies, waits for them, and re-layouts: 55.2 us -> 26.8 us
    ppermute x32 -> x16, starting transfers between devices: 36.5 us -> 17 us  [hop(): return lax.ppermute(a, 'tensor', [(i, i ^ step) for i in range(tensor)])]
    all_gather x1 -> x0, blocking collectives: 13.9 us -> none  [on_device(): gains = lax.all_gather(jnp.stack([gain_attn, gain_mlp]), 'dp', axis=0)]
  transfers between devices with their start and end apart: 52 -> 30, of which waited for: 24 -> 10; matrix products, arithmetic and copies ran while one was open for 39% -> 37% of each run, Pallas kernels for 6% -> 34%
where the time goes in v2:
time: 934 us; the launch traced here: 927 us
  Pallas kernels  320 us (34%)
  matrix products  192 us (21%)
  waiting for transfers between devices  133 us (14%)
  other arithmetic  92.3 us (10%)
  local copies, waits for them, and re-layouts  85 us (9%)
  blocking collectives  69.5 us (7%)
  starting transfers between devices  19.5 us (2%)
  between operations  15.7 us (2%)
    pallas_call x1, Pallas kernels, forward(): pl.pallas_call(functools.partial(forward_kernel, dp), in_specs=[vmem, vme...  282 us
    ppermute x16, waiting for transfers between devices, hop(): return lax.ppermute(a, 'tensor', [(i, i ^ step) for i in range(tensor)])  133 us
    dot_general x14, matrix products, dot_nt(): lax.dot_general(a, b, (((1,), (1,)), ((), ())), preferred_element_type=F32)  106 us
    all_gather x1, blocking collectives, on_device(): shares = lax.all_gather(parts, ('dp', 'tensor'), axis=0)  69.5 us
    dot_general x16, matrix products, dot_tn(): lax.dot_general(a, b, (((0,), (0,)), ((), ())), preferred_element_type=F32)  51.1 us
    pallas_call x1, Pallas kernels, attn_backward(): pl.pallas_call(functools.partial(attn_backward_kernel, blocks), grid=(ste...  37.7 us
    dot_general x12, matrix products, dot_nn(): return jnp.dot(a, b, preferred_element_type=F32)  35 us
    concatenate x4, other arithmetic, on_device(): jnp.concatenate([dot_tn(normed_mlp, grad_gate_pre).astype(BF16), dot_tn(n...  32.8 us
  transfers between devices with their start and end apart: 30, of which 10 were waited for; matrix products, arithmetic and copies ran while one was open for 37% of the time, Pallas kernels for 34%

profile of v2, /device:TPU:0, one launch (start us, length us, event | category | flops | bytes accessed | tf_op | source)
XLA Modules:
  0.0 927.2 jit_solution(4977107409909429248)
XLA Ops:
  33.6 282.1 %forward.1 = (bf16[4,256,2048]{2,1,0:T(8,128)(2,1)}, bf16[4,256,2048]{2,1,0:T(8,128)(2,1)}, bf16[4,256,2048]{2,1,0:T(8,128)(2,1)}, bf16[1024,512]{1,0:T(8,128)(2...) custom-call(bf16[256,2048]{1,0:T(8,128)(2,1)} %bitcast.161, ...), custom_call_target="tpu_custom_call" | custom-call | tf_op jit(solution)/shard_map/forward/pallas_call | solution.py:651
  315.7 5.8 fusion.92
  338.8 9.7 %pad_maximum_fusion.1 = bf16[2048,1536]{0,1:T(8,128)(2,1)S(1)} fusion(bf16[2048,512]{0,1:T(8,128)(2,1)S(1)} %convolution_convert_fusion.9, bf16[2048,512]{0,1:T(8,128)(2,1)S(1)} %convolution_convert_fusion.10, bf16[2048,512]{0,1:T(8,128)(2,1)S(1)} %convolution_convert_fusion.11), kind=kLoop, calls=%fused_computation.15 | loop fusion | flops 18874368 | bytes 12582912 | tf_op jit(solution)/shard_map/concatenate | solution.py:814
  371.4 10.1 %pad_maximum_fusion.2 = bf16[2048,1536]{0,1:T(8,128)(2,1)S(1)} fusion(bf16[2048,512]{0,1:T(8,128)(2,1)S(1)} %convolution_convert_fusion.6, bf16[2048,512]{0,1:T(8,128)(2,1)S(1)} %convolution_convert_fusion.7, bf16[2048,512]{0,1:T(8,128)(2,1)S(1)} %convolution_convert_fusion.8), kind=kLoop, calls=%fused_computation.16 | loop fusion | flops 18874368 | bytes 12582912 | tf_op jit(solution)/shard_map/concatenate | solution.py:814
  386.3 7.5 fusion.52
  405.7 7.3 fusion.70
  413.0 7.3 fusion.58
  420.3 7.4 fusion.54
  457.3 5.9 fusion.40
  479.4 10.0 %pad_maximum_fusion.3 = bf16[2048,1536]{0,1:T(8,128)(2,1)S(1)} fusion(bf16[2048,512]{0,1:T(8,128)(2,1)S(1)} %convolution_convert_fusion.3, bf16[2048,512]{0,1:T(8,128)(2,1)S(1)} %convolution_convert_fusion.4, bf16[2048,512]{0,1:T(8,128)(2,1)S(1)} %convolution_convert_fusion.5), kind=kLoop, calls=%fused_computation.17 | loop fusion | flops 18874368 | bytes 12582912 | tf_op jit(solution)/shard_map/concatenate | solution.py:814
  498.4 10.0 %add_convert_fusion.1 = bf16[1024,2048]{1,0:T(8,128)(2,1)S(1)} fusion(f32[1024,2048]{1,0:T(8,128)} %fusion.40, f32[1024,2048]{1,0:T(8,128)} %fusion.64, f32[1024,2048]{1,0:T(8,128)} %fusion.52, bf16[1024,512]{1,0:T(8,128)(2,1)} %get-tuple-element.120, bf16[2048,1536]{1,0:T(8,128)(2,1)S(1)} %constant_dynamic-update-slice_fusion.2), kind=kOutput, calls=%fused_computation.2 | convolution fusion | flops 2155872256 | bytes 32505856 | tf_op jit(solution)/shard_map/dot_general | solution.py:33
  509.9 6.9 fusion.34
  516.9 20.5 %add_convert_fusion = bf16[1024,2048]{1,0:T(8,128)(2,1)S(1)} fusion(f32[1024,2048]{1,0:T(8,128)} %fusion.34, f32[1024,2048]{1,0:T(8,128)} %fusion.42, f32[1024,2048]{1,0:T(8,128)} %fusion.46, f32[1024,2048]{1,0:T(8,128)} %fusion.54, f32[1024,2048]{1,0:T(8,128)} %fusion.58, f32[1024,2048]{1,0:T(8,128)} %fusion.70, f32[1024,2048]{1,0:T(8,128)} %fusion.66, ...), kind=kOutput, calls=%fused_computation.1 | convolution fusion | flops 2164260864 | bytes 66060288 | tf_op jit(solution)/shard_map/dot_general | solution.py:33
  538.9 7.4 convolution_convert_fusion
  567.9 26.9 %collective-permute-done.4 = bf16[128,2048]{1,0:T(8,128)(2,1)} collective-permute-done((bf16[128,2048]{1,0:T(8,128)(2,1)}, bf16[128,2048]{1,0:T(8,128)(2,1)}, u32[]{:S(2)}, u32[]{:S(2)}) %collective-permute-start.4) | collective-permute-done | bytes 524320 | tf_op jit(solution)/shard_map/ppermute | solution.py:706
  597.4 29.8 %collective-permute-done.8 = bf16[128,2048]{1,0:T(8,128)(2,1)S(1)} collective-permute-done((bf16[128,2048]{1,0:T(8,128)(2,1)S(1)}, bf16[128,2048]{1,0:T(8,128)(2,1)S(1)}, u32[]{:S(2)}, u32[]{:S(2)}) %collective-permute-start.8) | collective-permute-done | bytes 524320 | tf_op jit(solution)/shard_map/ppermute | solution.py:706
  633.0 18.4 %collective-permute-done.9 = bf16[256,2048]{1,0:T(8,128)(2,1)S(1)} collective-permute-done((bf16[256,2048]{1,0:T(8,128)(2,1)S(1)}, bf16[256,2048]{1,0:T(8,128)(2,1)S(1)}, u32[]{:S(2)}, u32[]{:S(2)}) %collective-permute-start.9) | collective-permute-done | bytes 1048608 | tf_op jit(solution)/shard_map/ppermute | solution.py:706
  662.6 19.3 %collective-permute-done.10 = bf16[256,2048]{1,0:T(8,128)(2,1)S(1)} collective-permute-done((bf16[256,2048]{1,0:T(8,128)(2,1)S(1)}, bf16[256,2048]{1,0:T(8,128)(2,1)S(1)}, u32[]{:S(2)}, u32[]{:S(2)}) %collective-permute-start.10) | collective-permute-done | bytes 1048608 | tf_op jit(solution)/shard_map/ppermute | solution.py:706
  697.3 37.7 %attn_backward.1 = (bf16[1024,512]{1,0:T(8,128)(2,1)}, bf16[1024,512]{1,0:T(8,128)(2,1)}, bf16[1024,512]{1,0:T(8,128)(2,1)}) custom-call(s32[1]{0:T(128)} %bitcast.21.key_ref, bf16[1024,2048]{1,0:T(8,128)(2,1)} %constant_dynamic-update-slice_fusion.4.g_ref, bf16[1024,512]{1,0:T(8,128)(2,1)} %get-tuple-element.135.wo, ...), custom_call_target="tpu_custom_call" | custom-call | tf_op jit(solution)/shard_map/attn_backward/pallas_call | solution.py:230
  748.7 5.8 fusion.21
  764.1 12.8 %collective-permute-done.14 = bf16[128,2048]{1,0:T(8,128)(2,1)S(1)} collective-permute-done((bf16[128,2048]{1,0:T(8,128)(2,1)S(1)}, bf16[128,2048]{1,0:T(8,128)(2,1)S(1)}, u32[]{:S(2)}, u32[]{:S(2)}) %collective-permute-start.14) | collective-permute-done | bytes 524320 | tf_op jit(solution)/shard_map/ppermute | solution.py:706
  781.5 10.6 %collective-permute-done.16 = bf16[128,2048]{1,0:T(8,128)(2,1)S(1)} collective-permute-done((bf16[128,2048]{1,0:T(8,128)(2,1)S(1)}, bf16[128,2048]{1,0:T(8,128)(2,1)S(1)}, u32[]{:S(2)}, u32[]{:S(2)}) %collective-permute-start.16) | collective-permute-done | bytes 524320 | tf_op jit(solution)/shard_map/ppermute | solution.py:706
  807.2 5.7 collective-permute-done.15
  819.4 69.5 %all-gather = f32[32,1,4096]{2,1,0:T(1,128)S(1)} all-gather(f32[1,1,4096]{2,1,0:T(1,128)S(1)} %reshape.301), channel_id=1, replica_groups=mesh['dp'=8,'tensor'=4] {'dp','tensor'}, dimensions={0}, use_global_device_ids=true | all-gather | bytes 540672 | tf_op jit(solution)/shard_map/all_gather | solution.py:850
  (377 shorter events, 276.9 us)
Async XLA Ops:
  7.2 398.0 %all-gather.4.cloned.1.call-start = ((), (), s32[]{:S(2)}) async-start(), calls=%async_computation.5 | async-start | bytes 3932160 | tf_op jit(solution)/shard_map/all_gather | solution.py:728
  12.5 415.3 %all-gather.6.cloned.1.call-start = ((), (), s32[]{:S(2)}) async-start(), calls=%async_computation.6 | async-start | bytes 3932160 | tf_op jit(solution)/shard_map/all_gather | solution.py:728
  13.5 780.9 %reduce-scatter.8.cloned.1.call-start = ((), (), s32[]{:S(2)}) async-start(), calls=%async_computation.8 | async-start | bytes 3932160 | tf_op jit(solution)/shard_map/reduce_scatter | solution.py:733
  361.0 435.6 %reduce-scatter.10.cloned.1.call-start = ((), (), s32[]{:S(2)}) async-start(), calls=%async_computation.9 | async-start | bytes 3932160 | tf_op jit(solution)/shard_map/reduce_scatter | solution.py:733
  386.2 41.9 %collective-permute-start.20 = (bf16[1024,1536]{0,1:T(8,128)(2,1)}, bf16[1024,1536]{0,1:T(8,128)(2,1)}, u32[]{:S(2)}, u32[]{:S(2)}) collective-permute-start(bf16[1024,1536]{0,1:T(8,128)(2,1)} %slice.383), channel_id=1, source_target_pairs={{0,4},{4,0},{8,12},{12,8},{16,20},{20,16},{24,28},{28,24},{1,5},{5... | collective-permute-start | bytes 9437192 | tf_op jit(solution)/shard_map/ppermute | solution.py:732
  405.2 31.8 %collective-permute-start = (bf16[1024,1536]{1,0:T(8,128)(2,1)}, bf16[1024,1536]{1,0:T(8,128)(2,1)}, u32[]{:S(2)}, u32[]{:S(2)}) collective-permute-start(bf16[1024,1536]{1,0:T(8,128)(2,1)} %all-gather.4.cloned.1.call-done), channel_id=1, source_target_pairs={{0,4},{4,0},{8,12},{12,8},{16,20},{20,16},{24,28},{28,24},{1,5},{5... | collective-permute-start | bytes 9437192 | tf_op jit(solution)/shard_map/ppermute | solution.py:729
  427.8 17.0 %collective-permute-start.1 = (bf16[1024,1536]{1,0:T(8,128)(2,1)}, bf16[1024,1536]{1,0:T(8,128)(2,1)}, u32[]{:S(2)}, u32[]{:S(2)}) collective-permute-start(bf16[1024,1536]{1,0:T(8,128)(2,1)} %all-gather.6.cloned.1.call-done), channel_id=1, source_target_pairs={{0,4},{4,0},{8,12},{12,8},{16,20},{20,16},{24,28},{28,24},{1,5},{5... | collective-permute-start | bytes 9437192 | tf_op jit(solution)/shard_map/ppermute | solution.py:729
  433.0 469.3 %reduce-scatter.12.cloned.1.call-start = ((), (), s32[]{:S(2)}) async-start(), calls=%async_computation.10 | async-start | bytes 3932160 | tf_op jit(solution)/shard_map/reduce_scatter | solution.py:733
  493.0 67.5 %collective-permute-start.21 = (bf16[1024,1536]{0,1:T(8,128)(2,1)}, bf16[1024,1536]{0,1:T(8,128)(2,1)}, u32[]{:S(2)}, u32[]{:S(2)}) collective-permute-start(bf16[1024,1536]{0,1:T(8,128)(2,1)} %slice.386), channel_id=1, source_target_pairs={{0,4},{4,0},{8,12},{12,8},{16,20},{20,16},{24,28},{28,24},{1,5},{5... | collective-permute-start | bytes 9437192 | tf_op jit(solution)/shard_map/ppermute | solution.py:732
  508.5 45.5 %collective-permute-start.2 = (bf16[128,2048]{1,0:T(8,128)(2,1)S(1)}, bf16[128,2048]{1,0:T(8,128)(2,1)}, u32[]{:S(2)}, u32[]{:S(2)}) collective-permute-start(bf16[128,2048]{1,0:T(8,128)(2,1)S(1)} %slice.338), channel_id=1, source_target_pairs={{0,2},{1,3},{2,0},{3,1},{4,6},{5,7},{6,4},{7,5},{8,10},{9,11},{10,... | collective-permute-start | bytes 1572872 | tf_op jit(solution)/shard_map/ppermute | solution.py:706
  537.5 21.7 %collective-permute-start.6 = (bf16[128,2048]{1,0:T(8,128)(2,1)S(1)}, bf16[128,2048]{1,0:T(8,128)(2,1)S(1)}, u32[]{:S(2)}, u32[]{:S(2)}) collective-permute-start(bf16[128,2048]{1,0:T(8,128)(2,1)S(1)} %slice.347), channel_id=1, source_target_pairs={{0,2},{1,3},{2,0},{3,1},{4,6},{5,7},{6,4},{7,5},{8,10},{9,11},{10,... | collective-permute-start | bytes 1572872 | tf_op jit(solution)/shard_map/ppermute | solution.py:706
  557.2 75.8 %collective-permute-start.3 = (bf16[256,2048]{1,0:T(8,128)(2,1)}, bf16[256,2048]{1,0:T(8,128)(2,1)}, u32[]{:S(2)}, u32[]{:S(2)}) collective-permute-start(bf16[256,2048]{1,0:T(8,128)(2,1)} %pad_maximum_fusion.11), channel_id=1, source_target_pairs={{0,1},{1,0},{2,3},{3,2},{4,5},{5,4},{6,7},{7,6},{8,9},{9,8},{10,11... | collective-permute-start | bytes 3145736 | tf_op jit(solution)/shard_map/ppermute | solution.py:706
  558.5 36.3 %collective-permute-start.4 = (bf16[128,2048]{1,0:T(8,128)(2,1)}, bf16[128,2048]{1,0:T(8,128)(2,1)}, u32[]{:S(2)}, u32[]{:S(2)}) collective-permute-start(bf16[128,2048]{1,0:T(8,128)(2,1)} %get-tuple-element.131), channel_id=1, source_target_pairs={{0,1},{1,0},{2,3},{3,2},{4,5},{5,4},{6,7},{7,6},{8,9},{9,8},{10,11... | collective-permute-start | bytes 1572872 | tf_op jit(solution)/shard_map/ppermute | solution.py:706
  564.5 340.1 %reduce-scatter.14.cloned.1.call-start = ((), (), s32[]{:S(2)}) async-start(), calls=%async_computation.11 | async-start | bytes 3932160 | tf_op jit(solution)/shard_map/reduce_scatter | solution.py:733
  565.8 67.1 %collective-permute-start.7 = (bf16[256,2048]{1,0:T(8,128)(2,1)S(1)}, bf16[256,2048]{1,0:T(8,128)(2,1)S(1)}, u32[]{:S(2)}, u32[]{:S(2)}) collective-permute-start(bf16[256,2048]{1,0:T(8,128)(2,1)S(1)} %pad_maximum_fusion.14), channel_id=1, source_target_pairs={{0,1},{1,0},{2,3},{3,2},{4,5},{5,4},{6,7},{7,6},{8,9},{9,8},{10,11... | collective-permute-start | bytes 3145736 | tf_op jit(solution)/shard_map/ppermute | solution.py:706
  567.2 60.0 %collective-permute-start.8 = (bf16[128,2048]{1,0:T(8,128)(2,1)S(1)}, bf16[128,2048]{1,0:T(8,128)(2,1)S(1)}, u32[]{:S(2)}, u32[]{:S(2)}) collective-permute-start(bf16[128,2048]{1,0:T(8,128)(2,1)S(1)} %copy-done.48), channel_id=1, source_target_pairs={{0,1},{1,0},{2,3},{3,2},{4,5},{5,4},{6,7},{7,6},{8,9},{9,8},{10,11... | collective-permute-start | bytes 1572872 | tf_op jit(solution)/shard_map/ppermute | solution.py:706
  596.1 36.8 %collective-permute-start.5 = (bf16[256,2048]{1,0:T(8,128)(2,1)S(1)}, bf16[256,2048]{1,0:T(8,128)(2,1)S(1)}, u32[]{:S(2)}, u32[]{:S(2)}) collective-permute-start(bf16[256,2048]{1,0:T(8,128)(2,1)S(1)} %pad_maximum_fusion.12), channel_id=1, source_target_pairs={{0,2},{1,3},{2,0},{3,1},{4,6},{5,7},{6,4},{7,5},{8,10},{9,11},{10,... | collective-permute-start | bytes 3145736 | tf_op jit(solution)/shard_map/ppermute | solution.py:706
  627.4 24.0 %collective-permute-start.9 = (bf16[256,2048]{1,0:T(8,128)(2,1)S(1)}, bf16[256,2048]{1,0:T(8,128)(2,1)S(1)}, u32[]{:S(2)}, u32[]{:S(2)}) collective-permute-start(bf16[256,2048]{1,0:T(8,128)(2,1)S(1)} %pad_maximum_fusion.15), channel_id=1, source_target_pairs={{0,2},{1,3},{2,0},{3,1},{4,6},{5,7},{6,4},{7,5},{8,10},{9,11},{10,... | collective-permute-start | bytes 3145736 | tf_op jit(solution)/shard_map/ppermute | solution.py:706
  632.0 53.4 %collective-permute-start.22 = (bf16[1024,1536]{0,1:T(8,128)(2,1)S(1)}, bf16[1024,1536]{0,1:T(8,128)(2,1)S(1)}, u32[]{:S(2)}, u32[]{:S(2)}) collective-permute-start(bf16[1024,1536]{0,1:T(8,128)(2,1)S(1)} %slice.389), channel_id=1, source_target_pairs={{0,4},{4,0},{8,12},{12,8},{16,20},{20,16},{24,28},{28,24},{1,5},{5... | collective-permute-start | bytes 9437192 | tf_op jit(solution)/shard_map/ppermute | solution.py:732
  658.4 23.5 %collective-permute-start.10 = (bf16[256,2048]{1,0:T(8,128)(2,1)S(1)}, bf16[256,2048]{1,0:T(8,128)(2,1)S(1)}, u32[]{:S(2)}, u32[]{:S(2)}) collective-permute-start(bf16[256,2048]{1,0:T(8,128)(2,1)S(1)} %get-tuple-element.106), channel_id=1, source_target_pairs={{0,1},{1,0},{2,3},{3,2},{4,5},{5,4},{6,7},{7,6},{8,9},{9,8},{10,11... | collective-permute-start | bytes 3145736 | tf_op jit(solution)/shard_map/ppermute | solution.py:706
  660.3 24.2 %collective-permute-start.11 = (bf16[256,2048]{1,0:T(8,128)(2,1)S(1)}, bf16[256,2048]{1,0:T(8,128)(2,1)S(1)}, u32[]{:S(2)}, u32[]{:S(2)}) collective-permute-start(bf16[256,2048]{1,0:T(8,128)(2,1)S(1)} %get-tuple-element.106), channel_id=1, source_target_pairs={{0,2},{1,3},{2,0},{3,1},{4,6},{5,7},{6,4},{7,5},{8,10},{9,11},{10,... | collective-permute-start | bytes 3145736 | tf_op jit(solution)/shard_map/ppermute | solution.py:706
  687.3 227.4 %reduce-scatter.6.cloned.1.call-start = ((), (), s32[]{:S(2)}) async-start(), calls=%async_computation.7 | async-start | bytes 5242880 | tf_op jit(solution)/shard_map/reduce_scatter | solution.py:733
  780.5 32.4 %collective-permute-start.15 = (bf16[256,2048]{1,0:T(8,128)(2,1)}, bf16[256,2048]{1,0:T(8,128)(2,1)}, u32[]{:S(2)}, u32[]{:S(2)}) collective-permute-start(bf16[256,2048]{1,0:T(8,128)(2,1)} %pad_maximum_fusion.16), channel_id=1, source_target_pairs={{0,1},{1,0},{2,3},{3,2},{4,5},{5,4},{6,7},{7,6},{8,9},{9,8},{10,11... | collective-permute-start | bytes 3145736 | tf_op jit(solution)/shard_map/ppermute | solution.py:706
  793.4 22.1 %collective-permute-start.17 = (bf16[256,2048]{1,0:T(8,128)(2,1)}, bf16[256,2048]{1,0:T(8,128)(2,1)}, u32[]{:S(2)}, u32[]{:S(2)}) collective-permute-start(bf16[256,2048]{1,0:T(8,128)(2,1)} %pad_maximum_fusion.17), channel_id=1, source_target_pairs={{0,2},{1,3},{2,0},{3,1},{4,6},{5,7},{6,4},{7,5},{8,10},{9,11},{10,... | collective-permute-start | bytes 3145736 | tf_op jit(solution)/shard_map/ppermute | solution.py:706
  (82 other events, 762.6 us)
Sparse Core Ops, SparseCore 0:
  12.6 83.0 all-gather.3
  97.2 83.2 all-gather.5
  361.1 61.1 reduce-scatter.7
  433.1 61.2 reduce-scatter.9
  564.7 60.9 reduce-scatter.11
  687.5 61.5 reduce-scatter.13
  761.9 78.2 reduce-scatter.5

commit v3 on v2

--- a/solution.py
+++ b/solution.py
@@ -14,11 +14,12 @@
 ROPE_BASE = 130000.0
 NEG = -1e30
 GROUP = 256
-FF_BLOCKS = 4
-FF_EARLY = 2
+FF_BLOCKS = 8
+FF_EARLY = 4
+TICK_AFTER = (3, 5, 6)
 F32 = jnp.float32
 BF16 = jnp.bfloat16
-VMEM_BYTES = 56 * 1024 * 1024
+VMEM_BYTES = 60 * 1024 * 1024
 
 
 def dot_nn(a, b):
@@ -426,13 +427,14 @@
         tx, ty = self.t % 2, self.t // 2
         self.other = {"dp": index + 1 - 2 * self.core}
         self.up, self.down = {"dp": index + 2}, {"dp": index - 2}
+        self.next, self.far = {"dp": index + 2 - 4 * (self.z % 2)}, {"dp": index + 4 - 8 * (self.z // 2)}
         self.x = {"tensor": self.t + 1 - 2 * tx}
         self.y = {"tensor": self.t + 2 - 4 * ty}
         self.spots = [
             (tx if i % 2 == 0 else 1 - tx) + 2 * (ty if i // 2 == 0 else 1 - ty) for i in range(4)
         ]
 
-    def greet(self):
+    def greet(self, far=False):
         barrier = pltpu.get_barrier_semaphore()
 
         def signal(device):
@@ -440,13 +442,13 @@
                 barrier, inc=1, device_id=device, device_id_type=pl.DeviceIdType.MESH
             )
 
-        for device in (self.other, self.x, self.y):
+        for device in (self.other, self.x, self.y) + ((self.far,) if far else ()):
             signal(device)
         pl.when(self.z + 1 < self.line)(lambda: signal(self.up))
         pl.when(self.z >= 1)(lambda: signal(self.down))
         ends = (self.z == 0) | (self.z == self.line - 1)
-        pl.when(ends)(lambda: pl.semaphore_wait(barrier, 4))
-        pl.when(jnp.logical_not(ends))(lambda: pl.semaphore_wait(barrier, 5))
+        pl.when(ends)(lambda: pl.semaphore_wait(barrier, 4 + far))
+        pl.when(jnp.logical_not(ends))(lambda: pl.semaphore_wait(barrier, 5 + far))
 
 
 def norm_rows(count, body, step=32):
@@ -473,6 +475,20 @@
     grads = SquareGather(me, gall_ref, sem_g)
     normed_mlp = SquareGather(me, normed_mlp_ref, sem_m)
     hops = range(1, me.line)
+    acts = []
+    for n, one in enumerate([wo] + wf):
+        for h in hops:
+
+            def act(n=n, one=one, h=h):
+                one.hop(h)
+                if h == 1 and n < nf:
+                    wf[n].start()
+
+            acts.append(act)
+
+    def poll(count=1):
+        for _ in range(min(count, len(acts))):
+            acts.pop(0)()
 
     gain.start()
     wa.start()
@@ -506,7 +522,6 @@
     wa.hop(1)
     normed.forward()
     wa.hop(2)
-    grads_started = False
     for h in range(3, me.line):
         wa.hop(h)
     wo.start()
@@ -514,7 +529,6 @@
     grads.start()
     normed.arrived()
     wa.arrived()
-    wf[0].start()
 
     rows = LEN // 4
     cols = q_ref.shape[1]
@@ -538,7 +552,7 @@
         k_ref[at, lanes] = (keys * cosine + swap_halves(keys) * sine).astype(BF16)
         v_ref[at, lanes] = product(2).astype(BF16)
 
-    wo.hop(1)
+    poll()
     head_lane = lax.broadcasted_iota(jnp.int32, (rows, 128), 1)
     for i in range(4):
         places = [(j, me.spots[j]) for j in key_blocks(i, rows)]
@@ -550,14 +564,9 @@
         def _(pair, at=at, spots=spots):
             attend(pair, 0, at, spots, head_lane, q_ref, k_ref, v_ref, mixed_ref, lse_ref, bias_ref)
 
-        if i == 0:
-            wo.hop(2)
+        poll()
         if i == 1:
-            for h in range(3, me.line):
-                wo.hop(h)
             grads.forward()
-        if i == 2:
-            wf[0].hop(1)
 
     wo.arrived()
     scatter = SquareScatter(me, stage_ref, landed_ref, sem_s)
@@ -583,12 +592,9 @@
     out_rows(2, 1)
     scatter.sides_ready()
     out_rows(0, None)
-    wf[0].hop(2)
+    poll()
     scatter.combine()
-    for h in range(3, me.line):
-        wf[0].hop(h)
-    if nf > 1:
-        wf[1].start()
+    poll(2)
     scatter.arrived()
 
     def second_norm(at):
@@ -603,13 +609,11 @@
     keep_m.start()
     keep_m.wait()
     normed_mlp.start()
-    if nf > 1:
-        wf[1].hop(1)
+    poll(3)
     normed_mlp.forward()
-    if nf > 1:
-        for h in range(2, me.line):
-            wf[1].hop(h)
+    poll(2)
     normed_mlp.arrived()
+    poll(len(acts))
     grads.arrived()
     for one in wf:
         one.arrived()
@@ -673,6 +677,744 @@
     )(x, wa, wo, wf, g, gains, cosine, sine, segc, segr)
 
 
+def add_into(total, other, rows, step=64):
+    @pl.loop(0, rows // step)
+    def _(n):
+        at = pl.ds(pl.multiple_of(n * step, step), step)
+        total[at, :] = (total[at, :].astype(F32) + other[at, :].astype(F32)).astype(total.dtype)
+
+
+class LineScatter:
+    def __init__(self, me, rows, mine, theirs, swapped, kept, landed, work, sems):
+        cut = lambda ref: ref.at[:, pl.ds(0, rows)]
+        self.me, self.rows = me, rows
+        self.mine, self.theirs, self.swapped = cut(mine), cut(theirs), cut(swapped)
+        self.kept, self.landed, self.work = cut(kept), cut(landed), cut(work)
+        self.sems = sems
+
+    def swap(self):
+        return remote(
+            self.theirs, self.swapped, self.sems.at[0], self.sems.at[1], self.me.other
+        )
+
+    def keep(self):
+        return pltpu.make_async_copy(self.mine, self.kept, self.sems.at[2])
+
+    def send(self, src, s, upward, z):
+        line = self.me.line
+        if upward:
+            slot, device = s, self.me.up
+        else:
+            slot, device = (s if s < z - 1 else line), self.me.down
+        return remote(
+            src, self.landed.at[slot], self.sems.at[3 + s], self.sems.at[3 + line + slot], device
+        )
+
+    def landing(self, slot):
+        line = self.me.line
+        return remote(
+            self.landed.at[slot], self.landed.at[slot], self.sems.at[3],
+            self.sems.at[3 + line + slot], self.me.other,
+        )
+
+    def load(self, src, n):
+        return pltpu.make_async_copy(src, self.work.at[n], self.sems.at[4 + 2 * self.me.line + n])
+
+    def reduce(self, free_sem):
+        line = self.me.line
+        self.swap().wait_recv()
+        for s in range(line):
+            add_into(self.mine.at[s], self.swapped.at[s], self.rows)
+        pl.semaphore_signal(
+            free_sem, inc=1, device_id=self.me.other, device_id_type=pl.DeviceIdType.MESH
+        )
+        self.keep().start()
+        self.swap().wait_send()
+        self.keep().wait()
+        for end, upward in ((0, True), (line - 1, False)):
+
+            @pl.when(self.me.z == end)
+            def _(end=end, upward=upward):
+                order = range(line - 1, end, -1) if upward else range(end)
+                for s in order:
+                    self.send(self.kept.at[s], s, upward, end).start()
+
+    def going(self, p):
+        line = self.me.line
+        for z, upward in ((p, True), (line - 1 - p, False)):
+            targets = list(range(line - 1, z, -1)) if upward else list(range(z))
+            yield z, upward, targets
+
+    def load_phase(self, p, first):
+        for z, upward, targets in self.going(p):
+
+            @pl.when(self.me.z == z)
+            def _(targets=targets):
+                for n, s in enumerate(targets):
+                    self.landing(s).wait_recv()
+                    self.load(self.landed.at[s], first + 2 * n).start()
+                    self.load(self.kept.at[s], first + 2 * n + 1).start()
+
+    def run_phase(self, p, first):
+        for z, upward, targets in self.going(p):
+
+            @pl.when(self.me.z == z)
+            def _(z=z, upward=upward, targets=targets):
+                for n, s in enumerate(targets):
+                    a, b = first + 2 * n, first + 2 * n + 1
+                    self.load(self.landed.at[s], a).wait()
+                    self.load(self.kept.at[s], b).wait()
+                    add_into(self.work.at[a], self.work.at[b], self.rows)
+                    self.send(self.work.at[a], s, upward, z).start()
+
+    def sent_phase(self, p, first):
+        for z, upward, targets in self.going(p):
+
+            @pl.when(self.me.z == z)
+            def _(z=z, upward=upward, targets=targets):
+                for n, s in enumerate(targets):
+                    self.send(self.work.at[first + 2 * n], s, upward, z).wait_send()
+
+    def load_last(self, first):
+        me = self.me
+        self.load(self.kept.at[me.z], first).start()
+
+        @pl.when(me.z >= 1)
+        def _():
+            self.landing(me.z).wait_recv()
+            self.load(self.landed.at[me.z], first + 1).start()
+
+        @pl.when(me.z < me.line - 1)
+        def _():
+            self.landing(me.line).wait_recv()
+            self.load(self.landed.at[me.line], first + 2).start()
+
+    def run_last(self, first, total):
+        me = self.me
+        here = total.at[pl.ds(0, self.rows)]
+        self.load(self.kept.at[me.z], first).wait()
+
+        def put(n, step=64):
+            @pl.loop(0, self.rows // step)
+            def _(i):
+                at = pl.ds(pl.multiple_of(i * step, step), step)
+                if n == first:
+                    here[at, :] = self.work[n, at, :].astype(F32)
+                else:
+                    here[at, :] += self.work[n, at, :].astype(F32)
+
+        put(first)
+
+        @pl.when(me.z >= 1)
+        def _():
+            self.load(self.landed.at[me.z], first + 1).wait()
+            put(first + 1)
+
+        @pl.when(me.z < me.line - 1)
+        def _():
+            self.load(self.landed.at[me.line], first + 2).wait()
+            put(first + 2)
+
+    def done(self):
+        line = self.me.line
+        for end, upward in ((0, True), (line - 1, False)):
+
+            @pl.when(self.me.z == end)
+            def _(end=end, upward=upward):
+                for s in range(line - 1, end, -1) if upward else range(end):
+                    self.send(self.kept.at[s], s, upward, end).wait_send()
+
+
+class Ticks:
+    def __init__(self, chunks, total, writers):
+        self.chunks, self.total, self.writers = chunks, total, writers
+        self.k = 0
+
+    def jobs(self, k):
+        count = len(self.chunks)
+        out = []
+        if 0 <= k < count:
+            out.append((self.chunks[k], 1, 0))
+        if 0 <= k - 1 < count:
+            out.append((self.chunks[k - 1], 2, 4))
+        return out
+
+    def tick(self):
+        k = self.k
+        for chunk, p, first in self.jobs(k - 1):
+            chunk.sent_phase(p, first)
+        last = self.chunks[k - 2] if 0 <= k - 2 < len(self.chunks) else None
+        for chunk, p, first in self.jobs(k):
+            chunk.load_phase(p, first)
+        if last is not None:
+            last.load_last(6)
+        for chunk, p, first in self.jobs(k):
+            chunk.run_phase(p, first)
+        if last is not None:
+            if k - 2 > 0:
+                self.writers[k - 3].wait()
+            last.run_last(6, self.total)
+            self.writers[k - 2].start()
+        self.k += 1
+
+    def rest(self):
+        while self.k < len(self.chunks) + 2:
+            self.tick()
+        self.writers[-1].wait()
+        for chunk in self.chunks:
+            chunk.done()
+
+
+class Writer:
+    def __init__(self, total, turned, parts, sem):
+        self.total, self.turned, self.parts, self.sem = total, turned, parts, sem
+
+    def copies(self):
+        for n, (dst, flip) in enumerate(self.parts):
+            rows = dst.shape[0] if not flip else dst.shape[1]
+            src = self.turned.at[n] if flip else self.total.at[pl.ds(n * 256, rows)]
+            yield pltpu.make_async_copy(src, dst, self.sem.at[n])
+
+    def start(self):
+        for n, (_, flip) in enumerate(self.parts):
+            if flip:
+                self.turned[n] = self.total[pl.ds(n * 256, 256), :].T
+        for copy in self.copies():
+            copy.start()
+
+    def wait(self):
+        for copy in self.copies():
+            copy.wait()
+
+
+def norm_back_rows(count, gain, values_of, grads_of, gain_ref, row, put, step=32):
+    @pl.loop(0, count // step)
+    def _(n):
+        at = pl.ds(pl.multiple_of(n * step, step), step)
+        values, grads = values_of(at), grads_of(at)
+        factor = norm_factor(values)
+        scaled = grads * gain
+        back = factor * scaled - values * factor * factor * factor * jnp.mean(
+            scaled * values, axis=-1, keepdims=True
+        )
+        gain_ref[row : row + 1, :] += jnp.sum(grads * values * factor, axis=0, keepdims=True)
+        put(at, back)
+
+
+def backward_kernel(
+    dp, x_ref, g_all, normed_all, mlp_all, middle_ref, gains_ref, wf_early, wf_late, qkv_full, out_full,
+    q_all, k_all, v_all, mixed_all, lse_all, cos_all, sin_all, segc_all, segr_all,
+    output_ref, input_grad_ref, gain_out_ref, gate_out, up_out, down_out, q_out, k_out, v_out, o_out,
+    late_full, hidden_all, kept_all, landed_all, y_all,
+    theirs, swapped, mine, work, total, turned, stage, landed, g2, own, gm, gp, gp_landed,
+    sem_late, sem_line, sem_write, sem_s, sem_g2, sem_gain, sem_c, sem_w, free_core, free_x, free_y,
+):
+    me = Place(dp)
+    me.greet(far=True)
+    early, late = wf_early.shape[0], wf_late.shape[0]
+    blocks = early + late
+    line, half = me.line, mlp_all.shape[2] // 2
+    local = x_ref.shape[0]
+    shard = half // line
+    rows = LEN // 4
+    fw = wf_late.shape[2] // 3
+    cols = q_all.shape[1]
+    groups = cols // GROUP
+    gathers = [LineGather(me, wf_late.at[b], late_full.at[b], sem_late.at[b]) for b in range(late)]
+    acts = []
+    for b in range(late):
+        def first(b=b):
+            gathers[b].hop(1)
+            if b + 1 < late:
+                gathers[b + 1].start()
+        acts.append(first)
+        for h in range(2, line):
+            acts.append(functools.partial(gathers[b].hop, h))
+    gathers[0].start()
+
+    def poll(count=1):
+        for _ in range(count):
+            if acts:
+                acts.pop(0)()
+
+    sizes = [3 * fw] * blocks + [cols] + [3 * GROUP] * groups
+    chunks = [
+        LineScatter(me, size, mine, theirs, swapped, kept_all.at[n], landed_all.at[n], work, sem_line.at[n])
+        for n, size in enumerate(sizes)
+    ]
+    writers = []
+    for n in range(blocks):
+        here = pl.ds(n * fw, fw)
+        parts = [(gate_out.at[:, here], True), (up_out.at[:, here], True), (down_out.at[here], False)]
+        writers.append(Writer(total, turned, parts, sem_write.at[n]))
+    writers.append(Writer(total, turned, [(o_out, False)], sem_write.at[blocks]))
+    for n in range(groups):
+        here = pl.ds(n * GROUP, GROUP)
+        parts = [(ref.at[:, here], True) for ref in (q_out, k_out, v_out)]
+        writers.append(Writer(total, turned, parts, sem_write.at[blocks + 1 + n]))
+    ticks = Ticks(chunks, total, writers)
+
+    def swap(n):
+        if n >= 1:
+            pl.semaphore_wait(free_core, 1)
+        chunks[n].swap().start()
+
+    def gain_row(which):
+        return jnp.concatenate(
+            [
+                gains_ref[side, pl.ds(s * 16 + which, 1), :].astype(F32)
+                for side in range(2)
+                for s in range(line)
+            ],
+            axis=1,
+        )
+
+    def products(left_of, right, first, size):
+        @pl.loop(0, line)
+        def _(s):
+            for side, dst in ((0, mine), (1, theirs)):
+                here = pl.ds(pl.multiple_of(side * half + s * shard, shard), shard)
+                dst[s, pl.ds(first, size), :] = dot_nn(left_of[...], right[:, here]).astype(BF16)
+
+    scatter = SquareScatter(me, stage, landed, sem_s)
+
+    def mlp(xs, gs, wb, sums, dgu_t, hid_t, hid):
+        loads = [
+            pltpu.make_async_copy(mlp_all.at[b], xs.at[pl.ds(b * rows, rows)], sem_c.at[b])
+            for b in range(4)
+        ] + [
+            pltpu.make_async_copy(g_all.at[b], gs.at[pl.ds(b * rows, rows)], sem_c.at[4 + b])
+            for b in range(4)
+        ]
+
+        def weights(n):
+            src = wf_early.at[n] if n < early else late_full.at[n - early]
+            return [
+                pltpu.make_async_copy(
+                    src.at[side], wb.at[n % 2, pl.ds(side * half, half)], sem_w.at[n % 2, side]
+                )
+                for side in range(2)
+            ]
+
+        def hidden_copy(n):
+            return pltpu.make_async_copy(
+                hid.at[n % 2], hidden_all.at[n], sem_c.at[8 + n % 2]
+            )
+
+        for copy in loads + weights(0):
+            copy.start()
+
+        @pl.loop(0, LEN // 64)
+        def _(i):
+            at = pl.ds(pl.multiple_of(i * 64, 64), 64)
+            sums[at, :] = jnp.zeros((64, 2 * half), F32)
+
+        for copy in loads:
+            copy.wait()
+        for n in range(blocks):
+            if n >= early:
+                while len(acts) > (blocks - 1 - n) * (line - 1):
+                    poll()
+                gathers[n - early].arrived()
+                for copy in weights(n):
+                    copy.start()
+            for copy in weights(n):
+                copy.wait()
+            if n + 1 < early:
+                for copy in weights(n + 1):
+                    copy.start()
+            if n >= 2:
+                hidden_copy(n - 2).wait()
+            w = wb.at[n % 2]
+            gu_w, down_w = w.at[:, pl.ds(0, 2 * fw)], w.at[:, pl.ds(2 * fw, fw)]
+
+            @pl.loop(0, 4)
+            def _(r, n=n, gu_w=gu_w, down_w=down_w):
+                at = pl.ds(pl.multiple_of(r * rows, rows), rows)
+                gu = dot_nn(xs[at, :], gu_w[...])
+                grad_hidden = dot_nn(gs[at, :], down_w[...])
+                gate_pre, upward = gu[:, :fw], gu[:, fw:]
+                sig = jax.nn.sigmoid(gate_pre)
+                activated = gate_pre * sig
+                hidden = (activated * upward).astype(BF16)
+                hid[n % 2, at, :] = hidden
+                hid_t[:, at] = hidden.T
+                grad_gate = grad_hidden * upward * sig * (1.0 + gate_pre * (1.0 - sig))
+                grad_up = grad_hidden * activated
+                dgu = jnp.concatenate([grad_gate, grad_up], axis=1).astype(BF16)
+                dgu_t[:, at] = dgu.T
+
+                @pl.loop(0, 4)
+                def _(c):
+                    here = pl.ds(pl.multiple_of(c * (half // 2), half // 2), half // 2)
+                    sums[at, here] += dot_nt(dgu, gu_w[here, :])
+
+            hidden_copy(n).start()
+            if n >= 1:
+                chunks[n - 1].reduce(free_core)
+            products(dgu_t, xs, 0, 2 * fw)
+            products(hid_t, gs, 2 * fw, fw)
+            swap(n)
+            if n < early:
+                poll()
+            if n in TICK_AFTER:
+                ticks.tick()
+        for n in range(max(0, blocks - 2), blocks):
+            hidden_copy(n).wait()
+
+        def to_stage(b, slot):
+            @pl.loop(0, rows // 64)
+            def _(i):
+                at = pl.ds(pl.multiple_of(i * 64, 64), 64)
+                there = pl.ds(pl.multiple_of(b * rows + i * 64, 64), 64)
+                if slot is None:
+                    own[at, :] = sums[there, :]
+                else:
+                    stage[slot, at, :] = sums[there, :].astype(BF16)
+
+        to_stage(3, 2)
+        scatter.diagonal_ready()
+        to_stage(1, 0)
+        to_stage(2, 1)
+        scatter.sides_ready()
+        to_stage(0, None)
+
+    pl.run_scoped(
+        mlp,
+        pltpu.VMEM((LEN, 2 * half), BF16),
+        pltpu.VMEM((LEN, 2 * half), BF16),
+        pltpu.VMEM((2, 2 * half, 3 * fw), BF16),
+        pltpu.VMEM((LEN, 2 * half), F32),
+        pltpu.VMEM((2 * fw, LEN), BF16),
+        pltpu.VMEM((fw, LEN), BF16),
+        pltpu.VMEM((2, LEN, fw), BF16),
+    )
+    gain_one, gain_two = gain_row(0), gain_row(1)
+    gp[...] = jnp.zeros(gp.shape, F32)
+    square = SquareGather(me, g2, sem_g2)
+
+    def free_landed():
+        for device, sem in ((me.x, free_x), (me.y, free_y)):
+            pl.semaphore_signal(
+                sem, inc=1, device_id=device, device_id_type=pl.DeviceIdType.MESH
+            )
+
+    def wait_free():
+        pl.semaphore_wait(free_x, 1)
+        pl.semaphore_wait(free_y, 1)
+
+    def summed(at):
+        return own[at, :] + landed[0, at, :].astype(F32) + landed[1, at, :].astype(F32)
+
+    def down(hidden, dw, rest):
+        hid_in = [
+            pltpu.make_async_copy(hidden_all.at[n], hidden.at[n], sem_c.at[n]) for n in range(blocks)
+        ]
+        dw_in = []
+        for n in range(blocks):
+            src = wf_early.at[n] if n < early else late_full.at[n - early]
+            for side in range(2):
+                dw_in.append(
+                    pltpu.make_async_copy(
+                        src.at[side, :, pl.ds(2 * fw, fw)], dw.at[n, pl.ds(side * half, half)],
+                        sem_c.at[8 + 2 * n + side],
+                    )
+                )
+        for copy in hid_in + dw_in:
+            copy.start()
+        chunks[blocks - 1].reduce(free_core)
+        ticks.tick()
+        for copy in hid_in + dw_in:
+            copy.wait()
+
+        @pl.loop(0, 4)
+        def _(b):
+            at = pl.ds(pl.multiple_of(b * rows, rows), rows)
+
+            @pl.loop(0, 2 * half // GROUP)
+            def _(c):
+                here = pl.ds(pl.multiple_of(c * GROUP, GROUP), GROUP)
+                value = sum(dot_nt(hidden[n, at, :], dw[n, here, :]) for n in range(blocks))
+                rest[b, :, here] = value.astype(BF16)
+
+        out = pltpu.make_async_copy(rest, y_all, sem_c.at[0])
+        out.start()
+        out.wait()
+
+    pl.run_scoped(
+        down,
+        pltpu.VMEM((blocks, LEN, fw), BF16),
+        pltpu.VMEM((blocks, 2 * half, fw), BF16),
+        pltpu.VMEM((4, local, 2 * half), BF16),
+    )
+    scatter.combine()
+
+    def attention(
+        rows_grad, q_ref, k_ref, v_ref, mixed_t, mixed, lse_ref, cos_ref, sin_ref, segc_ref, segr_ref,
+        normed, out_w, dm_ref, dqa_ref, dka_ref, dva_ref, part_t, bias_ref, middle, y_mine,
+    ):
+        ins = [
+            (middle_ref, middle), (g_all.at[0], g2.at[0]), (mixed_all, mixed), (q_all, q_ref),
+            (k_all, k_ref), (v_all, v_ref), (lse_all, lse_ref), (cos_all, cos_ref), (sin_all, sin_ref),
+            (segc_all, segc_ref), (segr_all, segr_ref), (out_full, out_w), (y_all.at[0], y_mine),
+        ] + [(normed_all.at[b], normed.at[pl.ds(b * rows, rows)]) for b in range(4)]
+        loads = [pltpu.make_async_copy(a, b, sem_c.at[n]) for n, (a, b) in enumerate(ins)]
+        for copy in loads:
+            copy.start()
+        ticks.tick()
+        scatter.arrived()
+
+        def second_norm_back(at, back):
+            grad = g2[0, at, :].astype(F32) + back
+            gm[at, :] = grad
+            g2[0, at, :] = grad.astype(BF16)
+
+        loads[0].wait()
+        loads[1].wait()
+        norm_back_rows(
+            local, gain_two, lambda at: middle[at, :], summed, gp, 1, second_norm_back
+        )
+        square.start()
+        free_landed()
+        scatter.done()
+        stage_in = [
+            pltpu.make_async_copy(y_all.at[b], stage.at[slot], sem_w.at[0, n])
+            for n, (b, slot) in enumerate(((3, 2), (1, 0)))
+        ] + [pltpu.make_async_copy(y_all.at[2], stage.at[1], sem_w.at[1, 0])]
+        for copy in stage_in:
+            copy.start()
+        for copy in loads[2:]:
+            copy.wait()
+        mixed_t[...] = mixed[...].T
+        square.forward()
+        ticks.tick()
+        for copy in stage_in:
+            copy.wait()
+        wait_free()
+        square.arrived()
+        scatter.diagonal_ready()
+        scatter.sides_ready()
+
+        @pl.loop(0, 4)
+        def _(b):
+            at = pl.ds(pl.multiple_of(b * rows, rows), rows)
+            dm_ref[at, :] = (
+                dot_nn(g2[b, :, :half], out_w[0]) + dot_nn(g2[b, :, half:], out_w[1])
+            ).astype(BF16)
+
+        @pl.loop(0, line)
+        def _(s):
+            for side, dst in ((0, mine), (1, theirs)):
+                here = pl.ds(pl.multiple_of(side * half + s * shard, shard), shard)
+                value = sum(
+                    dot_nn(mixed_t[:, pl.ds(b * rows, rows)], g2[b, :, here]) for b in range(4)
+                )
+                dst[s, pl.ds(0, cols), :] = value.astype(BF16)
+
+        swap(blocks)
+        head_lane = lax.broadcasted_iota(jnp.int32, (rows, 128), 1)
+        for group in range(groups):
+
+            @pl.loop(0, 4)
+            def _(b):
+                at = pl.ds(pl.multiple_of(b * rows, rows), rows)
+                dka_ref[at, :] = jnp.zeros((rows, GROUP), F32)
+                dva_ref[at, :] = jnp.zeros((rows, GROUP), F32)
+
+            for i in range(4):
+                places = [(j, me.spots[j]) for j in key_blocks(i, rows)]
+                at = pl.ds(pl.multiple_of(me.spots[i] * rows, rows), rows)
+                fill_bias(bias_ref, segc_ref[at, 0:1], segr_ref, i, places)
+                spots = [pl.ds(pl.multiple_of(p * rows, rows), rows) for _, p in places]
+
+                @pl.loop(0, GROUP // 128)
+                def _(pair, at=at, spots=spots, group=group):
+                    attend_back(
+                        pair, group * (GROUP // 128), at, spots, head_lane, q_ref, k_ref, v_ref,
+                        dm_ref, lse_ref, bias_ref, dqa_ref, dka_ref, dva_ref,
+                    )
+
+                if i == 1:
+                    chunks[blocks + group].reduce(free_core)
+                if i == 3 and group == 0:
+                    scatter.combine()
+
+            @pl.loop(0, 4)
+            def _(b, group=group):
+                at = pl.ds(pl.multiple_of(b * rows, rows), rows)
+                cosine, sine = cos_ref[at, :], sin_ref[at, :]
+                for part, ref in enumerate((dqa_ref, dka_ref, dva_ref)):
+                    value = ref[at, :]
+                    if part < 2:
+                        value = value * cosine - swap_halves(value) * sine
+                    value = value.astype(BF16)
+                    rows_grad[at, pl.ds(part * cols + group * GROUP, GROUP)] = value
+                    part_t[pl.ds(part * GROUP, GROUP), at] = value.T
+
+            products(part_t, normed, 0, 3 * GROUP)
+            swap(blocks + 1 + group)
+            ticks.tick()
+        scatter.arrived()
+
+        def output_rows(at):
+            total = middle[at, :] + y_mine[at, :].astype(F32)
+            total = total + landed[0, at, :].astype(F32) + landed[1, at, :].astype(F32)
+            output_ref[at, :] = total.astype(BF16)
+
+        norm_rows(local, output_rows)
+        free_landed()
+        scatter.done()
+
+    def normed_grads(rows_grad, qkv_w):
+        load = pltpu.make_async_copy(qkv_full, qkv_w, sem_c.at[0])
+        load.start()
+        chunks[blocks + groups].reduce(free_core)
+        load.wait()
+        wait_free()
+
+        def normed_grad(b, slot):
+            at = pl.ds(b * rows, rows)
+
+            @pl.loop(0, 2)
+            def _(side):
+                @pl.loop(0, half // GROUP)
+                def _(n):
+                    here = pl.ds(pl.multiple_of(n * GROUP, GROUP), GROUP)
+                    there = pl.ds(pl.multiple_of(side * half + n * GROUP, GROUP), GROUP)
+                    value = dot_nt(rows_grad[at, :], qkv_w[side, here, :])
+                    if slot is None:
+                        own[:, there] = value
+                    else:
+                        stage[slot, :, there] = value.astype(BF16)
+
+        normed_grad(3, 2)
+        scatter.diagonal_ready()
+        normed_grad(1, 0)
+        normed_grad(2, 1)
+        scatter.sides_ready()
+        normed_grad(0, None)
+
+    vmem = pltpu.VMEM
+    slab = vmem((LEN, cols), BF16)
+    table = vmem((LEN, GROUP), F32)
+
+    def heads(rows_grad):
+        pl.run_scoped(
+            functools.partial(attention, rows_grad),
+            slab, slab, slab, vmem((cols, LEN), BF16), slab, vmem((LEN, 128), F32), table, table,
+            vmem(segc_all.shape, jnp.int32), vmem(segr_all.shape, jnp.int32),
+            vmem((LEN, 2 * half), BF16), vmem(out_full.shape, BF16), slab, table, table, table,
+            vmem((3 * GROUP, LEN), BF16), vmem((3, rows, rows), F32), vmem((local, 2 * half), F32),
+            vmem((local, 2 * half), BF16),
+        )
+        pl.run_scoped(functools.partial(normed_grads, rows_grad), vmem(qkv_full.shape, BF16))
+
+    pl.run_scoped(heads, vmem((LEN, 3 * cols), BF16))
+    ticks.tick()
+    scatter.combine()
+    ticks.tick()
+    scatter.arrived()
+
+    def first_norm_back(at, back):
+        input_grad_ref[at, :] = gm[at, :] + back
+
+    norm_back_rows(
+        local, gain_one, lambda at: x_ref[at, :].astype(F32), summed, gp, 0, first_norm_back
+    )
+    scatter.done()
+    for n, device in enumerate((me.x, me.y, me.other, me.next, me.far)):
+        copy = remote(gp, gp_landed.at[n], sem_gain.at[n, 0], sem_gain.at[n, 1], device)
+        copy.start()
+        copy.wait()
+        if device is me.other:
+            gp[:, :half] += gp_landed[n, :, half:]
+            gp[:, half:] += gp_landed[n, :, :half]
+        else:
+            gp[...] += gp_landed[n]
+    gain_out_ref[...] = gp[...]
+    ticks.rest()
+    pl.semaphore_wait(free_core, 1)
+    square.done()
+    for one in gathers:
+        one.done()
+
+
+def backward(dp, x, g_all, normed_all, mlp_all, middle, gains, wf_early, wf_late, qkv, out, q, k, v, mixed, lse, cosine, sine, segc, segr):
+    line = dp // 2
+    local, d = x.shape
+    cols = q.shape[1]
+    early, late = wf_early.shape[0], wf_late.shape[0]
+    fcols = wf_late.shape[2]
+    fw = fcols // 3
+    blocks = early + late
+    groups = cols // GROUP
+    count = blocks + 1 + groups
+    shard = d // dp
+    ff = blocks * fw
+    most = max(fcols, cols, 3 * GROUP)
+    vm, hbm = pl.BlockSpec(memory_space=pltpu.VMEM), pl.BlockSpec(memory_space=pl.ANY)
+    S, vmem, dma = jax.ShapeDtypeStruct, pltpu.VMEM, pltpu.SemaphoreType.DMA
+    regular = pltpu.SemaphoreType.REGULAR
+    return pl.pallas_call(
+        functools.partial(backward_kernel, dp),
+        in_specs=[vm, hbm, hbm, hbm, hbm, vm] + [hbm] * 13,
+        out_specs=[vm, vm, vm] + [hbm] * 12,
+        out_shape=[
+            S((local, d), BF16), S((local, d), F32), S((8, d), F32),
+            S((shard, ff), F32), S((shard, ff), F32), S((ff, shard), F32),
+            S((shard, cols), F32), S((shard, cols), F32), S((shard, cols), F32), S((cols, shard), F32),
+            S((late, 2, d // 2, fcols), BF16), S((blocks, LEN, fw), BF16),
+            S((count, line, most, shard), BF16), S((count, line + 1, most, shard), BF16),
+            S((4, local, d), BF16),
+        ],
+        scratch_shapes=[
+            vmem((line, most, shard), BF16), vmem((line, most, shard), BF16),
+            vmem((line, most, shard), BF16), vmem((9, most, shard), BF16),
+            vmem((most, shard), F32), vmem((3, shard, 256), F32),
+            vmem((3, local, d), BF16), vmem((3, local, d), BF16), vmem((4, local, d), BF16),
+            vmem((local, d), F32), vmem((local, d), F32), vmem((8, d), F32), vmem((5, 8, d), F32),
+            dma((late, 6, line)), dma((count, 4 + 2 * line + 9)), dma((count, 3)), dma((12,)),
+            dma((8,)), dma((5, 2)), dma((8 + 2 * blocks,)), dma((2, 2)), regular, regular, regular,
+        ],
+        compiler_params=pltpu.CompilerParams(
+            vmem_limit_bytes=VMEM_BYTES, collective_id=1, has_side_effects=True
+        ),
+        name="backward",
+    )(x, g_all, normed_all, mlp_all, middle, gains, wf_early, wf_late, qkv, out, q, k, v, mixed, lse, cosine, sine, segc, segr)
+
+
+def attend_back(
+    pair, first, at, spots, head_lane, q_ref, k_ref, v_ref, dm_ref, lse_ref, bias_ref, dqa_ref, dka_ref, dva_ref
+):
+    scale = HEAD_DIM**-0.5
+    rows = at.size
+    lanes = pl.ds(pl.multiple_of((first + pair) * 128, 128), 128)
+    there = pl.ds(pl.multiple_of(pair * 128, 128), 128)
+    query, grad = q_ref[at, lanes], dm_ref[at, lanes]
+    logs = lse_ref[at, :]
+    outs = []
+    for h in range(2):
+        mine = (head_lane < HEAD_DIM) if h == 0 else (head_lane >= HEAD_DIM)
+        qm = jnp.where(mine, query, 0) * jnp.asarray(scale, BF16)
+        gm = jnp.where(mine, grad, 0)
+        log = jnp.sum(
+            jnp.where(head_lane == (first + pair) * 2 + h, logs, 0.0), axis=1, keepdims=True
+        )
+        weights = [
+            jnp.exp(dot_nt(qm, k_ref[s, lanes]) + bias_ref[n] - log) for n, s in enumerate(spots)
+        ]
+        grads = [dot_nt(gm, v_ref[s, lanes]) for s in spots]
+        inner = sum(jnp.sum(w * g, axis=1, keepdims=True) for w, g in zip(weights, grads))
+        dq = jnp.zeros((rows, 128), F32)
+        for w, g, s in zip(weights, grads, spots):
+            ds = (w * (g - inner)).astype(BF16)
+            dva_ref[s, there] += dot_tn(w.astype(BF16), gm)
+            dka_ref[s, there] += dot_tn(ds, qm)
+            dq = dq + dot_nn(ds, k_ref[s, lanes])
+        outs.append(dq)
+    dqa_ref[at, there] = jnp.where(head_lane < HEAD_DIM, outs[0], outs[1]) * scale
+
+
 def on_device(
     dp, tensor, hidden_in, doc_lengths, gain_attn, w_query, w_key, w_value, w_out, gain_mlp,
     w_gate, w_up, w_down, cotangent,
@@ -680,7 +1422,7 @@
     line = dp // 2
     core = lax.axis_index("dp") % 2
     place = lax.axis_index("tensor")
-    square = tensor == 4
+    square = tensor == 4 and dp == 8
     same_core = [[c + 2 * z for z in range(line)] for c in range(2)]
     sibling = [(i, i ^ 1) for i in range(dp)]
     d = hidden_in.shape[1]
@@ -760,41 +1502,47 @@
     g_local = own_first(cotangent)
     inputs = hidden_mine.astype(F32)
     factor_one = norm_factor(inputs)
-    early = FF_EARLY if square else 0
-    ff_sets = [jnp.concatenate(line_gather(shard), axis=0) for shard in shards[early:]]
     if square:
         gain_rows = jnp.pad(jnp.stack([gain_attn, gain_mlp]), ((0, 14), (0, 0)))
         (
             normed, g_all, normed_mlp, query, keys, values, mixed, lse, middle, qkv_full,
             out_full, ff_full, gains,
         ) = forward(
-            dp, hidden_mine, qkv_shard, w_out.T, jnp.stack(shards[:early]), g_local, gain_rows,
+            dp, hidden_mine, qkv_shard, w_out.T, jnp.stack(shards[:FF_EARLY]), g_local, gain_rows,
             cosine, sine, segc, segr,
         )
-        normed, g_all, normed_mlp = (a.reshape(LEN, d) for a in (normed, g_all, normed_mlp))
-        qkv_own, qkv_sib = qkv_full[0], qkv_full[1]
-        out_own, out_sib = out_full[0], out_full[1]
-        ff_sets = [ff_full[b].reshape(d, 3 * fb) for b in range(early)] + ff_sets
-        gains = gains.reshape(2 * line, 16, d // dp)[:, :2].astype(F32)
-        gain_one, gain_two = gains[:, 0].reshape(d), gains[:, 1].reshape(d)
-        factor_two = norm_factor(middle)
-    else:
-        gains = lax.all_gather(jnp.stack([gain_attn, gain_mlp]), "dp", axis=0)
-        gains = own_first(jnp.moveaxis(gains, 0, 1).reshape(2, d)).astype(F32)
-        gain_one, gain_two = gains[0], gains[1]
-        qkv_own, qkv_sib = line_gather(qkv_shard)
-        out_own, out_sib = line_gather(w_out.T)
-        normed = gather_rows((inputs * factor_one * gain_one).astype(BF16))
-        g_all = gather_rows(g_local)
-        query, keys, values, mixed, lse = attn_forward(
-            blocks, key, normed, qkv_own, qkv_sib, cosine, sine, segc, segr
-        )
-        attended = jnp.concatenate(
-            [dot_nt(mixed, out_own).astype(BF16), dot_nt(mixed, out_sib).astype(BF16)], axis=1
-        )
-        middle = inputs + scatter_rows(attended)
-        factor_two = norm_factor(middle)
-        normed_mlp = gather_rows((middle * factor_two * gain_two).astype(BF16))
+        (
+            output, input_grad, gain_sum, grad_gate, grad_up, grad_down, grad_query, grad_key,
+            grad_value, grad_out, *_,
+        ) = backward(
+            dp, hidden_mine, g_all, normed, normed_mlp, middle, gains, ff_full,
+            jnp.stack(shards[FF_EARLY:]), qkv_full, out_full, query, keys, values, mixed, lse,
+            cosine, sine, segc, segr,
+        )
+        share = d // (dp * tensor)
+        first = (lax.axis_index("dp") // 2) * (d // dp) + place * share
+        gain_sum = lax.dynamic_slice_in_dim(gain_sum, first, share, 1)
+        return (
+            true_order(output), true_order(input_grad), gain_sum[0], grad_query, grad_key,
+            grad_value, grad_out, gain_sum[1], grad_gate, grad_up, grad_down,
+        )
+    gains = lax.all_gather(jnp.stack([gain_attn, gain_mlp]), "dp", axis=0)
+    gains = own_first(jnp.moveaxis(gains, 0, 1).reshape(2, d)).astype(F32)
+    gain_one, gain_two = gains[0], gains[1]
+    qkv_own, qkv_sib = line_gather(qkv_shard)
+    out_own, out_sib = line_gather(w_out.T)
+    normed = gather_rows((inputs * factor_one * gain_one).astype(BF16))
+    g_all = gather_rows(g_local)
+    query, keys, values, mixed, lse = attn_forward(
+        blocks, key, normed, qkv_own, qkv_sib, cosine, sine, segc, segr
+    )
+    attended = jnp.concatenate(
+        [dot_nt(mixed, out_own).astype(BF16), dot_nt(mixed, out_sib).astype(BF16)], axis=1
+    )
+    middle = inputs + scatter_rows(attended)
+    factor_two = norm_factor(middle)
+    normed_mlp = gather_rows((middle * factor_two * gain_two).astype(BF16))
+    ff_sets = [jnp.concatenate(line_gather(shard), axis=0) for shard in shards]
 
     down_sum = jnp.zeros((LEN, d), F32)
     back_sum = jnp.zeros((LEN, d), F32)

time: 934 us -> 706 us (0.76)
  Pallas kernels: 320 us -> 643 us
  matrix products: 192 us -> 0 us
  waiting for transfers between devices: 133 us -> 0 us
  other arithmetic: 92.3 us -> 11.1 us
  blocking collectives: 69.5 us -> 0 us
  local copies, waits for them, and re-layouts: 85 us -> 43 us
  starting transfers between devices: 19.5 us -> 0 us
  between operations: 15.7 us -> 1.47 us
    pallas_call x1, Pallas kernels: 37.7 us -> 442 us  [backward(): pl.pallas_call(functools.partial(backward_kernel, dp), in_specs=[vm, hbm,...]
    dot_general x42 -> x0, matrix products: 192 us -> none  [the longest x14 106 us: dot_nt(): lax.dot_general(a, b, (((1,), (1,)), ((), ())), preferred_element_type=F32)]
    ppermute x23 -> x0, waiting for transfers between devices: 133 us -> none  [the longest x16 133 us: hop(): return lax.ppermute(a, 'tensor', [(i, i ^ step) for i in range(tensor)])]
    pallas_call x1, Pallas kernels: 282 us -> 201 us  [forward(): pl.pallas_call(functools.partial(forward_kernel, dp), in_specs=[vmem, vme...]
    all_gather x1 -> x0, blocking collectives: 69.5 us -> none  [on_device(): shares = lax.all_gather(parts, ('dp', 'tensor'), axis=0)]
    concatenate x16 -> x0, other arithmetic: 41.9 us -> none  [the longest x4 32.8 us: on_device(): jnp.concatenate([dot_tn(normed_mlp, grad_gate_pre).astype(BF16), dot_tn(n...]
    add x12 -> x0, other arithmetic: 24.6 us -> none  [the longest x5 15.2 us: line_scatter(): mine = own + lax.ppermute(sib, 'dp', sibling)]
    slice x16 -> x0, local copies, waits for them, and re-layouts: 22 us -> none  [the longest x4 9.19 us: on_device(): g[:, 2 * fb:]]
  transfers between devices with their start and end apart: 30 -> 0, of which waited for: 10 -> 0; matrix products, arithmetic and copies ran while one was open for 37% -> 0% of each run, Pallas kernels for 34% -> 0%
where the time goes in v3:
time: 706 us; the launch traced here: 699 us
  Pallas kernels  643 us (91%)
  local copies, waits for them, and re-layouts  43 us (6%)
  other arithmetic  11.1 us (2%)
    pallas_call x1, Pallas kernels, backward(): pl.pallas_call(functools.partial(backward_kernel, dp), in_specs=[vm, hbm,...  442 us
    pallas_call x1, Pallas kernels, forward(): pl.pallas_call(functools.partial(forward_kernel, dp), in_specs=[vmem, vme...  201 us
    unnamed x48, local copies, waits for them, and re-layouts  17 us

profile of v3, /device:TPU:0, one launch (start us, length us, event | category | flops | bytes accessed | tf_op | source)
XLA Modules:
  0.0 698.5 jit_solution(16277283410153049757)
XLA Ops:
  4.9 1.8 copy.57
  8.5 1.3 copy.61.cos_ref.cos_all
  10.9 1.3 copy.62.sin_ref.sin_all
  15.9 1.5 fusion.7
  18.6 1.3 pad_maximum_fusion.1.wf_ref
  20.0 1.3 pad_maximum_fusion.2.wf_late
  21.3 1.5 fusion.10
  22.8 1.5 fusion.11
  24.3 1.1 select_bitcast_fusion.4
  26.0 1.3 copy.81
  27.9 1.3 copy.80
  29.1 200.9 %forward.1 = (bf16[4,256,2048]{2,1,0:T(8,128)(2,1)}, bf16[4,256,2048]{2,1,0:T(8,128)(2,1)}, bf16[4,256,2048]{2,1,0:T(8,128)(2,1)}, bf16[1024,512]{1,0:T(8,128)(2...) custom-call(bf16[256,2048]{1,0:T(8,128)(2,1)} %bitcast.72, ...), custom_call_target="tpu_custom_call" | custom-call | tf_op jit(solution)/shard_map/forward/pallas_call | solution.py:655
  230.0 442.1 %backward.1 = (bf16[256,2048]{1,0:T(8,128)(2,1)}, f32[256,2048]{1,0:T(8,128)}, f32[8,2048]{1,0:T(8,128)}, f32[256,2048]{1,0:T(8,128)}, f32[256,2048]{1,0:T(8,128...) custom-call(bf16[256,2048]{1,0:T(8,128)(2,1)} %bitcast.73, ...), custom_call_target="tpu_custom_call" | custom-call | tf_op jit(solution)/shard_map/backward/pallas_call | solution.py:1358
  672.1 1.8 reshape.204
  675.1 1.6 copy.67
  676.8 1.6 reshape.205
  679.7 2.7 reshape.206
  683.4 1.6 copy.72
  685.0 2.7 reshape.207
  687.7 2.0 copy.98
  692.1 1.3 copy.102
  693.4 1.0 copy-done.1
  694.4 1.3 copy.103
  696.8 1.3 copy.104
  (74 shorter events, 19.9 us)
Async XLA Ops:
  7.3 2.5 copy-start.15
  7.3 2.5 copy-start.16
  7.3 2.4 copy-start.17
  10.8 1.4 copy-start.3
  10.9 2.1 copy-start.4
  13.7 1.5 copy-start.5
  15.9 1.7 copy-start.6
  15.9 1.7 copy-start.10
  15.9 1.7 copy-start.11
  17.4 1.0 copy-start.8
  17.4 1.0 copy-start.9
  17.6 0.9 copy-start.7
  685.0 4.7 copy-start.14
  685.0 5.5 copy-start.13
  687.7 3.6 copy-start.12
  687.7 4.4 copy-start.2
  692.1 2.3 copy-start.1
  694.4 2.3 copy-start

commit v4 on v2

--- a/solution.py
+++ b/solution.py
@@ -14,11 +14,10 @@
 ROPE_BASE = 130000.0
 NEG = -1e30
 GROUP = 256
-FF_BLOCKS = 4
-FF_EARLY = 2
+FF_BLOCKS = 8
 F32 = jnp.float32
 BF16 = jnp.bfloat16
-VMEM_BYTES = 56 * 1024 * 1024
+VMEM_BYTES = 60 * 1024 * 1024
 
 
 def dot_nn(a, b):
@@ -58,7 +57,7 @@
     inverse = jnp.power(ROPE_BASE, -jnp.arange(half, dtype=F32) * 2.0 / HEAD_DIM)
     angles = position.astype(F32)[:, None] * inverse
     cosine, sine = jnp.cos(angles), jnp.sin(angles)
-    heads = GROUP // HEAD_DIM
+    heads = 128 // HEAD_DIM
     return (
         jnp.tile(jnp.concatenate([cosine, cosine], axis=1), (1, heads)),
         jnp.tile(jnp.concatenate([-sine, sine], axis=1), (1, heads)),
@@ -322,16 +321,22 @@
 class SquareGather:
     def __init__(self, me, full, sems):
         self.me, self.full, self.sems = me, full, sems
-        self.half = full.shape[1] // 2
+        self.rows = full.shape[0] // 4
 
     def copies(self):
-        me, full, sems, half = self.me, self.full, self.sems, self.half
-        top, bottom = pl.ds(0, half), pl.ds(half, half)
+        me, full, sems, rows = self.me, self.full, self.sems, self.rows
+        half = rows // 2
+
+        def part(first, size):
+            return full.at[pl.ds(first, size)]
+
         return (
-            remote(full.at[0], full.at[1], sems.at[0], sems.at[1], me.x),
-            remote(full.at[0], full.at[2], sems.at[2], sems.at[3], me.y),
-            remote(full.at[1, top], full.at[3, top], sems.at[4], sems.at[5], me.y),
-            remote(full.at[2, bottom], full.at[3, bottom], sems.at[6], sems.at[7], me.x),
+            remote(part(0, rows), part(rows, rows), sems.at[0], sems.at[1], me.x),
+            remote(part(0, rows), part(2 * rows, rows), sems.at[2], sems.at[3], me.y),
+            remote(part(rows, half), part(3 * rows, half), sems.at[4], sems.at[5], me.y),
+            remote(
+                part(2 * rows + half, half), part(3 * rows + half, half), sems.at[6], sems.at[7], me.x
+            ),
         )
 
     def start(self):
@@ -420,12 +425,14 @@
 class Place:
     def __init__(self, dp):
         index = lax.axis_index("dp")
+        self.index, self.dp = index, dp
         self.line = dp // 2
         self.z, self.core = index // 2, index % 2
         self.t = lax.axis_index("tensor")
         tx, ty = self.t % 2, self.t // 2
         self.other = {"dp": index + 1 - 2 * self.core}
         self.up, self.down = {"dp": index + 2}, {"dp": index - 2}
+        self.next, self.far = {"dp": index + 2 - 4 * (self.z % 2)}, {"dp": index + 4 - 8 * (self.z // 2)}
         self.x = {"tensor": self.t + 1 - 2 * tx}
         self.y = {"tensor": self.t + 2 - 4 * ty}
         self.spots = [
@@ -434,187 +441,18 @@
 
     def greet(self):
         barrier = pltpu.get_barrier_semaphore()
-
-        def signal(device):
+        peers = [self.x, self.y] + [{"dp": (self.index + k) % self.dp} for k in range(1, self.dp)]
+        for device in peers:
             pl.semaphore_signal(
                 barrier, inc=1, device_id=device, device_id_type=pl.DeviceIdType.MESH
             )
-
-        for device in (self.other, self.x, self.y):
-            signal(device)
-        pl.when(self.z + 1 < self.line)(lambda: signal(self.up))
-        pl.when(self.z >= 1)(lambda: signal(self.down))
-        ends = (self.z == 0) | (self.z == self.line - 1)
-        pl.when(ends)(lambda: pl.semaphore_wait(barrier, 4))
-        pl.when(jnp.logical_not(ends))(lambda: pl.semaphore_wait(barrier, 5))
+        pl.semaphore_wait(barrier, len(peers))
 
 
 def norm_rows(count, body, step=32):
     @pl.loop(0, count // step)
     def _(n):
         body(pl.ds(pl.multiple_of(n * step, step), step))
-
-
-def forward_kernel(
-    dp, x_ref, wa_ref, wo_ref, wf_ref, g_ref, gain_ref, cos_ref, sin_ref, segc_ref, segr_ref,
-    normed_ref, gall_ref, normed_mlp_ref, q_ref, k_ref, v_ref, mixed_ref, lse_ref, middle_ref,
-    wa_full, wo_full, wf_full, gains_ref,
-    bias_ref, local_ref, stage_ref, landed_ref,
-    sem_gain, sem_a, sem_o, sem_f, sem_n, sem_g, sem_s, sem_m, sem_c,
-):
-    me = Place(dp)
-    me.greet()
-    nf = wf_ref.shape[0]
-    gain = LineGather(me, gain_ref, gains_ref, sem_gain)
-    wa = LineGather(me, wa_ref, wa_full, sem_a)
-    wo = LineGather(me, wo_ref, wo_full, sem_o)
-    wf = [LineGather(me, wf_ref.at[b], wf_full.at[b], sem_f.at[b]) for b in range(nf)]
-    normed = SquareGather(me, normed_ref, sem_n)
-    grads = SquareGather(me, gall_ref, sem_g)
-    normed_mlp = SquareGather(me, normed_mlp_ref, sem_m)
-    hops = range(1, me.line)
-
-    gain.start()
-    wa.start()
-    keep_g = pltpu.make_async_copy(g_ref, gall_ref.at[0], sem_c.at[0])
-    keep_g.start()
-    for h in hops:
-        gain.hop(h)
-    gain.arrived()
-
-    half = x_ref.shape[1] // 2
-    shard = gain_ref.shape[1]
-
-    def gain_row(which, width):
-        return jnp.concatenate(
-            [
-                gains_ref[side, pl.ds(s * 16 + which, 1), :].astype(F32)
-                for side in range(2)
-                for s in range(me.line)
-            ],
-            axis=1,
-        )
-
-    gain_one, gain_two = gain_row(0, shard), gain_row(1, shard)
-
-    def first_norm(at):
-        values = x_ref[at, :].astype(F32)
-        normed_ref[0, at, :] = (values * norm_factor(values) * gain_one).astype(BF16)
-
-    norm_rows(x_ref.shape[0], first_norm)
-    normed.start()
-    wa.hop(1)
-    normed.forward()
-    wa.hop(2)
-    grads_started = False
-    for h in range(3, me.line):
-        wa.hop(h)
-    wo.start()
-    keep_g.wait()
-    grads.start()
-    normed.arrived()
-    wa.arrived()
-    wf[0].start()
-
-    rows = LEN // 4
-    cols = q_ref.shape[1]
-    groups = cols // GROUP
-
-    @pl.loop(0, 4 * groups)
-    def _(n):
-        b, group = n // groups, n % groups
-        at = pl.ds(pl.multiple_of(b * rows, rows), rows)
-        lanes = pl.ds(pl.multiple_of(group * GROUP, GROUP), GROUP)
-        left, right = normed_ref[b, :, :half], normed_ref[b, :, half:]
-        cosine, sine = cos_ref[at, :], sin_ref[at, :]
-
-        def product(part):
-            here = pl.ds(pl.multiple_of(part * cols + group * GROUP, GROUP), GROUP)
-            return dot_nn(left, wa_full[0, :, here]) + dot_nn(right, wa_full[1, :, here])
-
-        query = product(0)
-        q_ref[at, lanes] = (query * cosine + swap_halves(query) * sine).astype(BF16)
-        keys = product(1)
-        k_ref[at, lanes] = (keys * cosine + swap_halves(keys) * sine).astype(BF16)
-        v_ref[at, lanes] = product(2).astype(BF16)
-
-    wo.hop(1)
-    head_lane = lax.broadcasted_iota(jnp.int32, (rows, 128), 1)
-    for i in range(4):
-        places = [(j, me.spots[j]) for j in key_blocks(i, rows)]
-        at = pl.ds(pl.multiple_of(me.spots[i] * rows, rows), rows)
-        fill_bias(bias_ref, segc_ref[at, 0:1], segr_ref, i, places)
-        spots = [pl.ds(pl.multiple_of(p * rows, rows), rows) for _, p in places]
-
-        @pl.loop(0, cols // 128)
-        def _(pair, at=at, spots=spots):
-            attend(pair, 0, at, spots, head_lane, q_ref, k_ref, v_ref, mixed_ref, lse_ref, bias_ref)
-
-        if i == 0:
-            wo.hop(2)
-        if i == 1:
-            for h in range(3, me.line):
-                wo.hop(h)
-            grads.forward()
-        if i == 2:
-            wf[0].hop(1)
-
-    wo.arrived()
-    scatter = SquareScatter(me, stage_ref, landed_ref, sem_s)
-
-    def out_rows(b, slot):
-        at = pl.ds(b * rows, rows)
-
-        @pl.loop(0, 2)
-        def _(side):
-            @pl.loop(0, half // GROUP)
-            def _(n):
-                here = pl.ds(pl.multiple_of(n * GROUP, GROUP), GROUP)
-                there = pl.ds(pl.multiple_of(side * half + n * GROUP, GROUP), GROUP)
-                total = dot_nt(mixed_ref[at, :], wo_full[side, here, :])
-                if slot is None:
-                    middle_ref[:, there] = total
-                else:
-                    stage_ref[slot, :, there] = total.astype(BF16)
-
-    out_rows(3, 2)
-    scatter.diagonal_ready()
-    out_rows(1, 0)
-    out_rows(2, 1)
-    scatter.sides_ready()
-    out_rows(0, None)
-    wf[0].hop(2)
-    scatter.combine()
-    for h in range(3, me.line):
-        wf[0].hop(h)
-    if nf > 1:
-        wf[1].start()
-    scatter.arrived()
-
-    def second_norm(at):
-        total = middle_ref[at, :] + landed_ref[0, at, :].astype(F32)
-        total = total + landed_ref[1, at, :].astype(F32)
-        middle = x_ref[at, :].astype(F32) + total
-        middle_ref[at, :] = middle
-        local_ref[at, :] = (middle * norm_factor(middle) * gain_two).astype(BF16)
-
-    norm_rows(x_ref.shape[0], second_norm)
-    keep_m = pltpu.make_async_copy(local_ref, normed_mlp_ref.at[0], sem_c.at[1])
-    keep_m.start()
-    keep_m.wait()
-    normed_mlp.start()
-    if nf > 1:
-        wf[1].hop(1)
-    normed_mlp.forward()
-    if nf > 1:
-        for h in range(2, me.line):
-            wf[1].hop(h)
-    normed_mlp.arrived()
-    grads.arrived()
-    for one in wf:
-        one.arrived()
-    for one in (gain, wa, wo, *wf, normed, grads, normed_mlp, scatter):
-        one.done()
 
 
 def attend(pair, first, at, spots, head_lane, q_ref, k_ref, v_ref, mixed_ref, lse_ref, bias_ref):
@@ -638,39 +476,961 @@
     lse_ref[at, :] = kept
 
 
-def forward(dp, x, wa, wo, wf, g, gains, cosine, sine, segc, segr):
+def add_into(total, other, rows, step=64):
+    @pl.loop(0, rows // step)
+    def _(n):
+        at = pl.ds(pl.multiple_of(n * step, step), step)
+        total[at, :] = (total[at, :].astype(F32) + other[at, :].astype(F32)).astype(total.dtype)
+
+
+class LineScatter:
+    def __init__(self, me, rows, mine, theirs, swapped, kept, landed, work, sems):
+        cut = lambda ref: ref.at[:, pl.ds(0, rows)]
+        self.me, self.rows = me, rows
+        self.mine, self.theirs, self.swapped = cut(mine), cut(theirs), cut(swapped)
+        self.kept, self.landed, self.work = cut(kept), cut(landed), cut(work)
+        self.sems = sems
+
+    def swap(self):
+        return remote(
+            self.theirs, self.swapped, self.sems.at[0], self.sems.at[1], self.me.other
+        )
+
+    def keep(self):
+        return pltpu.make_async_copy(self.mine, self.kept, self.sems.at[2])
+
+    def send(self, src, s, upward, z):
+        line = self.me.line
+        if upward:
+            slot, device = s, self.me.up
+        else:
+            slot, device = (s if s < z - 1 else line), self.me.down
+        return remote(
+            src, self.landed.at[slot], self.sems.at[3 + s], self.sems.at[3 + line + slot], device
+        )
+
+    def landing(self, slot):
+        line = self.me.line
+        return remote(
+            self.landed.at[slot], self.landed.at[slot], self.sems.at[3],
+            self.sems.at[3 + line + slot], self.me.other,
+        )
+
+    def load(self, src, n):
+        return pltpu.make_async_copy(src, self.work.at[n], self.sems.at[4 + 2 * self.me.line + n])
+
+    def reduce(self, free_sem):
+        line = self.me.line
+        self.swap().wait_recv()
+        for s in range(line):
+            add_into(self.mine.at[s], self.swapped.at[s], self.rows)
+        pl.semaphore_signal(
+            free_sem, inc=1, device_id=self.me.other, device_id_type=pl.DeviceIdType.MESH
+        )
+        self.keep().start()
+        self.swap().wait_send()
+        self.keep().wait()
+        for end, upward in ((0, True), (line - 1, False)):
+
+            @pl.when(self.me.z == end)
+            def _(end=end, upward=upward):
+                order = range(line - 1, end, -1) if upward else range(end)
+                for s in order:
+                    self.send(self.kept.at[s], s, upward, end).start()
+
+    def going(self, p):
+        line = self.me.line
+        for z, upward in ((p, True), (line - 1 - p, False)):
+            targets = list(range(line - 1, z, -1)) if upward else list(range(z))
+            yield z, upward, targets
+
+    def load_phase(self, p, first):
+        for z, upward, targets in self.going(p):
+
+            @pl.when(self.me.z == z)
+            def _(targets=targets):
+                for n, s in enumerate(targets):
+                    self.landing(s).wait_recv()
+                    self.load(self.landed.at[s], first + 2 * n).start()
+                    self.load(self.kept.at[s], first + 2 * n + 1).start()
+
+    def run_phase(self, p, first):
+        for z, upward, targets in self.going(p):
+
+            @pl.when(self.me.z == z)
+            def _(z=z, upward=upward, targets=targets):
+                for n, s in enumerate(targets):
+                    a, b = first + 2 * n, first + 2 * n + 1
+                    self.load(self.landed.at[s], a).wait()
+                    self.load(self.kept.at[s], b).wait()
+                    add_into(self.work.at[a], self.work.at[b], self.rows)
+                    self.send(self.work.at[a], s, upward, z).start()
+
+    def sent_phase(self, p, first):
+        for z, upward, targets in self.going(p):
+
+            @pl.when(self.me.z == z)
+            def _(z=z, upward=upward, targets=targets):
+                for n, s in enumerate(targets):
+                    self.send(self.work.at[first + 2 * n], s, upward, z).wait_send()
+
+    def load_last(self, first):
+        me = self.me
+        self.load(self.kept.at[me.z], first).start()
+
+        @pl.when(me.z >= 1)
+        def _():
+            self.landing(me.z).wait_recv()
+            self.load(self.landed.at[me.z], first + 1).start()
+
+        @pl.when(me.z < me.line - 1)
+        def _():
+            self.landing(me.line).wait_recv()
+            self.load(self.landed.at[me.line], first + 2).start()
+
+    def run_last(self, first, total):
+        me = self.me
+        here = total.at[pl.ds(0, self.rows)]
+        self.load(self.kept.at[me.z], first).wait()
+
+        def put(n, step=64):
+            @pl.loop(0, self.rows // step)
+            def _(i):
+                at = pl.ds(pl.multiple_of(i * step, step), step)
+                if n == first:
+                    here[at, :] = self.work[n, at, :].astype(F32)
+                else:
+                    here[at, :] += self.work[n, at, :].astype(F32)
+
+        put(first)
+
+        @pl.when(me.z >= 1)
+        def _():
+            self.load(self.landed.at[me.z], first + 1).wait()
+            put(first + 1)
+
+        @pl.when(me.z < me.line - 1)
+        def _():
+            self.load(self.landed.at[me.line], first + 2).wait()
+            put(first + 2)
+
+    def done(self):
+        line = self.me.line
+        for end, upward in ((0, True), (line - 1, False)):
+
+            @pl.when(self.me.z == end)
+            def _(end=end, upward=upward):
+                for s in range(line - 1, end, -1) if upward else range(end):
+                    self.send(self.kept.at[s], s, upward, end).wait_send()
+
+
+class Ticks:
+    def __init__(self, chunks, total, writers):
+        self.chunks, self.total, self.writers = chunks, total, writers
+        self.k = 0
+
+    def jobs(self, k):
+        count = len(self.chunks)
+        out = []
+        if 0 <= k < count:
+            out.append((self.chunks[k], 1, 0))
+        if 0 <= k - 1 < count:
+            out.append((self.chunks[k - 1], 2, 4))
+        return out
+
+    def tick(self):
+        k = self.k
+        for chunk, p, first in self.jobs(k - 1):
+            chunk.sent_phase(p, first)
+        last = self.chunks[k - 2] if 0 <= k - 2 < len(self.chunks) else None
+        for chunk, p, first in self.jobs(k):
+            chunk.load_phase(p, first)
+        if last is not None:
+            last.load_last(6)
+        for chunk, p, first in self.jobs(k):
+            chunk.run_phase(p, first)
+        if last is not None:
+            if k - 2 > 0:
+                self.writers[k - 3].wait()
+            last.run_last(6, self.total)
+            self.writers[k - 2].start()
+        self.k += 1
+
+    def rest(self):
+        while self.k < len(self.chunks) + 2:
+            self.tick()
+        self.writers[-1].wait()
+        for chunk in self.chunks:
+            chunk.done()
+
+
+class Writer:
+    def __init__(self, total, turned, parts, sem):
+        self.total, self.turned, self.parts, self.sem = total, turned, parts, sem
+
+    def copies(self):
+        for n, (dst, _) in enumerate(self.parts):
+            yield pltpu.make_async_copy(self.turned.at[n], dst, self.sem.at[n])
+
+    def start(self):
+        for n, (_, flip) in enumerate(self.parts):
+            block = self.total[pl.ds(n * 256, 256), :]
+            self.turned[n] = (block.T if flip else block).astype(BF16)
+        for copy in self.copies():
+            copy.start()
+
+    def wait(self):
+        for copy in self.copies():
+            copy.wait()
+
+
+def norm_back_rows(count, gain, values_of, grads_of, gain_ref, row, put, step=32):
+    @pl.loop(0, count // step)
+    def _(n):
+        at = pl.ds(pl.multiple_of(n * step, step), step)
+        values, grads = values_of(at), grads_of(at)
+        factor = norm_factor(values)
+        scaled = grads * gain
+        back = factor * scaled - values * factor * factor * factor * jnp.mean(
+            scaled * values, axis=-1, keepdims=True
+        )
+        gain_ref[row : row + 1, :] += jnp.sum(grads * values * factor, axis=0, keepdims=True)
+        put(at, back)
+
+
+def attend_back(
+    pair, first, at, spots, head_lane, q_ref, k_ref, v_ref, dm_ref, lse_ref, bias_ref, dqa_ref, dka_ref, dva_ref
+):
+    scale = HEAD_DIM**-0.5
+    rows = at.size
+    lanes = pl.ds(pl.multiple_of((first + pair) * 128, 128), 128)
+    there = pl.ds(pl.multiple_of(pair * 128, 128), 128)
+    query, grad = q_ref[at, lanes], dm_ref[at, lanes]
+    logs = lse_ref[at, :]
+    outs = []
+    for h in range(2):
+        mine = (head_lane < HEAD_DIM) if h == 0 else (head_lane >= HEAD_DIM)
+        qm = jnp.where(mine, query, 0) * jnp.asarray(scale, BF16)
+        gm = jnp.where(mine, grad, 0)
+        log = jnp.sum(
+            jnp.where(head_lane == (first + pair) * 2 + h, logs, 0.0), axis=1, keepdims=True
+        )
+        weights = [
+            jnp.exp(dot_nt(qm, k_ref[s, lanes]) + bias_ref[n] - log) for n, s in enumerate(spots)
+        ]
+        grads = [dot_nt(gm, v_ref[s, lanes]) for s in spots]
+        inner = sum(jnp.sum(w * g, axis=1, keepdims=True) for w, g in zip(weights, grads))
+        dq = jnp.zeros((rows, 128), F32)
+        for w, g, s in zip(weights, grads, spots):
+            ds = (w * (g - inner)).astype(BF16)
+            dva_ref[s, there] += dot_tn(w.astype(BF16), gm)
+            dka_ref[s, there] += dot_tn(ds, qm)
+            dq = dq + dot_nn(ds, k_ref[s, lanes])
+        outs.append(dq)
+    dqa_ref[at, there] = jnp.where(head_lane < HEAD_DIM, outs[0], outs[1]) * scale
+
+
+TICK_AFTER = (2, 4, 6)
+
+
+def layer_kernel(
+    dp, x_in, g_in, gain_ref, wq_in, wk_in, wv_in, wo_in, gate_in, up_in, down_in, cos_all, sin_all,
+    segc_all, segr_all,
+    output_out, input_grad_out, gain_out, gate_out, up_out, down_out, q_out, k_out, v_out, o_out,
+    wa_full, wo_full, wf_full, hidden_all, kept_all, landed_all, y_all, normed_all, q_all, k_all, v_all,
+    mixed_all, lse_all,
+    x_ref, wa_src, wo_src, wf_src, gains_full, rows_a, rows_m, rows_g,
+    theirs, swapped, mine, work, total, turned, stage, landed, own, gm, middle, gp, gp_landed,
+    sem_in, sem_gains, sem_a, sem_o, sem_f, sem_n, sem_m, sem_g, sem_g2, sem_s, sem_line, sem_write,
+    sem_gain, sem_c, sem_w, free_core, free_x, free_y,
+):
+    me = Place(dp)
+    line = me.line
+    d = x_in.shape[1]
+    half, local = d // 2, x_in.shape[0]
+    shard = half // line
+    rows = LEN // 4
+    blocks = wf_src.shape[0]
+    fw = wf_src.shape[2] // 3
+    cols = wq_in.shape[1]
+    groups = cols // GROUP
+
+    def at_block(b):
+        return pl.ds(pl.multiple_of(b * rows, rows), rows)
+
+    def true_columns(side, s):
+        core = me.core if side == 0 else 1 - me.core
+        return pl.ds(pl.multiple_of((2 * s + core) * shard, shard), shard)
+
+    def own_columns(side, s):
+        return pl.ds(side * half + s * shard, shard)
+
+    sides = [(side, s) for side in range(2) for s in range(line)]
+    x_loads = [
+        pltpu.make_async_copy(
+            x_in.at[:, true_columns(*p)], x_ref.at[:, own_columns(*p)], sem_in.at[n]
+        )
+        for n, p in enumerate(sides)
+    ]
+    g_loads = [
+        pltpu.make_async_copy(
+            g_in.at[:, true_columns(*p)], rows_g.at[pl.ds(0, local), own_columns(*p)],
+            sem_in.at[2 * line + n],
+        )
+        for n, p in enumerate(sides)
+    ]
+    first_sem = 4 * line
+    a_loads = [
+        pltpu.make_async_copy(ref, wa_src.at[:, pl.ds(n * cols, cols)], sem_in.at[first_sem + n])
+        for n, ref in enumerate((wq_in, wk_in, wv_in))
+    ]
+    f_loads = [
+        pltpu.make_async_copy(
+            ref.at[:, pl.ds(n * fw, fw)], wf_src.at[n, :, pl.ds(part * fw, fw)],
+            sem_in.at[first_sem + 3 + 2 * n + part],
+        )
+        for n in range(blocks)
+        for part, ref in enumerate((gate_in, up_in))
+    ]
+    for copy in a_loads + x_loads + g_loads + f_loads:
+        copy.start()
+    gains_full[0, pl.ds(pl.multiple_of(me.z * 16, 16), 16), :] = gain_ref[...]
+    me.greet()
+
+    def gain_copy(k, sender):
+        place = gains_full.at[k % 2, pl.ds(pl.multiple_of(sender // 2 * 16, 16), 16)]
+        return remote(
+            gain_ref, place, sem_gains.at[0, k], sem_gains.at[1, k], {"dp": (me.index + k) % dp}
+        )
+
+    for k in range(1, dp):
+        gain_copy(k, me.index).start()
+
+    wa = LineGather(me, wa_src, wa_full, sem_a)
+    wo = LineGather(me, wo_src, wo_full, sem_o)
+    gathers = [LineGather(me, wf_src.at[n], wf_full.at[n], sem_f.at[n]) for n in range(blocks)]
+    order = [wa, wo] + gathers
+    acts = []
+    for n, one in enumerate(order):
+        for h in range(1, line):
+
+            def act(n=n, one=one, h=h):
+                one.hop(h)
+                if h == 1 and n == 0:
+                    wo.start()
+                if h == 2 and n == 0:
+                    gathers[0].start()
+                if h == 1 and 1 <= n < blocks:
+                    order[n + 2].start()
+
+            acts.append(act)
+
+    def poll(count=1):
+        for _ in range(min(count, len(acts))):
+            acts.pop(0)()
+
+    def hops_done(n):
+        return len(acts) <= (blocks - 1 - n) * (line - 1)
+
+    for copy in a_loads:
+        copy.wait()
+    wa.start()
+    for k in range(1, dp):
+        gain_copy(k, (me.index + dp - k) % dp).wait_recv()
+    for copy in x_loads:
+        copy.wait()
+
+    def gain_row(which):
+        return jnp.concatenate(
+            [
+                gains_full[side, pl.ds(s * 16 + which, 1), :].astype(F32)
+                for side in range(2)
+                for s in range(line)
+            ],
+            axis=1,
+        )
+
+    gain_one, gain_two = gain_row(0), gain_row(1)
+
+    def first_norm(at):
+        values = x_ref[at, :].astype(F32)
+        rows_a[at, :] = (values * norm_factor(values) * gain_one).astype(BF16)
+
+    norm_rows(local, first_norm)
+    normed = SquareGather(me, rows_a, sem_n)
+    grads = SquareGather(me, rows_g, sem_g)
+    normed_mlp = SquareGather(me, rows_m, sem_m)
+    square = SquareGather(me, rows_a, sem_g2)
+    scatter = SquareScatter(me, stage, landed, sem_s)
+    normed.start()
+    for n in range(cols // 256):
+        wo_src[:, pl.ds(n * 256, 256)] = wo_in[pl.ds(n * 256, 256), :].T
+    for n in range(blocks):
+        wf_src[n, :, pl.ds(2 * fw, fw)] = down_in[pl.ds(n * fw, fw), :].T
+    for copy in f_loads:
+        copy.wait()
+    poll()
+    for copy in g_loads:
+        copy.wait()
+    normed.forward()
+    grads.start()
+    poll(line - 2)
+    normed.arrived()
+    wa.arrived()
+
+    def free_landed():
+        for device, sem in ((me.x, free_x), (me.y, free_y)):
+            pl.semaphore_signal(
+                sem, inc=1, device_id=device, device_id_type=pl.DeviceIdType.MESH
+            )
+
+    def wait_free():
+        pl.semaphore_wait(free_x, 1)
+        pl.semaphore_wait(free_y, 1)
+
+    def summed(at):
+        return own[at, :] + landed[0, at, :].astype(F32) + landed[1, at, :].astype(F32)
+
+    def doubled(ref, at):
+        part = ref[at, :]
+        return jnp.concatenate([part] * (GROUP // 128), axis=1)
+
+    head_lane = lax.broadcasted_iota(jnp.int32, (rows, 128), 1)
+
+    def forward(
+        wa_v, wo_v, q_ref, k_ref, v_ref, mixed_ref, lse_ref, cos_ref, sin_ref, segc_ref, segr_ref, bias_ref
+    ):
+        ins = [(cos_all, cos_ref), (sin_all, sin_ref), (segc_all, segc_ref), (segr_all, segr_ref)] + [
+            (wa_full.at[side], wa_v.at[pl.ds(side * half, half)]) for side in range(2)
+        ]
+        loads = [pltpu.make_async_copy(a, b, sem_c.at[n]) for n, (a, b) in enumerate(ins)]
+        for copy in loads:
+            copy.start()
+        for copy in loads:
+            copy.wait()
+
+        @pl.loop(0, 4 * groups)
+        def _(n):
+            b, group = n // groups, n % groups
+            at = at_block(b)
+            lanes = pl.ds(pl.multiple_of(group * GROUP, GROUP), GROUP)
+            cosine, sine = doubled(cos_ref, at), doubled(sin_ref, at)
+
+            def product(part):
+                here = pl.ds(pl.multiple_of(part * cols + group * GROUP, GROUP), GROUP)
+                return dot_nn(rows_a[at, :], wa_v[:, here])
+
+            query = product(0)
+            q_ref[at, lanes] = (query * cosine + swap_halves(query) * sine).astype(BF16)
+            keys = product(1)
+            k_ref[at, lanes] = (keys * cosine + swap_halves(keys) * sine).astype(BF16)
+            v_ref[at, lanes] = product(2).astype(BF16)
+
+        outs = [(q_ref, q_all), (k_ref, k_all), (v_ref, v_all), (rows_a, normed_all)]
+        stores = [pltpu.make_async_copy(a, b, sem_c.at[n]) for n, (a, b) in enumerate(outs)]
+        for copy in stores:
+            copy.start()
+        poll(2)
+        for i in range(4):
+            places = [(j, me.spots[j]) for j in key_blocks(i, rows)]
+            at = at_block(me.spots[i])
+            fill_bias(bias_ref, segc_ref[at, 0:1], segr_ref, i, places)
+            spots = [at_block(p) for _, p in places]
+
+            @pl.loop(0, cols // 128)
+            def _(pair, at=at, spots=spots):
+                attend(pair, 0, at, spots, head_lane, q_ref, k_ref, v_ref, mixed_ref, lse_ref, bias_ref)
+
+            if i == 0:
+                poll(line - 3)
+            if i == 1:
+                grads.forward()
+            if i == 2:
+                wo.arrived()
+                wo_load = [
+                    pltpu.make_async_copy(wo_full.at[side], wo_v.at[pl.ds(side * half, half)], sem_w.at[0, side])
+                    for side in range(2)
+                ]
+                for copy in wo_load:
+                    copy.start()
+                poll()
+        for n, (a, b) in enumerate(((mixed_ref, mixed_all), (lse_ref, lse_all))):
+            stores.append(pltpu.make_async_copy(a, b, sem_c.at[len(outs) + n]))
+            stores[-1].start()
+        for copy in wo_load:
+            copy.wait()
+
+        def out_rows(b, slot):
+            at = pl.ds(b * rows, rows)
+            wide = d // 4
+
+            @pl.loop(0, 4)
+            def _(n):
+                here = pl.ds(pl.multiple_of(n * wide, wide), wide)
+                value = dot_nt(mixed_ref[at, :], wo_v[here, :])
+                if slot is None:
+                    own[:, here] = value
+                else:
+                    stage[slot, :, here] = value.astype(BF16)
+
+        out_rows(3, 2)
+        scatter.diagonal_ready()
+        out_rows(1, 0)
+        out_rows(2, 1)
+        scatter.sides_ready()
+        out_rows(0, None)
+        poll(2)
+        scatter.combine()
+        poll(2)
+        for copy in stores:
+            copy.wait()
+        normed.done()
+        scatter.arrived()
+
+    V = pltpu.VMEM
+    slab = V((LEN, cols), BF16)
+    table, wide_table = V((LEN, 128), F32), V((LEN, GROUP), F32)
+    bias = V((3, rows, rows), F32)
+    segs = (V(segc_all.shape, jnp.int32), V(segr_all.shape, jnp.int32))
+    pl.run_scoped(
+        forward, V((d, 3 * cols), BF16), V((d, cols), BF16), slab, slab, slab, slab, table, table, table,
+        *segs, bias,
+    )
+
+    def second_norm(at):
+        values = x_ref[at, :].astype(F32) + summed(at)
+        middle[at, :] = values
+        rows_m[at, :] = (values * norm_factor(values) * gain_two).astype(BF16)
+
+    norm_rows(local, second_norm)
+    normed_mlp.start()
+    free_landed()
+    scatter.done()
+    poll(3)
+    normed_mlp.forward()
+    poll()
+    grads.arrived()
+    normed_mlp.arrived()
+
+    sizes = [3 * fw] * blocks + [cols] + [3 * GROUP] * groups
+    chunks = [
+        LineScatter(me, size, mine, theirs, swapped, kept_all.at[n], landed_all.at[n], work, sem_line.at[n])
+        for n, size in enumerate(sizes)
+    ]
+    writers = []
+    for n in range(blocks):
+        here = pl.ds(n * fw, fw)
+        parts = [(gate_out.at[:, here], True), (up_out.at[:, here], True), (down_out.at[here], False)]
+        writers.append(Writer(total, turned, parts, sem_write.at[n]))
+    parts = [(o_out.at[pl.ds(n * 256, 256)], False) for n in range(cols // 256)]
+    writers.append(Writer(total, turned, parts, sem_write.at[blocks]))
+    for n in range(groups):
+        here = pl.ds(n * GROUP, GROUP)
+        parts = [(ref.at[:, here], True) for ref in (q_out, k_out, v_out)]
+        writers.append(Writer(total, turned, parts, sem_write.at[blocks + 1 + n]))
+    ticks = Ticks(chunks, total, writers)
+
+    def swap(n):
+        if n >= 1:
+            pl.semaphore_wait(free_core, 1)
+        chunks[n].swap().start()
+
+    def products(left, right, first, size):
+        @pl.loop(0, line)
+        def _(s):
+            for side, dst in ((0, mine), (1, theirs)):
+                here = pl.ds(pl.multiple_of(side * half + s * shard, shard), shard)
+                dst[s, pl.ds(first, size), :] = dot_nn(left[...], right[:, here]).astype(BF16)
+
+    def mlp(wb, sums, dgu_t, hid_t, hid):
+        def weights(n):
+            return [
+                pltpu.make_async_copy(
+                    wf_full.at[n, side], wb.at[n % 2, pl.ds(side * half, half)], sem_w.at[n % 2, side]
+                )
+                for side in range(2)
+            ]
+
+        def hidden_copy(n):
+            return pltpu.make_async_copy(hid.at[n % 2], hidden_all.at[n], sem_c.at[n % 2])
+
+        fetched = [False] * (blocks + 1)
+
+        def fetch(n):
+            if n < blocks and not fetched[n]:
+                while not hops_done(n):
+                    poll()
+                gathers[n].arrived()
+                for copy in weights(n):
+                    copy.start()
+                fetched[n] = True
+
+        for n in range(blocks):
+            fetch(n)
+            if n == 0:
+
+                @pl.loop(0, LEN // 64)
+                def _(i):
+                    at = pl.ds(pl.multiple_of(i * 64, 64), 64)
+                    sums[at, :] = jnp.zeros((64, d), F32)
+
+            for copy in weights(n):
+                copy.wait()
+            if n == 1:
+                chunks[0].reduce(free_core)
+            if n + 1 < blocks and hops_done(n + 1):
+                fetch(n + 1)
+            if n >= 2:
+                hidden_copy(n - 2).wait()
+            w = wb.at[n % 2]
+            gu_w, down_w = w.at[:, pl.ds(0, 2 * fw)], w.at[:, pl.ds(2 * fw, fw)]
+
+            @pl.loop(0, 4)
+            def _(r, n=n, gu_w=gu_w, down_w=down_w):
+                at = at_block(r)
+                gu = dot_nn(rows_m[at, :], gu_w[...])
+                grad_hidden = dot_nn(rows_g[at, :], down_w[...])
+                gate_pre, upward = gu[:, :fw], gu[:, fw:]
+                sig = jax.nn.sigmoid(gate_pre)
+                activated = gate_pre * sig
+                hidden = (activated * upward).astype(BF16)
+                hid[n % 2, at, :] = hidden
+                hid_t[:, at] = hidden.T
+                grad_gate = grad_hidden * upward * sig * (1.0 + gate_pre * (1.0 - sig))
+                grad_up = grad_hidden * activated
+                dgu = jnp.concatenate([grad_gate, grad_up], axis=1).astype(BF16)
+                dgu_t[:, at] = dgu.T
+
+                @pl.loop(0, 4)
+                def _(c):
+                    here = pl.ds(pl.multiple_of(c * (half // 2), half // 2), half // 2)
+                    sums[at, here] += dot_nt(dgu, gu_w[here, :])
+
+            hidden_copy(n).start()
+            poll()
+            if n >= 2:
+                chunks[n - 1].reduce(free_core)
+            products(dgu_t, rows_m, 0, 2 * fw)
+            products(hid_t, rows_g, 2 * fw, fw)
+            swap(n)
+            poll()
+            if n in TICK_AFTER:
+                ticks.tick()
+        for n in range(max(0, blocks - 2), blocks):
+            hidden_copy(n).wait()
+        wait_free()
+
+        def to_stage(b, slot):
+            @pl.loop(0, rows // 64)
+            def _(i):
+                at = pl.ds(pl.multiple_of(i * 64, 64), 64)
+                there = pl.ds(pl.multiple_of(b * rows + i * 64, 64), 64)
+                if slot is None:
+                    own[at, :] = sums[there, :]
+                else:
+                    stage[slot, at, :] = sums[there, :].astype(BF16)
+
+        to_stage(3, 2)
+        scatter.diagonal_ready()
+        to_stage(1, 0)
+        to_stage(2, 1)
+        scatter.sides_ready()
+        to_stage(0, None)
+
+    pl.run_scoped(
+        mlp, V((2, d, 3 * fw), BF16), V((LEN, d), F32), V((2 * fw, LEN), BF16), V((fw, LEN), BF16),
+        V((2, LEN, fw), BF16),
+    )
+    gp[...] = jnp.zeros(gp.shape, F32)
+
+    def down(hidden, dw, rest):
+        ins = [(hidden_all.at[n], hidden.at[n]) for n in range(blocks)] + [
+            (wf_full.at[n, side, :, pl.ds(2 * fw, fw)], dw.at[n, pl.ds(side * half, half)])
+            for n in range(blocks)
+            for side in range(2)
+        ]
+        loads = [pltpu.make_async_copy(a, b, sem_c.at[n]) for n, (a, b) in enumerate(ins)]
+        for copy in loads:
+            copy.start()
+        chunks[blocks - 1].reduce(free_core)
+        ticks.tick()
+        for copy in loads:
+            copy.wait()
+
+        @pl.loop(0, 4)
+        def _(b):
+            at = at_block(b)
+
+            @pl.loop(0, d // GROUP)
+            def _(c):
+                here = pl.ds(pl.multiple_of(c * GROUP, GROUP), GROUP)
+                value = sum(dot_nt(hidden[n, at, :], dw[n, here, :]) for n in range(blocks))
+                rest[b, :, here] = value.astype(BF16)
+
+        out = pltpu.make_async_copy(rest, y_all, sem_c.at[0])
+        out.start()
+        out.wait()
+
+    pl.run_scoped(
+        down, V((blocks, LEN, fw), BF16), V((blocks, d, fw), BF16), V((4, local, d), BF16)
+    )
+    scatter.combine()
+    normed_mlp.done()
+    grads.done()
+
+    def attention(
+        q_ref, k_ref, v_ref, mixed_t, mixed, lse_ref, cos_ref, sin_ref, segc_ref, segr_ref, out_w,
+        dqa_ref, dka_ref, dva_ref, part_t, bias_ref, y_mine,
+    ):
+        ins = [
+            (mixed_all, mixed), (q_all, q_ref), (k_all, k_ref), (v_all, v_ref), (lse_all, lse_ref),
+            (cos_all, cos_ref), (sin_all, sin_ref), (segc_all, segc_ref), (segr_all, segr_ref),
+            (wo_full, out_w), (y_all.at[0], y_mine), (normed_all, rows_m),
+        ]
+        loads = [pltpu.make_async_copy(a, b, sem_c.at[n]) for n, (a, b) in enumerate(ins)]
+        for copy in loads:
+            copy.start()
+        ticks.tick()
+        scatter.arrived()
+
+        def second_norm_back(at, back):
+            grad = rows_g[at, :].astype(F32) + back
+            gm[at, :] = grad
+            rows_a[at, :] = grad.astype(BF16)
+
+        norm_back_rows(local, gain_two, lambda at: middle[at, :], summed, gp, 1, second_norm_back)
+        square.start()
+        free_landed()
+        scatter.done()
+        stage_in = [
+            pltpu.make_async_copy(y_all.at[b], stage.at[slot], sem_w.at[n // 2, n % 2])
+            for n, (b, slot) in enumerate(((3, 2), (1, 0), (2, 1)))
+        ]
+        for copy in stage_in:
+            copy.start()
+        for copy in loads:
+            copy.wait()
+        mixed_t[...] = mixed[...].T
+        square.forward()
+        ticks.tick()
+        for copy in stage_in:
+            copy.wait()
+        wait_free()
+        square.arrived()
+        scatter.diagonal_ready()
+        scatter.sides_ready()
+
+        @pl.loop(0, 4)
+        def _(b):
+            at = at_block(b)
+            rows_g[at, pl.ds(3 * cols, cols)] = (
+                dot_nn(rows_a[at, :half], out_w[0]) + dot_nn(rows_a[at, half:], out_w[1])
+            ).astype(BF16)
+
+        products(mixed_t, rows_a, 0, cols)
+        swap(blocks)
+        dm_ref = rows_g.at[:, pl.ds(3 * cols, cols)]
+        for group in range(groups):
+
+            @pl.loop(0, 4)
+            def _(b):
+                at = at_block(b)
+                dka_ref[at, :] = jnp.zeros((rows, GROUP), F32)
+                dva_ref[at, :] = jnp.zeros((rows, GROUP), F32)
+
+            for i in range(4):
+                places = [(j, me.spots[j]) for j in key_blocks(i, rows)]
+                at = at_block(me.spots[i])
+                fill_bias(bias_ref, segc_ref[at, 0:1], segr_ref, i, places)
+                spots = [at_block(p) for _, p in places]
+
+                @pl.loop(0, GROUP // 128)
+                def _(pair, at=at, spots=spots, group=group):
+                    attend_back(
+                        pair, group * (GROUP // 128), at, spots, head_lane, q_ref, k_ref, v_ref,
+                        dm_ref, lse_ref, bias_ref, dqa_ref, dka_ref, dva_ref,
+                    )
+
+                if i == 1:
+                    chunks[blocks + group].reduce(free_core)
+                if i == 2 and group == 0:
+                    ticks.tick()
+                if i == 3 and group == 0:
+                    scatter.combine()
+
+            @pl.loop(0, 4)
+            def _(b, group=group):
+                at = at_block(b)
+                cosine, sine = doubled(cos_ref, at), doubled(sin_ref, at)
+                for part, ref in enumerate((dqa_ref, dka_ref, dva_ref)):
+                    value = ref[at, :]
+                    if part < 2:
+                        value = value * cosine - swap_halves(value) * sine
+                    value = value.astype(BF16)
+                    rows_g[at, pl.ds(part * cols + group * GROUP, GROUP)] = value
+                    part_t[pl.ds(part * GROUP, GROUP), at] = value.T
+
+            products(part_t, rows_m, 0, 3 * GROUP)
+            swap(blocks + 1 + group)
+            if group == 0:
+                ticks.tick()
+        scatter.arrived()
+
+        def output_rows(at):
+            value = middle[at, :] + y_mine[at, :].astype(F32)
+            value = value + landed[0, at, :].astype(F32) + landed[1, at, :].astype(F32)
+            y_mine[at, :] = value.astype(BF16)
+
+        norm_rows(local, output_rows)
+        free_landed()
+        results = [
+            pltpu.make_async_copy(
+                y_mine.at[:, own_columns(*p)], output_out.at[:, true_columns(*p)], sem_in.at[n]
+            )
+            for n, p in enumerate(sides)
+        ]
+        for copy in results:
+            copy.start()
+        scatter.done()
+        for copy in results:
+            copy.wait()
+
+    pl.run_scoped(
+        attention, slab, slab, slab, V((cols, LEN), BF16), slab, table, table, table, *segs,
+        V(wo_full.shape, BF16), wide_table, wide_table, wide_table, V((3 * GROUP, LEN), BF16), bias,
+        V((local, d), BF16),
+    )
+
+    def normed_grads(qkv_w):
+        loads = [
+            pltpu.make_async_copy(wa_full.at[side], qkv_w.at[pl.ds(side * half, half)], sem_c.at[side])
+            for side in range(2)
+        ]
+        for copy in loads:
+            copy.start()
+        chunks[blocks + groups].reduce(free_core)
+        for copy in loads:
+            copy.wait()
+        wait_free()
+
+        def normed_grad(b, slot):
+            at = pl.ds(b * rows, rows)
+            wide = d // 4
+
+            @pl.loop(0, 4)
+            def _(n):
+                here = pl.ds(pl.multiple_of(n * wide, wide), wide)
+                value = dot_nt(rows_g[at, pl.ds(0, 3 * cols)], qkv_w[here, :])
+                if slot is None:
+                    own[:, here] = value
+                else:
+                    stage[slot, :, here] = value.astype(BF16)
+
+        normed_grad(3, 2)
+        scatter.diagonal_ready()
+        normed_grad(1, 0)
+        normed_grad(2, 1)
+        scatter.sides_ready()
+        normed_grad(0, None)
+
+    pl.run_scoped(normed_grads, V((d, 3 * cols), BF16))
+    ticks.tick()
+    scatter.combine()
+    ticks.tick()
+    scatter.arrived()
+
+    def first_norm_back(at, back):
+        gm[at, :] += back
+
+    norm_back_rows(
+        local, gain_one, lambda at: x_ref[at, :].astype(F32), summed, gp, 0, first_norm_back
+    )
+    results = [
+        pltpu.make_async_copy(
+            gm.at[:, own_columns(*p)], input_grad_out.at[:, true_columns(*p)], sem_in.at[n]
+        )
+        for n, p in enumerate(sides)
+    ]
+    for copy in results:
+        copy.start()
+    scatter.done()
+    exchange = [
+        remote(gp, gp_landed.at[n], sem_gain.at[n, 0], sem_gain.at[n, 1], device)
+        for n, device in enumerate((me.x, me.y, me.other, me.next, me.far))
+    ]
+
+    def add_gains(n):
+        exchange[n].wait()
+        if n == 2:
+            gp[:, :half] += gp_landed[n, :, half:]
+            gp[:, half:] += gp_landed[n, :, :half]
+        else:
+            gp[...] += gp_landed[n]
+
+    for n in range(3):
+        exchange[n].start()
+        add_gains(n)
+    exchange[3].start()
+    ticks.tick()
+    add_gains(3)
+    exchange[4].start()
+    ticks.tick()
+    add_gains(4)
+    gain_out[...] = gp[...]
+    ticks.rest()
+    pl.semaphore_wait(free_core, 1)
+    for k in range(1, dp):
+        gain_copy(k, me.index).wait_send()
+    for copy in results:
+        copy.wait()
+    for one in [wa, wo, square] + gathers:
+        one.done()
+
+
+def layer(dp, x, g, gains, wq, wk, wv, wo, gate, up, down, cosine, sine, segc, segr):
     line = dp // 2
     local, d = x.shape
-    cols = wo.shape[1]
-    nf, _, fcols = wf.shape
-    vmem, hbm = pl.BlockSpec(memory_space=pltpu.VMEM), pl.BlockSpec(memory_space=pl.ANY)
-    S = jax.ShapeDtypeStruct
+    cols, ff = wq.shape[1], gate.shape[1]
+    blocks, shard = FF_BLOCKS, d // dp
+    fw = ff // blocks
+    groups = cols // GROUP
+    count = blocks + 1 + groups
+    most = max(3 * fw, cols, 3 * GROUP)
+    vm, hbm = pl.BlockSpec(memory_space=pltpu.VMEM), pl.BlockSpec(memory_space=pl.ANY)
+    S, V, dma = jax.ShapeDtypeStruct, pltpu.VMEM, pltpu.SemaphoreType.DMA
+    regular = pltpu.SemaphoreType.REGULAR
     slab = S((LEN, cols), BF16)
-    rows = LEN // 4
-    dma = pltpu.SemaphoreType.DMA
+    piece = V((line, most, shard), BF16)
     return pl.pallas_call(
-        functools.partial(forward_kernel, dp),
-        in_specs=[vmem, vmem, vmem, hbm, hbm, vmem, vmem, vmem, vmem, vmem],
-        out_specs=[vmem, hbm, hbm, vmem, vmem, vmem, vmem, vmem, vmem, vmem, vmem, hbm, vmem],
+        functools.partial(layer_kernel, dp),
+        in_specs=[hbm, hbm, vm, hbm, hbm, hbm, vm, hbm, hbm, vm, hbm, hbm, hbm, hbm],
+        out_specs=[hbm, hbm, vm] + [hbm] * 20,
         out_shape=[
-            S((4, local, d), BF16), S((4, local, d), BF16), S((4, local, d), BF16),
-            slab, slab, slab, slab, S((LEN, 128), F32), S((local, d), F32),
+            S((local, d), BF16), S((local, d), F32), S((8, d), F32),
+            S((shard, ff), BF16), S((shard, ff), BF16), S((ff, shard), BF16),
+            S((shard, cols), BF16), S((shard, cols), BF16), S((shard, cols), BF16), S((cols, shard), BF16),
             S((2, d // 2, 3 * cols), BF16), S((2, d // 2, cols), BF16),
-            S((nf, 2, d // 2, fcols), BF16), S((2, line * 16, d // dp), BF16),
+            S((blocks, 2, d // 2, 3 * fw), BF16), S((blocks, LEN, fw), BF16),
+            S((count, line, most, shard), BF16), S((count, line + 1, most, shard), BF16),
+            S((4, local, d), BF16), S((LEN, d), BF16), slab, slab, slab, slab, S((LEN, 128), F32),
         ],
         scratch_shapes=[
-            pltpu.VMEM((3, rows, rows), F32),
-            pltpu.VMEM((local, d), BF16),
-            pltpu.VMEM((3, local, d), BF16),
-            pltpu.VMEM((3, local, d), BF16),
-            dma((6, line)), dma((6, line)), dma((6, line)), dma((nf, 6, line)),
-            dma((8,)), dma((8,)), dma((12,)), dma((8,)), dma((2,)),
+            V((local, d), BF16), V((shard, 3 * cols), BF16), V((shard, cols), BF16),
+            V((blocks, shard, 3 * fw), BF16), V((2, line * 16, shard), BF16),
+            V((LEN, d), BF16), V((LEN, d), BF16), V((LEN, d), BF16),
+            piece, piece, piece, V((9, most, shard), BF16), V((most, shard), F32), V((3, shard, 256), BF16),
+            V((3, local, d), BF16), V((3, local, d), BF16), V((local, d), F32), V((local, d), F32),
+            V((local, d), F32), V((8, d), F32), V((5, 8, d), F32),
+            dma((4 * line + 3 + 2 * blocks,)), dma((2, dp)), dma((6, line)), dma((6, line)),
+            dma((blocks, 6, line)), dma((8,)), dma((8,)), dma((8,)), dma((8,)), dma((12,)),
+            dma((count, 4 + 2 * line + 9)), dma((count, 3)), dma((5, 2)), dma((3 * blocks,)), dma((2, 2)),
+            regular, regular, regular,
         ],
         compiler_params=pltpu.CompilerParams(
             vmem_limit_bytes=VMEM_BYTES, collective_id=0, has_side_effects=True
         ),
-        name="forward",
-    )(x, wa, wo, wf, g, gains, cosine, sine, segc, segr)
+        name="layer",
+    )(x, g, gains, wq, wk, wv, wo, gate, up, down, cosine, sine, segc, segr)
 
 
 def on_device(
@@ -680,7 +1440,7 @@
     line = dp // 2
     core = lax.axis_index("dp") % 2
     place = lax.axis_index("tensor")
-    square = tensor == 4
+    square = tensor == 4 and dp == 8
     same_core = [[c + 2 * z for z in range(line)] for c in range(2)]
     sibling = [(i, i ^ 1) for i in range(dp)]
     d = hidden_in.shape[1]
@@ -746,7 +1506,28 @@
     segc = jnp.broadcast_to(segment[:, None], (LEN, 128))
     segr = jnp.broadcast_to(segment.reshape(blocks, 1, rows), (blocks, 8, rows))
     key = key.reshape(1)
-
+    cols = w_query.shape[1]
+    if square:
+        gain_rows = jnp.pad(
+            jnp.concatenate([gain_attn, gain_mlp]), (0, 14 * gain_attn.shape[0])
+        ).reshape(16, -1)
+        (
+            output, input_grad, gain_sum, grad_gate, grad_up, grad_down, grad_query, grad_key,
+            grad_value, grad_out, *_,
+        ) = layer(
+            dp, hidden_in, cotangent, gain_rows, w_query, w_key, w_value, w_out, w_gate, w_up,
+            w_down, cosine, sine, segc, segr,
+        )
+        share = d // (dp * tensor)
+        first = (lax.axis_index("dp") // 2) * (d // dp) + place * share
+        gain_sum = lax.dynamic_slice_in_dim(gain_sum, first, share, 1)
+        return (
+            output, input_grad, gain_sum[0], grad_query.astype(F32), grad_key.astype(F32),
+            grad_value.astype(F32), grad_out.astype(F32), gain_sum[1], grad_gate.astype(F32),
+            grad_up.astype(F32), grad_down.astype(F32),
+        )
+
+    cosine, sine = (jnp.tile(a, (1, GROUP // 128)) for a in (cosine, sine))
     ff = w_gate.shape[1]
     fb = ff // FF_BLOCKS
     down_t = w_down.T
@@ -755,46 +1536,26 @@
         for b in range(FF_BLOCKS)
     ]
     qkv_shard = jnp.concatenate([w_query, w_key, w_value], axis=1)
-    cols = w_query.shape[1]
-    hidden_mine = own_first(hidden_in)
     g_local = own_first(cotangent)
-    inputs = hidden_mine.astype(F32)
+    inputs = own_first(hidden_in).astype(F32)
     factor_one = norm_factor(inputs)
-    early = FF_EARLY if square else 0
-    ff_sets = [jnp.concatenate(line_gather(shard), axis=0) for shard in shards[early:]]
-    if square:
-        gain_rows = jnp.pad(jnp.stack([gain_attn, gain_mlp]), ((0, 14), (0, 0)))
-        (
-            normed, g_all, normed_mlp, query, keys, values, mixed, lse, middle, qkv_full,
-            out_full, ff_full, gains,
-        ) = forward(
-            dp, hidden_mine, qkv_shard, w_out.T, jnp.stack(shards[:early]), g_local, gain_rows,
-            cosine, sine, segc, segr,
-        )
-        normed, g_all, normed_mlp = (a.reshape(LEN, d) for a in (normed, g_all, normed_mlp))
-        qkv_own, qkv_sib = qkv_full[0], qkv_full[1]
-        out_own, out_sib = out_full[0], out_full[1]
-        ff_sets = [ff_full[b].reshape(d, 3 * fb) for b in range(early)] + ff_sets
-        gains = gains.reshape(2 * line, 16, d // dp)[:, :2].astype(F32)
-        gain_one, gain_two = gains[:, 0].reshape(d), gains[:, 1].reshape(d)
-        factor_two = norm_factor(middle)
-    else:
-        gains = lax.all_gather(jnp.stack([gain_attn, gain_mlp]), "dp", axis=0)
-        gains = own_first(jnp.moveaxis(gains, 0, 1).reshape(2, d)).astype(F32)
-        gain_one, gain_two = gains[0], gains[1]
-        qkv_own, qkv_sib = line_gather(qkv_shard)
-        out_own, out_sib = line_gather(w_out.T)
-        normed = gather_rows((inputs * factor_one * gain_one).astype(BF16))
-        g_all = gather_rows(g_local)
-        query, keys, values, mixed, lse = attn_forward(
-            blocks, key, normed, qkv_own, qkv_sib, cosine, sine, segc, segr
-        )
-        attended = jnp.concatenate(
-            [dot_nt(mixed, out_own).astype(BF16), dot_nt(mixed, out_sib).astype(BF16)], axis=1
-        )
-        middle = inputs + scatter_rows(attended)
-        factor_two = norm_factor(middle)
-        normed_mlp = gather_rows((middle * factor_two * gain_two).astype(BF16))
+    gains = lax.all_gather(jnp.stack([gain_attn, gain_mlp]), "dp", axis=0)
+    gains = own_first(jnp.moveaxis(gains, 0, 1).reshape(2, d)).astype(F32)
+    gain_one, gain_two = gains[0], gains[1]
+    qkv_own, qkv_sib = line_gather(qkv_shard)
+    out_own, out_sib = line_gather(w_out.T)
+    normed = gather_rows((inputs * factor_one * gain_one).astype(BF16))
+    g_all = gather_rows(g_local)
+    query, keys, values, mixed, lse = attn_forward(
+        blocks, key, normed, qkv_own, qkv_sib, cosine, sine, segc, segr
+    )
+    attended = jnp.concatenate(
+        [dot_nt(mixed, out_own).astype(BF16), dot_nt(mixed, out_sib).astype(BF16)], axis=1
+    )
+    middle = inputs + scatter_rows(attended)
+    factor_two = norm_factor(middle)
+    normed_mlp = gather_rows((middle * factor_two * gain_two).astype(BF16))
+    ff_sets = [jnp.concatenate(line_gather(shard), axis=0) for shard in shards]
 
     down_sum = jnp.zeros((LEN, d), F32)
     back_sum = jnp.zeros((LEN, d), F32)

time: 934 us -> 589 us (0.63)
  Pallas kernels: 320 us -> 554 us
  matrix products: 192 us -> 0 us
  waiting for transfers between devices: 133 us -> 0 us
  local copies, waits for them, and re-layouts: 85 us -> 7.97 us
  other arithmetic: 92.3 us -> 16.1 us
  blocking collectives: 69.5 us -> 0 us
  starting transfers between devices: 19.5 us -> 0 us
  between operations: 15.7 us -> 0.96 us
    pallas_call x2 -> x1, Pallas kernels: 320 us -> 554 us  [layer(): pl.pallas_call(functools.partial(layer_kernel, dp), in_specs=[hbm, hbm, v...]
    dot_general x42 -> x0, matrix products: 192 us -> none  [the longest x14 106 us: dot_nt(): lax.dot_general(a, b, (((1,), (1,)), ((), ())), preferred_element_type=F32)]
    ppermute x23 -> x0, waiting for transfers between devices: 133 us -> none  [the longest x16 133 us: hop(): return lax.ppermute(a, 'tensor', [(i, i ^ step) for i in range(tensor)])]
    all_gather x1 -> x0, blocking collectives: 69.5 us -> none  [on_device(): shares = lax.all_gather(parts, ('dp', 'tensor'), axis=0)]
    concatenate x19 -> x1, other arithmetic: 43.9 us -> 0.68 us  [on_device(): jnp.concatenate([gain_attn, gain_mlp])]
    slice x21 -> x0, local copies, waits for them, and re-layouts: 27.6 us -> none  [the longest x4 9.19 us: on_device(): g[:, 2 * fb:]]
    add x12 -> x0, other arithmetic: 24.6 us -> none  [the longest x5 15.2 us: line_scatter(): mine = own + lax.ppermute(sib, 'dp', sibling)]
    unnamed x171 -> x11, local copies, waits for them, and re-layouts: 26.8 us -> 2.31 us
  transfers between devices with their start and end apart: 30 -> 0, of which waited for: 10 -> 0; matrix products, arithmetic and copies ran while one was open for 37% -> 0% of each run, Pallas kernels for 34% -> 0%
where the time goes in v4:
time: 589 us; the launch traced here: 579 us
  Pallas kernels  554 us (94%)
  other arithmetic  16.1 us (3%)
  local copies, waits for them, and re-layouts  7.97 us (1%)
    pallas_call x1, Pallas kernels, layer(): pl.pallas_call(functools.partial(layer_kernel, dp), in_specs=[hbm, hbm, v...  554 us

profile of v4, /device:TPU:0, one launch (start us, length us, event | category | flops | bytes accessed | tf_op | source)
XLA Modules:
  0.0 579.0 jit_solution(7948613068225831310)
XLA Ops:
  0.7 0.8 reduce-window.7
  1.5 0.1 add_bitcast_fusion
  1.6 0.8 fusion.2
  2.4 0.7 fusion.5
  3.1 0.6 reshape.93.gain_ref
  3.7 0.6 broadcast_in_dim.36.segr_all
  4.3 0.5 fusion
  4.9 1.0 copy.25.cos_all
  5.9 1.0 broadcast_in_dim.34.segc_all
  7.0 1.0 copy.26.sin_all
  8.0 554.0 %layer.1 = (bf16[256,2048]{1,0:T(8,128)(2,1)}, f32[256,2048]{1,0:T(8,128)}, f32[8,2048]{1,0:T(8,128)}, bf16[256,2048]{1,0:T(8,128)(2,1)}, bf16[256,2048]{1,0:T(8...) custom-call(bf16[256,2048]{1,0:T(8,128)(2,1)} %x_in.1, ...), custom_call_target="tpu_custom_call" | custom-call | tf_op jit(solution)/shard_map/layer/pallas_call | solution.py:1404
  561.9 0.8 constant_dynamic-slice_fusion
  562.8 0.5 slice_bitcast_fusion
  563.3 1.8 convert_element_type.35
  565.1 1.9 convert_element_type.36
  567.0 1.8 convert_element_type.37
  568.8 1.8 convert_element_type.38
  570.6 2.9 convert_element_type.39
  573.5 1.6 convert_element_type.40
  575.0 0.0 copy-done.1
  575.0 1.5 convert_element_type.41
  576.5 0.0 copy-done.3
  576.5 1.0 copy.30
  577.5 1.3 copy.31
  (14 shorter events, 0.2 us)
Async XLA Ops:
  561.9 11.5 %copy-start.2 = (bf16[256,2048]{1,0:T(8,128)(2,1)S(1)}, bf16[256,2048]{1,0:T(8,128)(2,1)}, u32[]{:S(2)}) copy-start(bf16[256,2048]{1,0:T(8,128)(2,1)} %get-tuple-element.29) | copy-start | bytes 3145732
  565.1 9.9 %copy-start.1 = (bf16[2048,256]{1,0:T(8,128)(2,1)S(1)}, bf16[2048,256]{1,0:T(8,128)(2,1)}, u32[]{:S(2)}) copy-start(bf16[2048,256]{1,0:T(8,128)(2,1)} %get-tuple-element.30) | copy-start | bytes 3145732
  570.6 5.9 %copy-start.3 = (bf16[256,2048]{1,0:T(8,128)(2,1)S(1)}, bf16[256,2048]{1,0:T(8,128)(2,1)}, u32[]{:S(2)}) copy-start(bf16[256,2048]{1,0:T(8,128)(2,1)} %get-tuple-element.51) | copy-start | bytes 3145732
  573.5 4.0 copy-start
